TPU v7x, 256 devices: a whole 4x4x8 slice. The times are simulated.
256 devices in a mesh: blk: 64 (over x_hi, y, z), dsplit: 4 (over x_lo, core).
Axes of the slice: x: 4 (x_hi: 2, x_lo: 2; x = x_hi * 2 + x_lo), y: 4, z: 8, core: 2. Of those that a mesh axis runs over, the one named last changes fastest.
Arguments:
- amplitudes: bfloat16 [1280, 8, 800], P('blk', None, 'dsplit'), may hold values from -6 to 6
- integrals: bfloat16 [8, 800, 65536], P(None, 'dsplit', 'blk'), may hold values from -0.078125 to 0.078125
- residual_in: float32 [1280, 65536], P('dsplit', 'blk'), may hold values from -6 to 6
- pair_list: int32 [1280, 2], P('dsplit'), may hold values from 0 to 99, as said below
- ab_list: int32 [65536, 2], P('blk'), may hold values from 0 to 799, as said below
Outputs:
- residual_out: float32 [1280, 65536], P('dsplit', 'blk')
Inputs may be any that keep to these rules, and one draw needn't show every extreme that they name: `pair_list`: each row is a pair (i, j) of occupied orbitals with i <= j. `ab_list`: each row is a pair (a, b) of virtual orbitals with a <= b.
All inputs are finite; a program needn't handle non-finite values.
Results may differ from a plain program's by a relative error of at most 0.0003.
Values may be sent and summed in bfloat16 or wider, within the bound.
No kernel may reach another device: no remote copies, remote signals or barrier semaphores. Data moves between devices by JAX's collectives and lax.ppermute only.
A program may use at most 128 MiB of HBM per device.

v0:
```python
import jax
import jax.numpy as jnp
from jax import lax
from jax.sharding import PartitionSpec as P


def pair_scale(pairs):
    return jnp.where(pairs[:, 0] == pairs[:, 1], jnp.float32(0.5), jnp.float32(1.0))


def per_device(amplitudes, integrals, residual_in, pair_list, ab_list):
    weight = pair_scale(pair_list)[:, None] * pair_scale(ab_list)[None, :]
    rows = residual_in.shape[0]
    full_amps = lax.all_gather(amplitudes, "dsplit", axis=2, tiled=True)
    full_ints = lax.all_gather(integrals, "dsplit", axis=1, tiled=True)
    every_amp = lax.all_gather(full_amps, "blk", axis=0, tiled=True)
    first = lax.axis_index("dsplit") * rows
    mine = lax.dynamic_slice_in_dim(every_amp, first, rows, 0)
    ladder = jnp.dot(
        mine.reshape(rows, -1),
        full_ints.reshape(-1, full_ints.shape[2]),
        preferred_element_type=jnp.float32,
    )
    return residual_in + weight * ladder


def solution(mesh):
    placed = (
        P("blk", None, "dsplit"),
        P(None, "dsplit", "blk"),
        P("dsplit", "blk"),
        P("dsplit", None),
        P("blk", None),
    )
    return jax.shard_map(
        per_device, mesh=mesh, in_specs=placed, out_specs=P("dsplit", "blk"), check_vma=False
    )
```

profile of v0, /device:TPU:1, one launch (start us, length us, event | category | flops | bytes accessed | tf_op | source)
XLA Modules:
  0.0 389.0 jit_solution(17387429455078913884)
XLA Ops:
  6.5 0.0 copy-start.1
  6.5 0.0 copy-start
  6.5 0.0 all-gather.3.cloned.1.call-start
  6.5 1.2 copy.7
  7.8 14.6 %all_gather.9 = bf16[20,8,800]{0,1,2:T(8,128)(2,1)S(1)} all-gather(bf16[20,8,200]{0,1,2:T(8,128)(2,1)S(1)} %copy.7), channel_id=1, replica_groups=mesh['blk'=64,'dsplit'=4] {'dsplit'}, dimensions={2}, use_global_device_ids=true | all-gather | bytes 320000 | tf_op jit(solution)/shard_map/all_gather | solution.py:14
  22.3 2.7 copy.8
  25.0 0.0 all-gather.3.cloned.1.call-update
  25.0 0.0 all-gather.5.cloned.1.call-start
  25.1 0.7 all-gather.5.cloned.1.call-update
  25.8 0.0 copy-done.1
  25.8 0.0 copy-done
  25.8 0.0 copy-start.2
  25.8 221.9 %all-gather.3.cloned.1.call-done = bf16[1280,8,800]{2,1,0:T(8,128)(2,1)} async-done(((bf16[20,8,800]{2,1,0:T(8,128)(2,1)}), bf16[1280,8,800]{2,1,0:T(8,128)(2,1)}) %all-gather.3.cloned.1.call-update) | async-done | bytes 16384016 | tf_op jit(solution)/shard_map/all_gather | solution.py:16
  247.8 4.7 %constant_dynamic-slice_fusion = bf16[320,8,800]{2,1,0:T(8,128)(2,1)} fusion(bf16[1280,8,800]{2,1,0:T(8,128)(2,1)} %all-gather.3.cloned.1.call-done, s32[]{:T(128)S(6)} %select_n.22), kind=kLoop, calls=%fused_computation.8 | loop fusion | bytes 8192004 | tf_op jit(solution)/shard_map/dynamic_slice | solution.py:18
  252.5 118.0 %all-gather.5.cloned.1.call-done = bf16[8,800,1024]{2,1,0:T(8,128)(2,1)} async-done(((bf16[8,200,1024]{2,1,0:T(8,128)(2,1)}), bf16[8,800,1024]{2,1,0:T(8,128)(2,1)}) %all-gather.5.cloned.1.call-update) | async-done | bytes 13107216 | tf_op jit(solution)/shard_map/all_gather | solution.py:15
  370.4 0.0 copy-done.2
  370.4 11.7 %fusion.8 = f32[320,1024]{1,0:T(8,128)} fusion(f32[320,1024]{1,0:T(8,128)S(1)} %copy-done.2, bf16[8,800,1024]{2,1,0:T(8,128)(2,1)} %all-gather.5.cloned.1.call-done, bf16[320,8,800]{2,1,0:T(8,128)(2,1)} %constant_dynamic-slice_fusion, f32[1024]{0:T(1024)S(1)} %bitcast.8, f32[320]{0:T(512)S(1)} %fusion.11), kind=kOutput, calls=%fused_computation.4 | convolution fusion | flops 4195287040 | bytes 19830016 | tf_op jit(solution)/shard_map/dot_general | solution.py:19
  (2 shorter events, 0.0 us)
Async XLA Ops:
  6.5 19.2 %copy-start.1 = (s32[320,2]{0,1:T(2,128)S(1)}, s32[320,2]{0,1:T(2,128)}, u32[]{:S(2)}) copy-start(s32[320,2]{0,1:T(2,128)} %param.8) | copy-start | bytes 7684
  6.5 19.3 %copy-start = (s32[1024,2]{0,1:T(2,128)S(1)}, s32[1024,2]{0,1:T(2,128)}, u32[]{:S(2)}) copy-start(s32[1024,2]{0,1:T(2,128)} %param.9) | copy-start | bytes 24580
  6.5 241.2 %all-gather.3.cloned.1.call-start = ((), (), s32[]{:S(2)}) async-start(), calls=%async_computation | async-start | bytes 18636800 | tf_op jit(solution)/shard_map/all_gather | solution.py:16
  25.0 345.4 %all-gather.5.cloned.1.call-start = ((), (), s32[]{:S(2)}) async-start(), calls=%async_computation.1 | async-start | bytes 16384000 | tf_op jit(solution)/shard_map/all_gather | solution.py:15
  25.8 344.6 %copy-start.2 = (f32[320,1024]{1,0:T(8,128)S(1)}, f32[320,1024]{1,0:T(8,128)}, u32[]{:S(2)}) copy-start(f32[320,1024]{1,0:T(8,128)} %param.7) | copy-start | bytes 3932164
Sparse Core Ops, SparseCore 0:
  25.1 222.5 all-gather.2
  249.6 120.8 all-gather.4
where the time goes:
time: 389 us
  waiting for transfers between devices  341 us (88%)
  blocking collectives  14.6 us (4%)
  between operations  13.4 us (3%)
  matrix products  11.7 us (3%)
  local copies, waits for them, and re-layouts  8.58 us (2%)
    all_gather x1, waiting for transfers between devices, per_device(): every_amp = lax.all_gather(full_amps, 'blk', axis=0, tiled=True)  222 us
    all_gather x1, waiting for transfers between devices, per_device(): full_ints = lax.all_gather(integrals, 'dsplit', axis=1, tiled=True)  118 us
    all_gather x1, blocking collectives, per_device(): full_amps = lax.all_gather(amplitudes, 'dsplit', axis=2, tiled=True)  14.6 us
    dot_general x1, matrix products, per_device(): jnp.dot(mine.reshape(rows, -1), full_ints.reshape(-1, full_ints.shape[2])...  11.7 us
  transfers between devices with their start and end apart: 2, of which 2 were waited for; matrix products, arithmetic and copies ran while one was open for 1% of the time, Pallas kernels for 0%

commit v1 on v0

v1 whole, which is shorter than its diff:
```python
import functools

import jax
import jax.numpy as jnp
from jax import lax
from jax.experimental import pallas as pl
from jax.experimental.pallas import tpu as pltpu
from jax.sharding import Mesh
from jax.sharding import PartitionSpec as P

XH, Y, Z, XL = 2, 4, 8, 2
BLK = ("xh", "y", "z")
DS = ("xl", "core")
VMEM = pl.BlockSpec(memory_space=pltpu.VMEM)
SMEM = pl.BlockSpec(memory_space=pltpu.SMEM)
F32, BF16, F16 = jnp.float32, jnp.bfloat16, jnp.float16
LIMIT = 48 * 1024 * 1024


def params():
    return pltpu.CompilerParams(vmem_limit_bytes=LIMIT)


def to_core(hop):
    return [(2 * y + k, 2 * ((y + 2 * k + hop) % Y) + y // 2) for y in range(Y) for k in range(2)]


def turn(n, step):
    return [(i, (i + step) % n) for i in range(n)]


def pack_pairs(place_ref, *refs):
    blocks, out_ref, held = refs[:4], refs[4], refs[5]
    for j in range(4):
        held[lax.rem(j + 4 - place_ref[0], 4)] = blocks[j][...]
    out_ref[...] = jnp.concatenate([held[0], held[3], held[2], held[1]], axis=0)


def pack_ring(place_ref, *refs):
    blocks, out_ref, held = refs[:Z], refs[Z], refs[Z + 1]
    for dz in range(Z):
        held[lax.rem(place_ref[1] + dz, Z)] = blocks[dz][...]
    out_ref[...] = jnp.concatenate([held[i] for i in range(Z)], axis=0)


def part_kernel(count, *refs):
    blocks, own_ref, other_ref, out_ref, held = refs[:count], *refs[count:]

    @pl.when(pl.program_id(0) == 0)
    def _():
        for part in range(2):
            held[part] = jnp.concatenate([b[part * 40:part * 40 + 40, :] for b in blocks], axis=0)

    total = jnp.dot(held[0], own_ref[...], preferred_element_type=F32)
    total += jnp.dot(held[1], other_ref[...], preferred_element_type=F32)
    out_ref[...] = total


def partial_ladder(blocks, own, other, width=256):
    count = len(blocks)
    rows, depth, columns = count * 40, own.shape[0], own.shape[1]
    whole = pl.BlockSpec(blocks[0].shape, lambda n: (0, 0))
    weights = pl.BlockSpec((depth, width), lambda n: (0, n))
    return pl.pallas_call(
        functools.partial(part_kernel, count),
        out_shape=jax.ShapeDtypeStruct((rows, columns), F32),
        grid=(columns // width,),
        in_specs=[whole] * count + [weights] * 2,
        out_specs=pl.BlockSpec((rows, width), lambda n: (0, n)),
        scratch_shapes=[pltpu.VMEM((2, rows, depth), BF16)],
        compiler_params=params(),
        cost_estimate=pl.CostEstimate(flops=4 * rows * depth * columns, bytes_accessed=4 * depth * columns, transcendentals=0),
    )(*blocks, own, other)


def last_kernel(place_ref, s0, s1, s2, s3, own_ref, other_ref, in_ref, row_ref, col_ref, *refs):
    remote, out_ref = refs[:Z], refs[Z]
    held, total = refs[Z + 1], refs[Z + 2]
    y, z = place_ref[0], place_ref[1]
    for j, slot in enumerate((s0, s1, s2, s3)):

        @pl.when(pl.program_id(0) == 0)
        def _(j=j, slot=slot):
            held[lax.rem(j + 4 - y, 4)] = slot[...]

    for dz in range(Z):
        total[lax.rem(z + dz, Z)] = remote[dz][...]
    for a, (mine, mate) in enumerate(((0, 2), (3, 1))):
        ladder = jnp.dot(held[mine], own_ref[...], preferred_element_type=F32)
        ladder += jnp.dot(held[mate], other_ref[...], preferred_element_type=F32)
        ladder += jnp.concatenate([total[i, a * 20:a * 20 + 20] for i in range(Z)], axis=0)
        rows = pl.ds(a * 160, 160)
        out_ref[rows, :] = in_ref[rows, :] + (row_ref[rows, :] * col_ref[...]) * ladder


def finish(place, slots, own, other, residual, row, col, remote, width=256):
    depth, columns = own.shape
    slot = pl.BlockSpec(slots[0].shape, lambda n: (0, 0))
    weights = pl.BlockSpec((depth, width), lambda n: (0, n))
    wide = pl.BlockSpec((residual.shape[0], width), lambda n: (0, n))
    return pl.pallas_call(
        last_kernel,
        out_shape=jax.ShapeDtypeStruct(residual.shape, F32),
        grid=(columns // width,),
        in_specs=[SMEM] + [slot] * 4 + [weights] * 2 + [wide]
        + [pl.BlockSpec(row.shape, lambda n: (0, 0)), pl.BlockSpec((1, width), lambda n: (0, n))]
        + [pl.BlockSpec((40, width), lambda n: (0, n))] * Z,
        out_specs=wide,
        scratch_shapes=[pltpu.VMEM((4, 160, depth), BF16), pltpu.VMEM((Z, 40, width), F32)],
        compiler_params=params(),
        cost_estimate=pl.CostEstimate(flops=4 * 320 * depth * columns, bytes_accessed=4 * depth * columns, transcendentals=0),
    )(place, *slots, own, other, residual, row, col, *remote)


def pair_scale(pairs):
    return jnp.where(pairs[:, 0] == pairs[:, 1], F32(0.5), F32(1.0))


def per_device(amplitudes, integrals, residual_in, pair_list, ab_list):
    xh, y, z, xl = (lax.axis_index(n) for n in ("xh", "y", "z", "xl"))
    place = jnp.stack([y, z]).astype(jnp.int32)
    row = pair_scale(pair_list)[:, None]
    col = pair_scale(ab_list)[None, :]

    mine = amplitudes.reshape(amplitudes.shape[0], -1)
    own = integrals.reshape(-1, integrals.shape[2])
    mates = lax.ppermute(mine, "xh", turn(2, 1))
    other = lax.ppermute(own, "core", turn(2, 1))
    leaves = xh != xl
    gone = jnp.where(leaves, mine, mates)
    kept = jnp.where(leaves, mates, mine)

    slots = [lax.ppermute(gone, ("y", "core"), to_core(j)) for j in range(4)]
    around = [kept] + [lax.ppermute(kept, "z", turn(Z, -dz)) for dz in range(1, Z)]

    block = pl.pallas_call(
        pack_pairs,
        out_shape=jax.ShapeDtypeStruct((80, 1600), BF16),
        in_specs=[SMEM] + [VMEM] * 4,
        out_specs=VMEM,
        scratch_shapes=[pltpu.VMEM((4, 20, 1600), BF16)],
        compiler_params=params(),
    )(place, *slots)
    stack = pl.pallas_call(
        pack_ring,
        out_shape=jax.ShapeDtypeStruct((160, 1600), BF16),
        in_specs=[SMEM] + [VMEM] * Z,
        out_specs=VMEM,
        scratch_shapes=[pltpu.VMEM((Z, 20, 1600), BF16)],
        compiler_params=params(),
    )(place, *around)

    ring = {0: block}
    for step in range(1, Z // 2):
        ring[step] = lax.ppermute(ring[step - 1], "z", turn(Z, -1))
        ring[-step] = lax.ppermute(ring[1 - step], "z", turn(Z, 1))
    ring[Z // 2] = lax.ppermute(ring[Z // 2 - 1], "z", turn(Z, -1))
    full = [lax.ppermute(stack, ("y", "core"), to_core(j)) for j in (0, 2, 1, 3)]
    full = [full[0], full[2], full[1], full[3]]

    remote = [None] * Z
    for group in ((0, 1, -1), (2, -2), (3, -3, 4)):
        part = partial_ladder([ring[d] for d in group], own, other).astype(F16)
        back = lax.ppermute(part, "xl", turn(XL, 1)).astype(F32)
        for n, d in enumerate(group):
            remote[d % Z] = back[40 * n:40 * n + 40]
    return finish(place, full, own, other, residual_in, row, col, remote)


def solution(mesh):
    fine = Mesh(mesh.devices.reshape(XH, Y, Z, XL, 2), BLK + DS)
    placed = (P(BLK, None, DS), P(None, DS, BLK), P(DS, BLK), P(DS, None), P(BLK, None))
    return jax.shard_map(per_device, mesh=fine, in_specs=placed, out_specs=P(DS, BLK), check_vma=False)
```

time: 389 us -> 120 us (0.31)
  waiting for transfers between devices: 341 us -> 42.8 us
  starting transfers between devices: 0.04 us -> 52.5 us
  Pallas kernels: 0 us -> 19.8 us
  blocking collectives: 14.6 us -> 0 us
  between operations: 13.4 us -> 0.3 us
  matrix products: 11.7 us -> 0 us
  local copies, waits for them, and re-layouts: 8.58 us -> 4.13 us
    all_gather x2 -> x0, waiting for transfers between devices: 340 us -> none  [the longest x1 222 us: per_device(): every_amp = lax.all_gather(full_amps, 'blk', axis=0, tiled=True)]
    ppermute x0 -> x27, starting transfers between devices: none -> 52.5 us  [the longest x3 11.9 us: per_device(): ring[step] = lax.ppermute(ring[step - 1], 'z', turn(Z, -1))]
    ppermute x0 -> x27, waiting for transfers between devices: none -> 42.8 us  [the longest x4 19.3 us: per_device(): lax.ppermute(stack, ('y', 'core'), to_core(j))]
    pallas_call x0 -> x6, Pallas kernels: none -> 19.8 us  [the longest x3 12 us: partial_ladder(): pl.pallas_call(functools.partial(part_kernel, count), out_shape=jax.Shape...]
    all_gather x1 -> x0, blocking collectives: 14.6 us -> none  [per_device(): full_amps = lax.all_gather(amplitudes, 'dsplit', axis=2, tiled=True)]
    dot_general x1 -> x0, matrix products: 11.7 us -> none  [per_device(): jnp.dot(mine.reshape(rows, -1), full_ints.reshape(-1, full_ints.shape[2])...]
    dynamic_slice x1 -> x0, local copies, waits for them, and re-layouts: 4.71 us -> none  [per_device(): mine = lax.dynamic_slice_in_dim(every_amp, first, rows, 0)]
  transfers between devices with their start and end apart: 2 -> 27, of which waited for: 2 -> 10; matrix products, arithmetic and copies ran while one was open for 1% -> 2% of each run, Pallas kernels for 0% -> 11%
where the time goes in v1:
time: 120 us
  starting transfers between devices  52.5 us (44%)
  waiting for transfers between devices  42.8 us (36%)
  Pallas kernels  19.8 us (16%)
  local copies, waits for them, and re-layouts  4.13 us (3%)
    ppermute x4, waiting for transfers between devices, per_device(): lax.ppermute(stack, ('y', 'core'), to_core(j))  19.3 us
    pallas_call x3, Pallas kernels, partial_ladder(): pl.pallas_call(functools.partial(part_kernel, count), out_shape=jax.Shape...  12 us
    ppermute x3, starting transfers between devices, per_device(): ring[step] = lax.ppermute(ring[step - 1], 'z', turn(Z, -1))  11.9 us
    ppermute x4, starting transfers between devices, per_device(): lax.ppermute(stack, ('y', 'core'), to_core(j))  11.2 us
    ppermute x7, starting transfers between devices, per_device(): lax.ppermute(kept, 'z', turn(Z, -dz))  10.9 us
    ppermute x3, waiting for transfers between devices, per_device(): ring[step] = lax.ppermute(ring[step - 1], 'z', turn(Z, -1))  9.81 us
    ppermute x4, starting transfers between devices, per_device(): slots = [lax.ppermute(gone, ('y', 'core'), to_core(j)) for j in range(4)]  8.17 us
    pallas_call x1, Pallas kernels, finish(): pl.pallas_call(last_kernel, out_shape=jax.ShapeDtypeStruct(residual.shape...  6.43 us
  transfers between devices with their start and end apart: 27, of which 10 were waited for; matrix products, arithmetic and copies ran while one was open for 2% of the time, Pallas kernels for 11%

profile of v1, /device:TPU:1, one launch (start us, length us, event | category | flops | bytes accessed | tf_op | source)
XLA Modules:
  0.0 119.7 jit_solution(5640260415122481510)
XLA Ops:
  0.0 3.2 %collective-permute-start.12 = (bf16[1600,1024]{1,0:T(8,128)(2,1)}, bf16[1600,1024]{1,0:T(8,128)(2,1)}, u32[]{:S(2)}, u32[]{:S(2)}) collective-permute-start(bf16[1600,1024]{1,0:T(8,128)(2,1)} %bitcast.5), channel_id=1, source_target_pairs={{0,1},{1,0},{2,3},{3,2},{4,5},{5,4},{6,7},{7,6},{8,9},{9,8},{10,11... | collective-permute-start | bytes 9830408 | tf_op jit(solution)/shard_map/ppermute | solution.py:128
  3.2 1.1 reshape.30
  4.3 1.1 collective-permute-start
  5.4 4.5 %collective-permute-done = bf16[20,1600]{1,0:T(8,128)(2,1)S(1)} collective-permute-done((bf16[20,1600]{1,0:T(8,128)(2,1)S(1)}, bf16[20,1600]{1,0:T(8,128)(2,1)S(1)}, u32[]{:S(2)}, u32[]{:S(2)}) %collective-permute-start) | collective-permute-done | bytes 64032 | tf_op jit(solution)/shard_map/ppermute | solution.py:127
  9.9 0.3 collective-permute-start.16
  10.2 3.7 %collective-permute-start.15 = (bf16[20,1600]{1,0:T(8,128)(2,1)S(1)}, bf16[20,1600]{1,0:T(8,128)(2,1)S(1)}, u32[]{:S(2)}, u32[]{:S(2)}) collective-permute-start(bf16[20,1600]{1,0:T(8,128)(2,1)S(1)} %get-tuple-element.13), channel_id=1, source_target_pairs={{0,64},{1,0},{32,96},{33,32},{64,1},{65,65},{96,33},{97,97},{2,66}... | collective-permute-start | bytes 192008 | tf_op jit(solution)/shard_map/ppermute | solution.py:133
  14.0 2.2 %collective-permute-start.14 = (bf16[20,1600]{1,0:T(8,128)(2,1)S(1)}, bf16[20,1600]{1,0:T(8,128)(2,1)S(1)}, u32[]{:S(2)}, u32[]{:S(2)}) collective-permute-start(bf16[20,1600]{1,0:T(8,128)(2,1)S(1)} %get-tuple-element.13), channel_id=1, source_target_pairs={{0,32},{1,96},{32,64},{33,0},{64,97},{65,33},{96,1},{97,65},{2,34}... | collective-permute-start | bytes 192008 | tf_op jit(solution)/shard_map/ppermute | solution.py:133
  16.2 1.9 %collective-permute-start.13 = (bf16[20,1600]{1,0:T(8,128)(2,1)S(1)}, bf16[20,1600]{1,0:T(8,128)(2,1)S(1)}, u32[]{:S(2)}, u32[]{:S(2)}) collective-permute-start(bf16[20,1600]{1,0:T(8,128)(2,1)S(1)} %get-tuple-element.13), channel_id=1, source_target_pairs={{0,0},{1,64},{32,32},{33,96},{64,65},{65,1},{96,97},{97,33},{2,2},... | collective-permute-start | bytes 192008 | tf_op jit(solution)/shard_map/ppermute | solution.py:133
  18.1 0.1 pad_add_fusion.place_ref
  18.2 0.9 collective-permute-done.14.refs_1_
  19.1 3.7 %collective-permute-done.13.refs_0_ = bf16[20,1600]{1,0:T(8,128)(2,1)S(1)} collective-permute-done((bf16[20,1600]{1,0:T(8,128)(2,1)S(1)}, bf16[20,1600]{1,0:T(8,128)(2,1)S(1)}, u32[]{:S(2)}, u32[]{:S(2)}) %collective-permute-start.13) | collective-permute-done | bytes 64032 | tf_op jit(solution)/shard_map/ppermute | solution.py:133
  22.9 0.6 shard_map.56.refs_0_
  23.5 5.7 %collective-permute-start.17 = (bf16[80,1600]{1,0:T(8,128)(2,1)S(1)}, bf16[80,1600]{1,0:T(8,128)(2,1)S(1)}, u32[]{:S(2)}, u32[]{:S(2)}) collective-permute-start(bf16[80,1600]{1,0:T(8,128)(2,1)S(1)} %shard_map.56.refs_0_), channel_id=1, source_target_pairs={{0,28},{4,0},{8,4},{12,8},{16,12},{20,16},{24,20},{28,24},{1,29},{... | collective-permute-start | bytes 768008 | tf_op jit(solution)/shard_map/ppermute | solution.py:155
  29.1 3.4 %collective-permute-done.17.refs_1_ = bf16[80,1600]{1,0:T(8,128)(2,1)S(1)} collective-permute-done((bf16[80,1600]{1,0:T(8,128)(2,1)S(1)}, bf16[80,1600]{1,0:T(8,128)(2,1)S(1)}, u32[]{:S(2)}, u32[]{:S(2)}) %collective-permute-start.17) | collective-permute-done | bytes 256032 | tf_op jit(solution)/shard_map/ppermute | solution.py:155
  32.5 3.1 %collective-permute-start.20 = (bf16[80,1600]{1,0:T(8,128)(2,1)S(1)}, bf16[80,1600]{1,0:T(8,128)(2,1)S(1)}, u32[]{:S(2)}, u32[]{:S(2)}) collective-permute-start(bf16[80,1600]{1,0:T(8,128)(2,1)S(1)} %collective-permute-done.17.refs_1_), channel_id=1, source_target_pairs={{0,28},{4,0},{8,4},{12,8},{16,12},{20,16},{24,20},{28,24},{1,29},{... | collective-permute-start | bytes 768008 | tf_op jit(solution)/shard_map/ppermute | solution.py:155
  35.6 3.4 %collective-permute-done.20.refs_0_ = bf16[80,1600]{1,0:T(8,128)(2,1)S(1)} collective-permute-done((bf16[80,1600]{1,0:T(8,128)(2,1)S(1)}, bf16[80,1600]{1,0:T(8,128)(2,1)S(1)}, u32[]{:S(2)}, u32[]{:S(2)}) %collective-permute-start.20) | collective-permute-done | bytes 256032 | tf_op jit(solution)/shard_map/ppermute | solution.py:155
  39.0 3.1 %collective-permute-start.23 = (bf16[80,1600]{1,0:T(8,128)(2,1)S(1)}, bf16[80,1600]{1,0:T(8,128)(2,1)S(1)}, u32[]{:S(2)}, u32[]{:S(2)}) collective-permute-start(bf16[80,1600]{1,0:T(8,128)(2,1)S(1)} %collective-permute-done.20.refs_0_), channel_id=1, source_target_pairs={{0,28},{4,0},{8,4},{12,8},{16,12},{20,16},{24,20},{28,24},{1,29},{... | collective-permute-start | bytes 768008 | tf_op jit(solution)/shard_map/ppermute | solution.py:155
  42.1 0.8 fusion.4
  42.9 0.1 copy.7
  43.0 0.1 copy.6
  43.2 0.1 collective-permute-start.24
  43.3 3.1 %collective-permute-done.23.refs_0_ = bf16[80,1600]{1,0:T(8,128)(2,1)S(1)} collective-permute-done((bf16[80,1600]{1,0:T(8,128)(2,1)S(1)}, bf16[80,1600]{1,0:T(8,128)(2,1)S(1)}, u32[]{:S(2)}, u32[]{:S(2)}) %collective-permute-start.23) | collective-permute-done | bytes 256032 | tf_op jit(solution)/shard_map/ppermute | solution.py:155
  46.4 3.1 %collective-permute-start.25 = (bf16[80,1600]{1,0:T(8,128)(2,1)S(1)}, bf16[80,1600]{1,0:T(8,128)(2,1)S(1)}, u32[]{:S(2)}, u32[]{:S(2)}) collective-permute-start(bf16[80,1600]{1,0:T(8,128)(2,1)S(1)} %collective-permute-done.23.refs_0_), channel_id=1, source_target_pairs={{0,28},{4,0},{8,4},{12,8},{16,12},{20,16},{24,20},{28,24},{1,29},{... | collective-permute-start | bytes 768008 | tf_op jit(solution)/shard_map/ppermute | solution.py:157
  49.5 0.1 collective-permute-start.7
  49.6 0.1 collective-permute-start.6
  49.7 1.3 %collective-permute-start.5 = (bf16[20,1600]{1,0:T(8,128)(2,1)S(1)}, bf16[20,1600]{1,0:T(8,128)(2,1)S(1)}, u32[]{:S(2)}, u32[]{:S(2)}) collective-permute-start(bf16[20,1600]{1,0:T(8,128)(2,1)S(1)} %get-tuple-element.14.refs_0_), channel_id=1, source_target_pairs={{0,12},{4,16},{8,20},{12,24},{16,28},{20,0},{24,4},{28,8},{1,13},{... | collective-permute-start | bytes 192008 | tf_op jit(solution)/shard_map/ppermute | solution.py:134
  51.0 1.9 %copy-done = bf16[8,200,1024]{2,1,0:T(8,128)(2,1)S(1)} copy-done((bf16[8,200,1024]{2,1,0:T(8,128)(2,1)S(1)}, bf16[8,200,1024]{2,1,0:T(8,128)(2,1)}, u32[]{:S(2)}) %copy-start) | copy-done | bytes 3276824
  53.0 4.1 %shard_map.57 = f32[120,1024]{1,0:T(8,128)S(1)} custom-call(bf16[80,1600]{1,0:T(8,128)(2,1)S(1)} %shard_map.56.refs_0_, bf16[80,1600]{1,0:T(8,128)(2,1)S(1)} %collective-permute-done.17.refs_1_, bf16[80,1600]{1,0:T(8,128)(2,1)S(1)} %collective-permute-done.18.refs_2_, bf16[1600,1024]{1,0:T(8,128)(2,1)S(1)} %bitcast.7, ...), custom_call_target="tpu_custom_call" | custom-call | flops 786432000 | bytes 6553600 | tf_op jit(solution)/shard_map/pallas_call | solution.py:64
  57.1 4.3 %collective-permute-start.4 = (bf16[20,1600]{1,0:T(8,128)(2,1)S(1)}, bf16[20,1600]{1,0:T(8,128)(2,1)S(1)}, u32[]{:S(2)}, u32[]{:S(2)}) collective-permute-start(bf16[20,1600]{1,0:T(8,128)(2,1)S(1)} %get-tuple-element.14.refs_0_), channel_id=1, source_target_pairs={{0,16},{4,20},{8,24},{12,28},{16,0},{20,4},{24,8},{28,12},{1,17},{... | collective-permute-start | bytes 192008 | tf_op jit(solution)/shard_map/ppermute | solution.py:134
  61.4 2.1 %collective-permute-start.3 = (bf16[20,1600]{1,0:T(8,128)(2,1)S(1)}, bf16[20,1600]{1,0:T(8,128)(2,1)S(1)}, u32[]{:S(2)}, u32[]{:S(2)}) collective-permute-start(bf16[20,1600]{1,0:T(8,128)(2,1)S(1)} %get-tuple-element.14.refs_0_), channel_id=1, source_target_pairs={{0,20},{4,24},{8,28},{12,0},{16,4},{20,8},{24,12},{28,16},{1,21},{... | collective-permute-start | bytes 192008 | tf_op jit(solution)/shard_map/ppermute | solution.py:134
  63.5 4.0 %shard_map.59 = f32[120,1024]{1,0:T(8,128)S(1)} custom-call(bf16[80,1600]{1,0:T(8,128)(2,1)S(1)} %collective-permute-done.23.refs_0_, bf16[80,1600]{1,0:T(8,128)(2,1)S(1)} %collective-permute-done.24.refs_1_, bf16[80,1600]{1,0:T(8,128)(2,1)S(1)} %collective-permute-done.25.refs_2_, bf16[1600,1024]{1,0:T(8,128)(2,1)S(1)} %bitcast.8, ...), custom_call_target="tpu_custom_call" | custom-call | flops 786432000 | bytes 6553600 | tf_op jit(solution)/shard_map/pallas_call | solution.py:64
  67.5 0.0 copy-start.3
  67.5 1.3 %collective-permute-start.26 = (f16[120,1024]{1,0:T(8,128)(2,1)S(1)}, f16[120,1024]{1,0:T(8,128)(2,1)S(1)}, u32[]{:S(2)}, u32[]{:S(2)}) collective-permute-start(f16[120,1024]{1,0:T(8,128)(2,1)S(1)} %convert_element_type.22), channel_id=1, source_target_pairs={{0,2},{2,0},{1,3},{3,1},{4,6},{6,4},{5,7},{7,5},{8,10},{10,8},{9,1... | collective-permute-start | bytes 737288 | tf_op jit(solution)/shard_map/ppermute | solution.py:164
  68.8 4.0 %shard_map.58 = f32[80,1024]{1,0:T(8,128)S(1)} custom-call(bf16[80,1600]{1,0:T(8,128)(2,1)S(1)} %collective-permute-done.20.refs_0_, bf16[80,1600]{1,0:T(8,128)(2,1)S(1)} %collective-permute-done.21.refs_1_, bf16[1600,1024]{1,0:T(8,128)(2,1)S(1)} %bitcast.9, bf16[1600,1024]{1,0:T(8,128)(2,1)} %collective-permute-done.12.refs_4_.refs_3_.other_ref), custom_call_target="tpu_custom_call" | custom-call | flops 524288000 | bytes 6553600 | tf_op jit(solution)/shard_map/pallas_call | solution.py:64
  72.9 1.6 %collective-permute-start.2 = (bf16[20,1600]{1,0:T(8,128)(2,1)S(1)}, bf16[20,1600]{1,0:T(8,128)(2,1)S(1)}, u32[]{:S(2)}, u32[]{:S(2)}) collective-permute-start(bf16[20,1600]{1,0:T(8,128)(2,1)S(1)} %get-tuple-element.14.refs_0_), channel_id=1, source_target_pairs={{0,24},{4,28},{8,0},{12,4},{16,8},{20,12},{24,16},{28,20},{1,25},{... | collective-permute-start | bytes 192008 | tf_op jit(solution)/shard_map/ppermute | solution.py:134
  74.5 1.4 %collective-permute-start.1 = (bf16[20,1600]{1,0:T(8,128)(2,1)S(1)}, bf16[20,1600]{1,0:T(8,128)(2,1)S(1)}, u32[]{:S(2)}, u32[]{:S(2)}) collective-permute-start(bf16[20,1600]{1,0:T(8,128)(2,1)S(1)} %get-tuple-element.14.refs_0_), channel_id=1, source_target_pairs={{0,28},{4,0},{8,4},{12,8},{16,12},{20,16},{24,20},{28,24},{1,29},{... | collective-permute-start | bytes 192008 | tf_op jit(solution)/shard_map/ppermute | solution.py:134
  75.9 0.3 collective-permute-start.22
  76.1 1.2 %collective-permute-start.19 = (f16[120,1024]{1,0:T(8,128)(2,1)S(1)}, f16[120,1024]{1,0:T(8,128)(2,1)S(1)}, u32[]{:S(2)}, u32[]{:S(2)}) collective-permute-start(f16[120,1024]{1,0:T(8,128)(2,1)S(1)} %convert_element_type.18), channel_id=1, source_target_pairs={{0,2},{2,0},{1,3},{3,1},{4,6},{6,4},{5,7},{7,5},{8,10},{10,8},{9,1... | collective-permute-start | bytes 737288 | tf_op jit(solution)/shard_map/ppermute | solution.py:164
  77.4 0.4 collective-permute-done.2.refs_2_
  77.7 4.0 %collective-permute-done.1.refs_1_ = bf16[20,1600]{1,0:T(8,128)(2,1)S(1)} collective-permute-done((bf16[20,1600]{1,0:T(8,128)(2,1)S(1)}, bf16[20,1600]{1,0:T(8,128)(2,1)S(1)}, u32[]{:S(2)}, u32[]{:S(2)}) %collective-permute-start.1) | collective-permute-done | bytes 64032 | tf_op jit(solution)/shard_map/ppermute | solution.py:134
  81.8 0.7 shard_map.55
  82.5 2.8 %collective-permute-start.11 = (bf16[160,1600]{1,0:T(8,128)(2,1)S(1)}, bf16[160,1600]{1,0:T(8,128)(2,1)S(1)}, u32[]{:S(2)}, u32[]{:S(2)}) collective-permute-start(bf16[160,1600]{1,0:T(8,128)(2,1)S(1)} %shard_map.55), channel_id=1, source_target_pairs={{0,96},{1,32},{32,0},{33,64},{64,33},{65,97},{96,65},{97,1},{2,98}... | collective-permute-start | bytes 1536008 | tf_op jit(solution)/shard_map/ppermute | solution.py:158
  85.2 6.5 %collective-permute-start.10 = (bf16[160,1600]{1,0:T(8,128)(2,1)S(1)}, bf16[160,1600]{1,0:T(8,128)(2,1)S(1)}, u32[]{:S(2)}, u32[]{:S(2)}) collective-permute-start(bf16[160,1600]{1,0:T(8,128)(2,1)S(1)} %shard_map.55), channel_id=1, source_target_pairs={{0,64},{1,0},{32,96},{33,32},{64,1},{65,65},{96,33},{97,97},{2,66}... | collective-permute-start | bytes 1536008 | tf_op jit(solution)/shard_map/ppermute | solution.py:158
  91.7 0.1 collective-permute-start.9
  91.8 1.9 %collective-permute-start.8 = (bf16[160,1600]{1,0:T(8,128)(2,1)S(1)}, bf16[160,1600]{1,0:T(8,128)(2,1)S(1)}, u32[]{:S(2)}, u32[]{:S(2)}) collective-permute-start(bf16[160,1600]{1,0:T(8,128)(2,1)S(1)} %shard_map.55), channel_id=1, source_target_pairs={{0,0},{1,64},{32,32},{33,96},{64,65},{65,1},{96,97},{97,33},{2,2},... | collective-permute-start | bytes 1536008 | tf_op jit(solution)/shard_map/ppermute | solution.py:158
  94.0 3.7 %collective-permute-done.11.s3 = bf16[160,1600]{1,0:T(8,128)(2,1)S(1)} collective-permute-done((bf16[160,1600]{1,0:T(8,128)(2,1)S(1)}, bf16[160,1600]{1,0:T(8,128)(2,1)S(1)}, u32[]{:S(2)}, u32[]{:S(2)}) %collective-permute-start.11) | collective-permute-done | bytes 512032 | tf_op jit(solution)/shard_map/ppermute | solution.py:158
  97.7 15.6 %collective-permute-done.9.s1 = bf16[160,1600]{1,0:T(8,128)(2,1)S(1)} collective-permute-done((bf16[160,1600]{1,0:T(8,128)(2,1)S(1)}, bf16[160,1600]{1,0:T(8,128)(2,1)S(1)}, u32[]{:S(2)}, u32[]{:S(2)}) %collective-permute-start.9) | collective-permute-done | bytes 512032 | tf_op jit(solution)/shard_map/ppermute | solution.py:158
  113.3 6.4 %shard_map.60 = f32[320,1024]{1,0:T(8,128)} custom-call(s32[2]{0:T(128)S(1)} %pad_add_fusion.place_ref, bf16[160,1600]{1,0:T(8,128)(2,1)S(1)} %collective-permute-done.8.s0, bf16[160,1600]{1,0:T(8,128)(2,1)S(1)} %collective-permute-done.9.s1, bf16[160,1600]{1,0:T(8,128)(2,1)S(1)} %collective-permute-done.10.s2, ...), custom_call_target="tpu_custom_call" | custom-call | flops 2097152000 | bytes 6553600 | tf_op jit(solution)/shard_map/pallas_call | solution.py:101
  (37 shorter events, 0.4 us)
Async XLA Ops:
  0.0 49.7 %collective-permute-start.12 = (bf16[1600,1024]{1,0:T(8,128)(2,1)}, bf16[1600,1024]{1,0:T(8,128)(2,1)}, u32[]{:S(2)}, u32[]{:S(2)}) collective-permute-start(bf16[1600,1024]{1,0:T(8,128)(2,1)} %bitcast.5), channel_id=1, source_target_pairs={{0,1},{1,0},{2,3},{3,2},{4,5},{5,4},{6,7},{7,6},{8,9},{9,8},{10,11... | collective-permute-start | bytes 9830408 | tf_op jit(solution)/shard_map/ppermute | solution.py:128
  4.3 5.6 %collective-permute-start = (bf16[20,1600]{1,0:T(8,128)(2,1)S(1)}, bf16[20,1600]{1,0:T(8,128)(2,1)S(1)}, u32[]{:S(2)}, u32[]{:S(2)}) collective-permute-start(bf16[20,1600]{1,0:T(8,128)(2,1)S(1)} %reshape.30), channel_id=1, source_target_pairs={{0,128},{128,0},{1,129},{129,1},{2,130},{130,2},{3,131},{131,3},{4... | collective-permute-start | bytes 192008 | tf_op jit(solution)/shard_map/ppermute | solution.py:127
  9.9 8.3 %collective-permute-start.16 = (bf16[20,1600]{1,0:T(8,128)(2,1)S(1)}, bf16[20,1600]{1,0:T(8,128)(2,1)S(1)}, u32[]{:S(2)}, u32[]{:S(2)}) collective-permute-start(bf16[20,1600]{1,0:T(8,128)(2,1)S(1)} %get-tuple-element.13), channel_id=1, source_target_pairs={{0,96},{1,32},{32,0},{33,64},{64,33},{65,97},{96,65},{97,1},{2,98}... | collective-permute-start | bytes 192008 | tf_op jit(solution)/shard_map/ppermute | solution.py:133
  10.2 8.0 %collective-permute-start.15 = (bf16[20,1600]{1,0:T(8,128)(2,1)S(1)}, bf16[20,1600]{1,0:T(8,128)(2,1)S(1)}, u32[]{:S(2)}, u32[]{:S(2)}) collective-permute-start(bf16[20,1600]{1,0:T(8,128)(2,1)S(1)} %get-tuple-element.13), channel_id=1, source_target_pairs={{0,64},{1,0},{32,96},{33,32},{64,1},{65,65},{96,33},{97,97},{2,66}... | collective-permute-start | bytes 192008 | tf_op jit(solution)/shard_map/ppermute | solution.py:133
  14.0 5.1 %collective-permute-start.14 = (bf16[20,1600]{1,0:T(8,128)(2,1)S(1)}, bf16[20,1600]{1,0:T(8,128)(2,1)S(1)}, u32[]{:S(2)}, u32[]{:S(2)}) collective-permute-start(bf16[20,1600]{1,0:T(8,128)(2,1)S(1)} %get-tuple-element.13), channel_id=1, source_target_pairs={{0,32},{1,96},{32,64},{33,0},{64,97},{65,33},{96,1},{97,65},{2,34}... | collective-permute-start | bytes 192008 | tf_op jit(solution)/shard_map/ppermute | solution.py:133
  16.2 6.7 %collective-permute-start.13 = (bf16[20,1600]{1,0:T(8,128)(2,1)S(1)}, bf16[20,1600]{1,0:T(8,128)(2,1)S(1)}, u32[]{:S(2)}, u32[]{:S(2)}) collective-permute-start(bf16[20,1600]{1,0:T(8,128)(2,1)S(1)} %get-tuple-element.13), channel_id=1, source_target_pairs={{0,0},{1,64},{32,32},{33,96},{64,65},{65,1},{96,97},{97,33},{2,2},... | collective-permute-start | bytes 192008 | tf_op jit(solution)/shard_map/ppermute | solution.py:133
  23.5 9.0 %collective-permute-start.17 = (bf16[80,1600]{1,0:T(8,128)(2,1)S(1)}, bf16[80,1600]{1,0:T(8,128)(2,1)S(1)}, u32[]{:S(2)}, u32[]{:S(2)}) collective-permute-start(bf16[80,1600]{1,0:T(8,128)(2,1)S(1)} %shard_map.56.refs_0_), channel_id=1, source_target_pairs={{0,28},{4,0},{8,4},{12,8},{16,12},{20,16},{24,20},{28,24},{1,29},{... | collective-permute-start | bytes 768008 | tf_op jit(solution)/shard_map/ppermute | solution.py:155
  29.1 6.5 %collective-permute-start.18 = (bf16[80,1600]{1,0:T(8,128)(2,1)S(1)}, bf16[80,1600]{1,0:T(8,128)(2,1)S(1)}, u32[]{:S(2)}, u32[]{:S(2)}) collective-permute-start(bf16[80,1600]{1,0:T(8,128)(2,1)S(1)} %shard_map.56.refs_0_), channel_id=1, source_target_pairs={{0,4},{4,8},{8,12},{12,16},{16,20},{20,24},{24,28},{28,0},{1,5},{5... | collective-permute-start | bytes 768008 | tf_op jit(solution)/shard_map/ppermute | solution.py:156
  32.5 6.5 %collective-permute-start.20 = (bf16[80,1600]{1,0:T(8,128)(2,1)S(1)}, bf16[80,1600]{1,0:T(8,128)(2,1)S(1)}, u32[]{:S(2)}, u32[]{:S(2)}) collective-permute-start(bf16[80,1600]{1,0:T(8,128)(2,1)S(1)} %collective-permute-done.17.refs_1_), channel_id=1, source_target_pairs={{0,28},{4,0},{8,4},{12,8},{16,12},{20,16},{24,20},{28,24},{1,29},{... | collective-permute-start | bytes 768008 | tf_op jit(solution)/shard_map/ppermute | solution.py:155
  35.6 7.5 %collective-permute-start.21 = (bf16[80,1600]{1,0:T(8,128)(2,1)S(1)}, bf16[80,1600]{1,0:T(8,128)(2,1)S(1)}, u32[]{:S(2)}, u32[]{:S(2)}) collective-permute-start(bf16[80,1600]{1,0:T(8,128)(2,1)S(1)} %collective-permute-done.18.refs_2_), channel_id=1, source_target_pairs={{0,4},{4,8},{8,12},{12,16},{16,20},{20,24},{24,28},{28,0},{1,5},{5... | collective-permute-start | bytes 768008 | tf_op jit(solution)/shard_map/ppermute | solution.py:156
  39.0 7.4 %collective-permute-start.23 = (bf16[80,1600]{1,0:T(8,128)(2,1)S(1)}, bf16[80,1600]{1,0:T(8,128)(2,1)S(1)}, u32[]{:S(2)}, u32[]{:S(2)}) collective-permute-start(bf16[80,1600]{1,0:T(8,128)(2,1)S(1)} %collective-permute-done.20.refs_0_), channel_id=1, source_target_pairs={{0,28},{4,0},{8,4},{12,8},{16,12},{20,16},{24,20},{28,24},{1,29},{... | collective-permute-start | bytes 768008 | tf_op jit(solution)/shard_map/ppermute | solution.py:155
  43.2 13.9 %collective-permute-start.24 = (bf16[80,1600]{1,0:T(8,128)(2,1)S(1)}, bf16[80,1600]{1,0:T(8,128)(2,1)S(1)}, u32[]{:S(2)}, u32[]{:S(2)}) collective-permute-start(bf16[80,1600]{1,0:T(8,128)(2,1)S(1)} %collective-permute-done.21.refs_1_), channel_id=1, source_target_pairs={{0,4},{4,8},{8,12},{12,16},{16,20},{20,24},{24,28},{28,0},{1,5},{5... | collective-permute-start | bytes 768008 | tf_op jit(solution)/shard_map/ppermute | solution.py:156
  46.4 15.0 %collective-permute-start.25 = (bf16[80,1600]{1,0:T(8,128)(2,1)S(1)}, bf16[80,1600]{1,0:T(8,128)(2,1)S(1)}, u32[]{:S(2)}, u32[]{:S(2)}) collective-permute-start(bf16[80,1600]{1,0:T(8,128)(2,1)S(1)} %collective-permute-done.23.refs_0_), channel_id=1, source_target_pairs={{0,28},{4,0},{8,4},{12,8},{16,12},{20,16},{24,20},{28,24},{1,29},{... | collective-permute-start | bytes 768008 | tf_op jit(solution)/shard_map/ppermute | solution.py:157
  49.5 18.0 %collective-permute-start.7 = (bf16[20,1600]{1,0:T(8,128)(2,1)S(1)}, bf16[20,1600]{1,0:T(8,128)(2,1)S(1)}, u32[]{:S(2)}, u32[]{:S(2)}) collective-permute-start(bf16[20,1600]{1,0:T(8,128)(2,1)S(1)} %get-tuple-element.14.refs_0_), channel_id=1, source_target_pairs={{0,4},{4,8},{8,12},{12,16},{16,20},{20,24},{24,28},{28,0},{1,5},{5... | collective-permute-start | bytes 192008 | tf_op jit(solution)/shard_map/ppermute | solution.py:134
  49.6 23.3 %collective-permute-start.6 = (bf16[20,1600]{1,0:T(8,128)(2,1)S(1)}, bf16[20,1600]{1,0:T(8,128)(2,1)S(1)}, u32[]{:S(2)}, u32[]{:S(2)}) collective-permute-start(bf16[20,1600]{1,0:T(8,128)(2,1)S(1)} %get-tuple-element.14.refs_0_), channel_id=1, source_target_pairs={{0,8},{4,12},{8,16},{12,20},{16,24},{20,28},{24,0},{28,4},{1,9},{5... | collective-permute-start | bytes 192008 | tf_op jit(solution)/shard_map/ppermute | solution.py:134
  49.7 24.8 %collective-permute-start.5 = (bf16[20,1600]{1,0:T(8,128)(2,1)S(1)}, bf16[20,1600]{1,0:T(8,128)(2,1)S(1)}, u32[]{:S(2)}, u32[]{:S(2)}) collective-permute-start(bf16[20,1600]{1,0:T(8,128)(2,1)S(1)} %get-tuple-element.14.refs_0_), channel_id=1, source_target_pairs={{0,12},{4,16},{8,20},{12,24},{16,28},{20,0},{24,4},{28,8},{1,13},{... | collective-permute-start | bytes 192008 | tf_op jit(solution)/shard_map/ppermute | solution.py:134
  51.0 1.9 %copy-start = (bf16[8,200,1024]{2,1,0:T(8,128)(2,1)S(1)}, bf16[8,200,1024]{2,1,0:T(8,128)(2,1)}, u32[]{:S(2)}) copy-start(bf16[8,200,1024]{2,1,0:T(8,128)(2,1)} %param.6) | copy-start | bytes 9830404
  52.9 10.5 %copy-start.1 = (bf16[8,200,1024]{2,1,0:T(8,128)(2,1)S(1)}, bf16[8,200,1024]{2,1,0:T(8,128)(2,1)}, u32[]{:S(2)}) copy-start(bf16[8,200,1024]{2,1,0:T(8,128)(2,1)} %param.6) | copy-start | bytes 9830404
  57.1 18.8 %collective-permute-start.4 = (bf16[20,1600]{1,0:T(8,128)(2,1)S(1)}, bf16[20,1600]{1,0:T(8,128)(2,1)S(1)}, u32[]{:S(2)}, u32[]{:S(2)}) collective-permute-start(bf16[20,1600]{1,0:T(8,128)(2,1)S(1)} %get-tuple-element.14.refs_0_), channel_id=1, source_target_pairs={{0,16},{4,20},{8,24},{12,28},{16,0},{20,4},{24,8},{28,12},{1,17},{... | collective-permute-start | bytes 192008 | tf_op jit(solution)/shard_map/ppermute | solution.py:134
  61.4 14.8 %collective-permute-start.3 = (bf16[20,1600]{1,0:T(8,128)(2,1)S(1)}, bf16[20,1600]{1,0:T(8,128)(2,1)S(1)}, u32[]{:S(2)}, u32[]{:S(2)}) collective-permute-start(bf16[20,1600]{1,0:T(8,128)(2,1)S(1)} %get-tuple-element.14.refs_0_), channel_id=1, source_target_pairs={{0,20},{4,24},{8,28},{12,0},{16,4},{20,8},{24,12},{28,16},{1,21},{... | collective-permute-start | bytes 192008 | tf_op jit(solution)/shard_map/ppermute | solution.py:134
  67.5 9.9 %copy-start.3 = (s32[1024,2]{0,1:T(2,128)S(1)}, s32[1024,2]{0,1:T(2,128)}, u32[]{:S(2)}) copy-start(s32[1024,2]{0,1:T(2,128)} %param.9) | copy-start | bytes 24580
  67.5 24.3 %collective-permute-start.26 = (f16[120,1024]{1,0:T(8,128)(2,1)S(1)}, f16[120,1024]{1,0:T(8,128)(2,1)S(1)}, u32[]{:S(2)}, u32[]{:S(2)}) collective-permute-start(f16[120,1024]{1,0:T(8,128)(2,1)S(1)} %convert_element_type.22), channel_id=1, source_target_pairs={{0,2},{2,0},{1,3},{3,1},{4,6},{6,4},{5,7},{7,5},{8,10},{10,8},{9,1... | collective-permute-start | bytes 737288 | tf_op jit(solution)/shard_map/ppermute | solution.py:164
  72.8 40.5 %copy-start.2 = (f32[320,1024]{1,0:T(8,128)S(1)}, f32[320,1024]{1,0:T(8,128)}, u32[]{:S(2)}) copy-start(f32[320,1024]{1,0:T(8,128)} %in_ref.1) | copy-start | bytes 3932164
  72.9 4.8 %collective-permute-start.2 = (bf16[20,1600]{1,0:T(8,128)(2,1)S(1)}, bf16[20,1600]{1,0:T(8,128)(2,1)S(1)}, u32[]{:S(2)}, u32[]{:S(2)}) collective-permute-start(bf16[20,1600]{1,0:T(8,128)(2,1)S(1)} %get-tuple-element.14.refs_0_), channel_id=1, source_target_pairs={{0,24},{4,28},{8,0},{12,4},{16,8},{20,12},{24,16},{28,20},{1,25},{... | collective-permute-start | bytes 192008 | tf_op jit(solution)/shard_map/ppermute | solution.py:134
  74.5 7.3 %collective-permute-start.1 = (bf16[20,1600]{1,0:T(8,128)(2,1)S(1)}, bf16[20,1600]{1,0:T(8,128)(2,1)S(1)}, u32[]{:S(2)}, u32[]{:S(2)}) collective-permute-start(bf16[20,1600]{1,0:T(8,128)(2,1)S(1)} %get-tuple-element.14.refs_0_), channel_id=1, source_target_pairs={{0,28},{4,0},{8,4},{12,8},{16,12},{20,16},{24,20},{28,24},{1,29},{... | collective-permute-start | bytes 192008 | tf_op jit(solution)/shard_map/ppermute | solution.py:134
  75.9 15.8 %collective-permute-start.22 = (f16[80,1024]{1,0:T(8,128)(2,1)S(1)}, f16[80,1024]{1,0:T(8,128)(2,1)S(1)}, u32[]{:S(2)}, u32[]{:S(2)}) collective-permute-start(f16[80,1024]{1,0:T(8,128)(2,1)S(1)} %convert_element_type.20), channel_id=1, source_target_pairs={{0,2},{2,0},{1,3},{3,1},{4,6},{6,4},{5,7},{7,5},{8,10},{10,8},{9,1... | collective-permute-start | bytes 491528 | tf_op jit(solution)/shard_map/ppermute | solution.py:164
  76.1 17.7 %collective-permute-start.19 = (f16[120,1024]{1,0:T(8,128)(2,1)S(1)}, f16[120,1024]{1,0:T(8,128)(2,1)S(1)}, u32[]{:S(2)}, u32[]{:S(2)}) collective-permute-start(f16[120,1024]{1,0:T(8,128)(2,1)S(1)} %convert_element_type.18), channel_id=1, source_target_pairs={{0,2},{2,0},{1,3},{3,1},{4,6},{6,4},{5,7},{7,5},{8,10},{10,8},{9,1... | collective-permute-start | bytes 737288 | tf_op jit(solution)/shard_map/ppermute | solution.py:164
  82.5 15.2 %collective-permute-start.11 = (bf16[160,1600]{1,0:T(8,128)(2,1)S(1)}, bf16[160,1600]{1,0:T(8,128)(2,1)S(1)}, u32[]{:S(2)}, u32[]{:S(2)}) collective-permute-start(bf16[160,1600]{1,0:T(8,128)(2,1)S(1)} %shard_map.55), channel_id=1, source_target_pairs={{0,96},{1,32},{32,0},{33,64},{64,33},{65,97},{96,65},{97,1},{2,98}... | collective-permute-start | bytes 1536008 | tf_op jit(solution)/shard_map/ppermute | solution.py:158
  85.2 12.5 %collective-permute-start.10 = (bf16[160,1600]{1,0:T(8,128)(2,1)S(1)}, bf16[160,1600]{1,0:T(8,128)(2,1)S(1)}, u32[]{:S(2)}, u32[]{:S(2)}) collective-permute-start(bf16[160,1600]{1,0:T(8,128)(2,1)S(1)} %shard_map.55), channel_id=1, source_target_pairs={{0,64},{1,0},{32,96},{33,32},{64,1},{65,65},{96,33},{97,97},{2,66}... | collective-permute-start | bytes 1536008 | tf_op jit(solution)/shard_map/ppermute | solution.py:158
  91.7 21.6 %collective-permute-start.9 = (bf16[160,1600]{1,0:T(8,128)(2,1)S(1)}, bf16[160,1600]{1,0:T(8,128)(2,1)S(1)}, u32[]{:S(2)}, u32[]{:S(2)}) collective-permute-start(bf16[160,1600]{1,0:T(8,128)(2,1)S(1)} %shard_map.55), channel_id=1, source_target_pairs={{0,32},{1,96},{32,64},{33,0},{64,97},{65,33},{96,1},{97,65},{2,34}... | collective-permute-start | bytes 1536008 | tf_op jit(solution)/shard_map/ppermute | solution.py:158
  91.8 21.5 %collective-permute-start.8 = (bf16[160,1600]{1,0:T(8,128)(2,1)S(1)}, bf16[160,1600]{1,0:T(8,128)(2,1)S(1)}, u32[]{:S(2)}, u32[]{:S(2)}) collective-permute-start(bf16[160,1600]{1,0:T(8,128)(2,1)S(1)} %shard_map.55), channel_id=1, source_target_pairs={{0,0},{1,64},{32,32},{33,96},{64,65},{65,1},{96,97},{97,33},{2,2},... | collective-permute-start | bytes 1536008 | tf_op jit(solution)/shard_map/ppermute | solution.py:158

commit v2 on v0

v2 whole, which is shorter than its diff:
```python
import jax
import jax.numpy as jnp
from jax import lax
from jax.experimental import pallas as pl
from jax.experimental.pallas import tpu as pltpu
from jax.sharding import Mesh
from jax.sharding import PartitionSpec as P

XH, Y, Z, XL = 2, 4, 8, 2
BLK = ("xh", "y", "z")
DS = ("xl", "core")
VMEM = pl.BlockSpec(memory_space=pltpu.VMEM)
SMEM = pl.BlockSpec(memory_space=pltpu.SMEM)
F32, BF16, F16 = jnp.float32, jnp.bfloat16, jnp.float16
MIB = 1024 * 1024


def turn(n, step):
    return [(i, (i + step) % n) for i in range(n)]


def ring(x):
    route = [(2 * z + c, 2 * ((z + 2 * c - 1) % Z) + c) for z in range(Z) for c in range(2)]
    return lax.ppermute(x, ("z", "core"), route)


def swap(x):
    route = [(2 * y + c, 2 * (3 - y if c else y ^ 1) + c) for y in range(Y) for c in range(2)]
    return lax.ppermute(x, ("y", "core"), route)


def cross(x, flip, hop):
    route = [(x * Y + y, (x ^ flip) * Y + (y ^ (2 * hop))) for x in range(XH) for y in range(Y)]
    return lax.ppermute(x, ("xh", "y"), route)


def mate(x):
    return lax.ppermute(x, "core", turn(2, 1))


def trade(x):
    return lax.ppermute(x, "xl", turn(XL, 1)).astype(F32)


def pack_kernel(place_ref, s0, s1, s2, s3, out_ref, held):
    for n, slot in enumerate((s0, s1, s2, s3)):
        kind = jnp.bitwise_xor(place_ref[2], n // 2)
        side = jnp.bitwise_xor(place_ref[3], n % 2)
        held[2 * side + kind] = slot[...]
    out_ref[...] = jnp.concatenate([held[n] for n in range(4)], axis=0)


def pack(place, *slots):
    rows, depth = slots[0].shape
    return pl.pallas_call(
        pack_kernel,
        out_shape=jax.ShapeDtypeStruct((4 * rows, depth), BF16),
        in_specs=[SMEM] + [VMEM] * 4,
        out_specs=VMEM,
        scratch_shapes=[pltpu.VMEM((4, rows, depth), BF16)],
        compiler_params=pltpu.CompilerParams(vmem_limit_bytes=4 * MIB),
    )(place, *slots)


def join_kernel(mine_ref, mate_ref, out_ref):
    other = mate_ref[...]
    out_ref[...] = jnp.concatenate([mine_ref[...], jnp.concatenate([other[40:], other[:40]], axis=0)], axis=1)


def join(mine, other):
    return pl.pallas_call(
        join_kernel,
        out_shape=jax.ShapeDtypeStruct((mine.shape[0], 2 * mine.shape[1]), BF16),
        in_specs=[VMEM] * 2,
        out_specs=VMEM,
        compiler_params=pltpu.CompilerParams(vmem_limit_bytes=4 * MIB),
    )(mine, other)


def collect(count, *parts):
    def kernel(*refs):
        pieces = [r[at:at + count, :] for r, (_, at) in zip(refs, parts)]
        refs[-1][...] = jnp.concatenate(pieces, axis=0)

    return pl.pallas_call(
        kernel,
        out_shape=jax.ShapeDtypeStruct((count * len(parts), parts[0][0].shape[1]), F32),
        in_specs=[VMEM] * len(parts),
        out_specs=VMEM,
        compiler_params=pltpu.CompilerParams(vmem_limit_bytes=4 * MIB),
    )(*[p for p, _ in parts])


def last_kernel(place_ref, in_ref, row_ref, col_ref, *refs):
    h0, s0, h1, s1, h2, s2, h3, s3, h4, s4, c1, c2, c3, b0, b2, b3, b4, out_ref, total, done, sems = refs
    here, there = place_ref[0] % 2, 1 - place_ref[0] % 2
    z, turned = place_ref[1], place_ref[4]

    def put(half, shift, kept, at, back, start):
        value = kept[at:at + 20, :] + back[start:start + 20, :]
        total[half, lax.rem(z + shift + Z, Z)] = value

    put(here, 0, h0, 0, b0, 0)
    put(there, 0, s0, 0, b0, 20)
    put(here, 4, h4, 0, b4, 0)
    put(there, 4, s4, 0, b4, 20)
    for step, h, s, c, back, start in ((1, h1, s1, c1, b0, 40), (2, h2, s2, c2, b2, 0), (3, h3, s3, c3, b3, 0)):
        put(here, turned * step, h, 0, back, start)
        put(there, turned * step, s, 0, back, start + 20)
        put(here, -turned * step, c, 0, back, start + 40)
        put(there, -turned * step, c, 40, back, start + 60)
    copies = []
    for n in range(4):
        a, first = n // 2, 4 * (n % 2)
        rows = pl.ds(n * 80, 80)
        ladder = jnp.concatenate([total[a, i] for i in range(first, first + 4)], axis=0)
        done[rows, :] = in_ref[rows, :] + (row_ref[rows, :] * col_ref[...]) * ladder
        copies.append(pltpu.make_async_copy(done.at[rows], out_ref.at[rows], sems.at[n]))
        copies[-1].start()
    for copy in copies:
        copy.wait()


def finish(place, residual, row, col, parts):
    return pl.pallas_call(
        last_kernel,
        out_shape=jax.ShapeDtypeStruct(residual.shape, F32),
        in_specs=[SMEM] + [VMEM] * (3 + len(parts)),
        out_specs=pl.BlockSpec(memory_space=pl.ANY),
        scratch_shapes=[
            pltpu.VMEM((2, Z, 20, residual.shape[1]), F32),
            pltpu.VMEM(residual.shape, F32),
            pltpu.SemaphoreType.DMA((4,)),
        ],
        compiler_params=pltpu.CompilerParams(vmem_limit_bytes=12 * MIB),
    )(place, residual, row, col, *parts)


def pair_scale(pairs):
    return jnp.where(pairs[:, 0] == pairs[:, 1], F32(0.5), F32(1.0))


def per_device(amplitudes, integrals, residual_in, pair_list, ab_list):
    xh, y, z, xl, core = (lax.axis_index(n) for n in ("xh", "y", "z", "xl", "core"))
    place = jnp.stack([y, z, xh != xl, (y // 2) ^ core, 1 - 2 * core]).astype(jnp.int32)
    row = pair_scale(pair_list)[:, None]
    col = pair_scale(ab_list)[None, :]
    tie = lax.optimization_barrier

    mine = amplitudes.reshape(amplitudes.shape[0], -1)
    own = integrals.reshape(-1, integrals.shape[2])
    slots = [cross(mine, n // 2, n % 2) for n in (3, 2, 1)] + [mine]
    slots = slots[::-1]
    other = mate(own)
    slots, other = tie((slots, other))
    weights = jnp.concatenate([own, other], axis=0)

    def dot(x):
        return jnp.dot(x, weights, preferred_element_type=F32)

    def low(*parts):
        return collect(20, *parts).astype(F16)

    def share(h, s):
        return mate(collect(40, (h, 40), (s, 40)))

    mine = pack(place, *slots)
    held0 = join(mine, mate(mine))
    held1, swap0 = ring(held0), swap(held0[:40])
    held1, weights = tie((held1, weights))
    held2, swap1 = ring(held1), swap(held1)
    h0, s0, h1 = dot(held0[:40]), dot(swap0), dot(held1)
    held2, h0, s0, h1 = tie((held2, h0, s0, h1))
    held3, swap2 = ring(held2), swap(held2)
    s1, h2 = dot(swap1), dot(held2)
    c1 = share(h1, s1)
    goes0 = low((h0, 20), (s0, 20), (h1, 20), (s1, 20), (c1, 20), (c1, 60))
    held3, goes0, h2 = tie((held3, goes0, h2))
    swap3, held4 = swap(held3), ring(held3[:40])
    b0 = trade(goes0)
    s2, h3 = dot(swap2), dot(held3)
    held4, s2, h3 = tie((held4, s2, h3))
    swap4 = swap(held4)
    c2 = share(h2, s2)
    b2 = trade(low((h2, 20), (s2, 20), (c2, 20), (c2, 60)))
    h4, s3 = dot(held4), dot(swap3)
    c3 = share(h3, s3)
    swap4, c2, c3, h4 = tie((swap4, c2, c3, h4))
    b3 = trade(low((h3, 20), (s3, 20), (c3, 20), (c3, 60)))
    s4 = dot(swap4)
    b4 = trade(low((h4, 20), (s4, 20)))
    parts = (h0, s0, h1, s1, h2, s2, h3, s3, h4, s4, c1, c2, c3, b0, b2, b3, b4)
    return finish(place, residual_in, row, col, parts)


def solution(mesh):
    fine = Mesh(mesh.devices.reshape(XH, Y, Z, XL, 2), BLK + DS)
    placed = (P(BLK, None, DS), P(None, DS, BLK), P(DS, BLK), P(DS, None), P(BLK, None))
    return jax.shard_map(per_device, mesh=fine, in_specs=placed, out_specs=P(DS, BLK), check_vma=False)
```

time: 389 us -> 80 us (0.21)
  waiting for transfers between devices: 341 us -> 28.1 us
  starting transfers between devices: 0.04 us -> 29.6 us
  blocking collectives: 14.6 us -> 0 us
  between operations: 13.4 us -> 0.42 us
  local copies, waits for them, and re-layouts: 8.58 us -> 2.24 us
    all_gather x2 -> x0, waiting for transfers between devices: 340 us -> none  [the longest x1 222 us: per_device(): every_amp = lax.all_gather(full_amps, 'blk', axis=0, tiled=True)]
    ppermute x0 -> x21, starting transfers between devices: none -> 29.6 us  [the longest x5 16.5 us: mate(): return lax.ppermute(x, 'core', turn(2, 1))]
    ppermute x0 -> x21, waiting for transfers between devices: none -> 28.1 us  [the longest x4 14.9 us: ring(): return lax.ppermute(x, ('z', 'core'), route)]
    all_gather x1 -> x0, blocking collectives: 14.6 us -> none  [per_device(): full_amps = lax.all_gather(amplitudes, 'dsplit', axis=2, tiled=True)]
    dynamic_slice x1 -> x0, local copies, waits for them, and re-layouts: 4.71 us -> none  [per_device(): mine = lax.dynamic_slice_in_dim(every_amp, first, rows, 0)]
    dot_general x1 -> x10, matrix products: 11.7 us -> 12.7 us  [dot(): return jnp.dot(x, weights, preferred_element_type=F32)]
  transfers between devices with their start and end apart: 2 -> 21, of which waited for: 2 -> 10; matrix products, arithmetic and copies ran while one was open for 1% -> 24% of each run, Pallas kernels for 0% -> 0%
where the time goes in v2:
time: 80 us; the launch traced here: 79.8 us
  starting transfers between devices  29.6 us (37%)
  waiting for transfers between devices  28.1 us (35%)
  matrix products  12.7 us (16%)
  other arithmetic  3.88 us (5%)
  Pallas kernels  2.86 us (4%)
  local copies, waits for them, and re-layouts  2.24 us (3%)
    ppermute x5, starting transfers between devices, mate(): return lax.ppermute(x, 'core', turn(2, 1))  16.5 us
    ppermute x4, waiting for transfers between devices, ring(): return lax.ppermute(x, ('z', 'core'), route)  14.9 us
    dot_general x10, matrix products, dot(): return jnp.dot(x, weights, preferred_element_type=F32)  12.7 us
    ppermute x4, waiting for transfers between devices, trade(): return lax.ppermute(x, 'xl', turn(XL, 1)).astype(F32)  5.94 us
    ppermute x3, starting transfers between devices, cross(): return lax.ppermute(x, ('xh', 'y'), route)  5.74 us
    ppermute x3, waiting for transfers between devices, cross(): return lax.ppermute(x, ('xh', 'y'), route)  5.36 us
    concatenate x1, other arithmetic, per_device(): weights = jnp.concatenate([own, other], axis=0)  3.68 us
    ppermute x5, starting transfers between devices, swap(): return lax.ppermute(x, ('y', 'core'), route)  3.15 us
  transfers between devices with their start and end apart: 21, of which 10 were waited for; matrix products, arithmetic and copies ran while one was open for 24% of the time, Pallas kernels for 0%

profile of v2, /device:TPU:1, one launch (start us, length us, event | category | flops | bytes accessed | tf_op | source)
XLA Modules:
  0.0 79.8 jit_solution(10435388780775617772)
XLA Ops:
  0.0 3.2 %collective-permute-start.3 = (bf16[1600,1024]{1,0:T(8,128)(2,1)}, bf16[1600,1024]{1,0:T(8,128)(2,1)}, u32[]{:S(2)}, u32[]{:S(2)}) collective-permute-start(bf16[1600,1024]{1,0:T(8,128)(2,1)} %bitcast.27), channel_id=1, source_target_pairs={{0,1},{1,0},{2,3},{3,2},{4,5},{5,4},{6,7},{7,6},{8,9},{9,8},{10,11... | collective-permute-start | bytes 9830408 | tf_op jit(solution)/shard_map/ppermute | solution.py:38
  3.2 1.1 %reshape.30.s0 = bf16[20,1600]{1,0:T(8,128)(2,1)S(1)} reshape(bf16[20,8,200]{2,1,0:T(8,128)(2,1)} %param.5) | data formatting | bytes 128000 | tf_op jit(solution)/shard_map/reshape | solution.py:150
  4.3 1.3 %collective-permute-start = (bf16[20,1600]{1,0:T(8,128)(2,1)S(1)}, bf16[20,1600]{1,0:T(8,128)(2,1)S(1)}, u32[]{:S(2)}, u32[]{:S(2)}) collective-permute-start(bf16[20,1600]{1,0:T(8,128)(2,1)S(1)} %reshape.30.s0), channel_id=1, source_target_pairs={{0,64},{32,96},{64,0},{96,32},{128,192},{160,224},{192,128},{224,1... | collective-permute-start | bytes 192008 | tf_op jit(solution)/shard_map/ppermute | solution.py:34
  5.6 2.7 %collective-permute-start.1 = (bf16[20,1600]{1,0:T(8,128)(2,1)S(1)}, bf16[20,1600]{1,0:T(8,128)(2,1)S(1)}, u32[]{:S(2)}, u32[]{:S(2)}) collective-permute-start(bf16[20,1600]{1,0:T(8,128)(2,1)S(1)} %reshape.30.s0), channel_id=1, source_target_pairs={{0,128},{32,160},{64,192},{96,224},{128,0},{160,32},{192,64},{224,... | collective-permute-start | bytes 192008 | tf_op jit(solution)/shard_map/ppermute | solution.py:34
  8.3 1.7 %collective-permute-start.2 = (bf16[20,1600]{1,0:T(8,128)(2,1)S(1)}, bf16[20,1600]{1,0:T(8,128)(2,1)S(1)}, u32[]{:S(2)}, u32[]{:S(2)}) collective-permute-start(bf16[20,1600]{1,0:T(8,128)(2,1)S(1)} %reshape.30.s0), channel_id=1, source_target_pairs={{0,192},{32,224},{64,128},{96,160},{128,64},{160,96},{192,0},{224,... | collective-permute-start | bytes 192008 | tf_op jit(solution)/shard_map/ppermute | solution.py:34
  10.0 0.1 stack.27.place_ref
  10.1 0.7 collective-permute-done.1.s2
  10.8 4.7 %collective-permute-done.2.s3 = bf16[20,1600]{1,0:T(8,128)(2,1)S(1)} collective-permute-done((bf16[20,1600]{1,0:T(8,128)(2,1)S(1)}, bf16[20,1600]{1,0:T(8,128)(2,1)S(1)}, u32[]{:S(2)}, u32[]{:S(2)}) %collective-permute-start.2) | collective-permute-done | bytes 64032 | tf_op jit(solution)/shard_map/ppermute | solution.py:34
  15.5 0.6 shard_map.55.mine_ref
  16.1 1.8 %collective-permute-start.4 = (bf16[80,1600]{1,0:T(8,128)(2,1)S(1)}, bf16[80,1600]{1,0:T(8,128)(2,1)S(1)}, u32[]{:S(2)}, u32[]{:S(2)}) collective-permute-start(bf16[80,1600]{1,0:T(8,128)(2,1)S(1)} %shard_map.55.mine_ref), channel_id=1, source_target_pairs={{0,1},{1,0},{2,3},{3,2},{4,5},{5,4},{6,7},{7,6},{8,9},{9,8},{10,11... | collective-permute-start | bytes 768008 | tf_op jit(solution)/shard_map/ppermute | solution.py:38
  17.9 0.8 fusion.3
  18.7 0.1 copy.6
  18.8 0.1 copy.7
  19.0 0.1 collective-permute-done.4.mate_ref
  19.1 0.1 shard_map.56
  19.2 1.7 %collective-permute-start.5 = (bf16[80,3200]{1,0:T(8,128)(2,1)S(1)}, bf16[80,3200]{1,0:T(8,128)(2,1)S(1)}, u32[]{:S(2)}, u32[]{:S(2)}) collective-permute-start(bf16[80,3200]{1,0:T(8,128)(2,1)S(1)} %shard_map.56), channel_id=1, source_target_pairs={{0,28},{1,5},{4,0},{5,9},{8,4},{9,13},{12,8},{13,17},{16,12},{17,2... | collective-permute-start | bytes 1536008 | tf_op jit(solution)/shard_map/ppermute | solution.py:24
  20.9 3.7 %pad_maximum_fusion = bf16[3200,1024]{1,0:T(8,128)(2,1)S(1)} fusion(bf16[1600,1024]{1,0:T(8,128)(2,1)} %collective-permute-done.3, bf16[1600,1024]{1,0:T(8,128)(2,1)} %bitcast.28), kind=kLoop, calls=%fused_computation | loop fusion | flops 13107200 | bytes 13107200 | tf_op jit(solution)/shard_map/concatenate | solution.py:156
  24.6 0.9 %collective-permute-start.7 = (bf16[40,3200]{1,0:T(8,128)(2,1)S(1)}, bf16[40,3200]{1,0:T(8,128)(2,1)S(1)}, u32[]{:S(2)}, u32[]{:S(2)}) collective-permute-start(bf16[40,3200]{1,0:T(8,128)(2,1)S(1)} %slice.25), channel_id=1, source_target_pairs={{0,32},{1,97},{32,0},{33,65},{64,96},{65,33},{96,64},{97,1},{2,34}... | collective-permute-start | bytes 768008 | tf_op jit(solution)/shard_map/ppermute | solution.py:29
  25.5 5.8 %collective-permute-done.5 = bf16[80,3200]{1,0:T(8,128)(2,1)S(1)} collective-permute-done((bf16[80,3200]{1,0:T(8,128)(2,1)S(1)}, bf16[80,3200]{1,0:T(8,128)(2,1)S(1)}, u32[]{:S(2)}, u32[]{:S(2)}) %collective-permute-start.5) | collective-permute-done | bytes 512032 | tf_op jit(solution)/shard_map/ppermute | solution.py:24
  31.3 0.8 collective-permute-start.8
  32.1 1.2 %fusion.1.refs_0_ = f32[40,1024]{1,0:T(8,128)S(1)} fusion(bf16[3200,1024]{1,0:T(8,128)(2,1)S(1)} %pad_maximum_fusion, bf16[80,3200]{1,0:T(8,128)(2,1)S(1)} %shard_map.56), kind=kOutput, calls=%fused_computation.4 | convolution fusion | flops 262144000 | bytes 6973440 | tf_op jit(solution)/shard_map/dot_general | solution.py:159
  33.4 1.3 %fusion.4.refs_1_ = f32[40,1024]{1,0:T(8,128)S(1)} fusion(bf16[40,3200]{1,0:T(8,128)(2,1)S(1)} %collective-permute-done.7, bf16[3200,1024]{1,0:T(8,128)(2,1)S(1)} %pad_maximum_fusion), kind=kOutput, calls=%fused_computation.7 | convolution fusion | flops 262144000 | bytes 6973440 | tf_op jit(solution)/shard_map/dot_general | solution.py:159
  34.6 1.3 %fusion.5.refs_0_.refs_2_ = f32[80,1024]{1,0:T(8,128)S(1)} fusion(bf16[80,3200]{1,0:T(8,128)(2,1)S(1)} %collective-permute-done.5, bf16[3200,1024]{1,0:T(8,128)(2,1)S(1)} %pad_maximum_fusion), kind=kOutput, calls=%fused_computation.8 | convolution fusion | flops 524288000 | bytes 7393280 | tf_op jit(solution)/shard_map/dot_general | solution.py:159
  35.9 4.5 %collective-permute-done.6 = bf16[80,3200]{1,0:T(8,128)(2,1)S(1)} collective-permute-done((bf16[80,3200]{1,0:T(8,128)(2,1)S(1)}, bf16[80,3200]{1,0:T(8,128)(2,1)S(1)}, u32[]{:S(2)}, u32[]{:S(2)}) %collective-permute-start.6) | collective-permute-done | bytes 512032 | tf_op jit(solution)/shard_map/ppermute | solution.py:24
  40.4 0.8 collective-permute-start.12
  41.2 1.3 %fusion.6.refs_1_.refs_3_ = f32[80,1024]{1,0:T(8,128)S(1)} fusion(bf16[80,3200]{1,0:T(8,128)(2,1)S(1)} %collective-permute-done.8, bf16[3200,1024]{1,0:T(8,128)(2,1)S(1)} %pad_maximum_fusion), kind=kOutput, calls=%fused_computation.9 | convolution fusion | flops 524288000 | bytes 7393280 | tf_op jit(solution)/shard_map/dot_general | solution.py:159
  42.5 5.8 %collective-permute-start.10 = (f32[80,1024]{1,0:T(8,128)S(1)}, f32[80,1024]{1,0:T(8,128)S(1)}, u32[]{:S(2)}, u32[]{:S(2)}) collective-permute-start(f32[80,1024]{1,0:T(8,128)S(1)} %shard_map.57), channel_id=1, source_target_pairs={{0,1},{1,0},{2,3},{3,2},{4,5},{5,4},{6,7},{7,6},{8,9},{9,8},{10,11... | collective-permute-start | bytes 983048 | tf_op jit(solution)/shard_map/ppermute | solution.py:38
  48.3 1.3 %fusion.7.refs_0_.refs_4_ = f32[80,1024]{1,0:T(8,128)S(1)} fusion(bf16[80,3200]{1,0:T(8,128)(2,1)S(1)} %collective-permute-done.6, bf16[3200,1024]{1,0:T(8,128)(2,1)S(1)} %pad_maximum_fusion), kind=kOutput, calls=%fused_computation.10 | convolution fusion | flops 524288000 | bytes 7393280 | tf_op jit(solution)/shard_map/dot_general | solution.py:159
  49.7 0.6 collective-permute-start.13
  50.3 1.3 %fusion.9.refs_0_.refs_6_ = f32[80,1024]{1,0:T(8,128)S(1)} fusion(bf16[80,3200]{1,0:T(8,128)(2,1)S(1)} %collective-permute-done.9, bf16[3200,1024]{1,0:T(8,128)(2,1)S(1)} %pad_maximum_fusion), kind=kOutput, calls=%fused_computation.12 | convolution fusion | flops 524288000 | bytes 7393280 | tf_op jit(solution)/shard_map/dot_general | solution.py:159
  51.6 0.1 collective-permute-start.11
  51.7 0.4 collective-permute-start.17
  52.1 1.3 %fusion.8.refs_1_.refs_5_ = f32[80,1024]{1,0:T(8,128)S(1)} fusion(bf16[80,3200]{1,0:T(8,128)(2,1)S(1)} %collective-permute-done.12, bf16[3200,1024]{1,0:T(8,128)(2,1)S(1)} %pad_maximum_fusion), kind=kOutput, calls=%fused_computation.11 | convolution fusion | flops 524288000 | bytes 7393280 | tf_op jit(solution)/shard_map/dot_general | solution.py:159
  53.4 4.6 %collective-permute-done.11 = bf16[40,3200]{1,0:T(8,128)(2,1)S(1)} collective-permute-done((bf16[40,3200]{1,0:T(8,128)(2,1)S(1)}, bf16[40,3200]{1,0:T(8,128)(2,1)S(1)}, u32[]{:S(2)}, u32[]{:S(2)}) %collective-permute-start.11) | collective-permute-done | bytes 256032 | tf_op jit(solution)/shard_map/ppermute | solution.py:24
  58.1 4.2 %collective-permute-start.15 = (f32[80,1024]{1,0:T(8,128)S(1)}, f32[80,1024]{1,0:T(8,128)S(1)}, u32[]{:S(2)}, u32[]{:S(2)}) collective-permute-start(f32[80,1024]{1,0:T(8,128)S(1)} %shard_map.59), channel_id=1, source_target_pairs={{0,1},{1,0},{2,3},{3,2},{4,5},{5,4},{6,7},{7,6},{8,9},{9,8},{10,11... | collective-permute-start | bytes 983048 | tf_op jit(solution)/shard_map/ppermute | solution.py:38
  62.3 0.1 collective-permute-start.14
  62.4 1.3 %fusion.10.refs_1_.refs_7_ = f32[80,1024]{1,0:T(8,128)S(1)} fusion(bf16[80,3200]{1,0:T(8,128)(2,1)S(1)} %collective-permute-done.13, bf16[3200,1024]{1,0:T(8,128)(2,1)S(1)} %pad_maximum_fusion), kind=kOutput, calls=%fused_computation.13 | convolution fusion | flops 524288000 | bytes 7393280 | tf_op jit(solution)/shard_map/dot_general | solution.py:159
  63.7 1.4 %collective-permute-start.16 = (f32[80,1024]{1,0:T(8,128)S(1)}, f32[80,1024]{1,0:T(8,128)S(1)}, u32[]{:S(2)}, u32[]{:S(2)}) collective-permute-start(f32[80,1024]{1,0:T(8,128)S(1)} %shard_map.60), channel_id=1, source_target_pairs={{0,1},{1,0},{2,3},{3,2},{4,5},{5,4},{6,7},{7,6},{8,9},{9,8},{10,11... | collective-permute-start | bytes 983048 | tf_op jit(solution)/shard_map/ppermute | solution.py:38
  65.2 1.2 %fusion.11.refs_0_.refs_8_ = f32[40,1024]{1,0:T(8,128)S(1)} fusion(bf16[40,3200]{1,0:T(8,128)(2,1)S(1)} %collective-permute-done.11, bf16[3200,1024]{1,0:T(8,128)(2,1)S(1)} %pad_maximum_fusion), kind=kOutput, calls=%fused_computation.14 | convolution fusion | flops 262144000 | bytes 6973440 | tf_op jit(solution)/shard_map/dot_general | solution.py:159
  66.5 0.4 collective-permute-start.18
  66.9 1.7 %collective-permute-done.14 = bf16[40,3200]{1,0:T(8,128)(2,1)S(1)} collective-permute-done((bf16[40,3200]{1,0:T(8,128)(2,1)S(1)}, bf16[40,3200]{1,0:T(8,128)(2,1)S(1)}, u32[]{:S(2)}, u32[]{:S(2)}) %collective-permute-start.14) | collective-permute-done | bytes 256032 | tf_op jit(solution)/shard_map/ppermute | solution.py:29
  68.7 1.3 %fusion.12.refs_1_.refs_9_ = f32[40,1024]{1,0:T(8,128)S(1)} fusion(bf16[40,3200]{1,0:T(8,128)(2,1)S(1)} %collective-permute-done.14, bf16[3200,1024]{1,0:T(8,128)(2,1)S(1)} %pad_maximum_fusion), kind=kOutput, calls=%fused_computation.15 | convolution fusion | flops 262144000 | bytes 6973440 | tf_op jit(solution)/shard_map/dot_general | solution.py:159
  70.0 0.4 collective-permute-start.20
  70.4 1.2 %collective-permute-start.19 = (f16[80,1024]{1,0:T(8,128)(2,1)S(1)}, f16[80,1024]{1,0:T(8,128)(2,1)S(1)}, u32[]{:S(2)}, u32[]{:S(2)}) collective-permute-start(f16[80,1024]{1,0:T(8,128)(2,1)S(1)} %convert_element_type.29), channel_id=1, source_target_pairs={{0,2},{2,0},{1,3},{3,1},{4,6},{6,4},{5,7},{7,5},{8,10},{10,8},{9,1... | collective-permute-start | bytes 491528 | tf_op jit(solution)/shard_map/ppermute | solution.py:42
  71.7 0.7 collective-permute-done.18
  72.5 1.8 %collective-permute-done.20 = f16[40,1024]{1,0:T(8,128)(2,1)S(1)} collective-permute-done((f16[40,1024]{1,0:T(8,128)(2,1)S(1)}, f16[40,1024]{1,0:T(8,128)(2,1)S(1)}, u32[]{:S(2)}, u32[]{:S(2)}) %collective-permute-start.20) | collective-permute-done | bytes 81952 | tf_op jit(solution)/shard_map/ppermute | solution.py:42
  74.2 3.5 %collective-permute-done.19 = f16[80,1024]{1,0:T(8,128)(2,1)S(1)} collective-permute-done((f16[80,1024]{1,0:T(8,128)(2,1)S(1)}, f16[80,1024]{1,0:T(8,128)(2,1)S(1)}, u32[]{:S(2)}, u32[]{:S(2)}) %collective-permute-start.19) | collective-permute-done | bytes 163872 | tf_op jit(solution)/shard_map/ppermute | solution.py:42
  77.8 1.9 %shard_map.64 = f32[320,1024]{1,0:T(8,128)} custom-call(s32[5]{0:T(128)S(1)} %stack.27.place_ref, f32[320,1024]{1,0:T(8,128)S(1)} %copy-done, f32[320,1]{1,0:T(8,128)S(1)} %compare_select_fusion.row_ref, f32[1,1024]{1,0:T(1,128)S(1)} %fusion.col_ref, f32[40,1024]{1,0:T(8,128)S(1)} %fusion.1.refs_0_, f32[40,1024]{1,0:T(8,128)S(1)} %fusion.4.refs_1_, ...), custom_call_target="tpu_custom_call" | custom-call | tf_op jit(solution)/shard_map/pallas_call | solution.py:125
  (36 shorter events, 0.5 us)
Async XLA Ops:
  0.0 15.5 %collective-permute-start.3 = (bf16[1600,1024]{1,0:T(8,128)(2,1)}, bf16[1600,1024]{1,0:T(8,128)(2,1)}, u32[]{:S(2)}, u32[]{:S(2)}) collective-permute-start(bf16[1600,1024]{1,0:T(8,128)(2,1)} %bitcast.27), channel_id=1, source_target_pairs={{0,1},{1,0},{2,3},{3,2},{4,5},{5,4},{6,7},{7,6},{8,9},{9,8},{10,11... | collective-permute-start | bytes 9830408 | tf_op jit(solution)/shard_map/ppermute | solution.py:38
  4.3 5.8 %collective-permute-start = (bf16[20,1600]{1,0:T(8,128)(2,1)S(1)}, bf16[20,1600]{1,0:T(8,128)(2,1)S(1)}, u32[]{:S(2)}, u32[]{:S(2)}) collective-permute-start(bf16[20,1600]{1,0:T(8,128)(2,1)S(1)} %reshape.30.s0), channel_id=1, source_target_pairs={{0,64},{32,96},{64,0},{96,32},{128,192},{160,224},{192,128},{224,1... | collective-permute-start | bytes 192008 | tf_op jit(solution)/shard_map/ppermute | solution.py:34
  5.6 5.2 %collective-permute-start.1 = (bf16[20,1600]{1,0:T(8,128)(2,1)S(1)}, bf16[20,1600]{1,0:T(8,128)(2,1)S(1)}, u32[]{:S(2)}, u32[]{:S(2)}) collective-permute-start(bf16[20,1600]{1,0:T(8,128)(2,1)S(1)} %reshape.30.s0), channel_id=1, source_target_pairs={{0,128},{32,160},{64,192},{96,224},{128,0},{160,32},{192,64},{224,... | collective-permute-start | bytes 192008 | tf_op jit(solution)/shard_map/ppermute | solution.py:34
  8.3 7.2 %collective-permute-start.2 = (bf16[20,1600]{1,0:T(8,128)(2,1)S(1)}, bf16[20,1600]{1,0:T(8,128)(2,1)S(1)}, u32[]{:S(2)}, u32[]{:S(2)}) collective-permute-start(bf16[20,1600]{1,0:T(8,128)(2,1)S(1)} %reshape.30.s0), channel_id=1, source_target_pairs={{0,192},{32,224},{64,128},{96,160},{128,64},{160,96},{192,0},{224,... | collective-permute-start | bytes 192008 | tf_op jit(solution)/shard_map/ppermute | solution.py:34
  16.1 3.0 %collective-permute-start.4 = (bf16[80,1600]{1,0:T(8,128)(2,1)S(1)}, bf16[80,1600]{1,0:T(8,128)(2,1)S(1)}, u32[]{:S(2)}, u32[]{:S(2)}) collective-permute-start(bf16[80,1600]{1,0:T(8,128)(2,1)S(1)} %shard_map.55.mine_ref), channel_id=1, source_target_pairs={{0,1},{1,0},{2,3},{3,2},{4,5},{5,4},{6,7},{7,6},{8,9},{9,8},{10,11... | collective-permute-start | bytes 768008 | tf_op jit(solution)/shard_map/ppermute | solution.py:38
  19.2 12.1 %collective-permute-start.5 = (bf16[80,3200]{1,0:T(8,128)(2,1)S(1)}, bf16[80,3200]{1,0:T(8,128)(2,1)S(1)}, u32[]{:S(2)}, u32[]{:S(2)}) collective-permute-start(bf16[80,3200]{1,0:T(8,128)(2,1)S(1)} %shard_map.56), channel_id=1, source_target_pairs={{0,28},{1,5},{4,0},{5,9},{8,4},{9,13},{12,8},{13,17},{16,12},{17,2... | collective-permute-start | bytes 1536008 | tf_op jit(solution)/shard_map/ppermute | solution.py:24
  24.6 8.7 %collective-permute-start.7 = (bf16[40,3200]{1,0:T(8,128)(2,1)S(1)}, bf16[40,3200]{1,0:T(8,128)(2,1)S(1)}, u32[]{:S(2)}, u32[]{:S(2)}) collective-permute-start(bf16[40,3200]{1,0:T(8,128)(2,1)S(1)} %slice.25), channel_id=1, source_target_pairs={{0,32},{1,97},{32,0},{33,65},{64,96},{65,33},{96,64},{97,1},{2,34}... | collective-permute-start | bytes 768008 | tf_op jit(solution)/shard_map/ppermute | solution.py:29
  31.3 9.1 %collective-permute-start.6 = (bf16[80,3200]{1,0:T(8,128)(2,1)S(1)}, bf16[80,3200]{1,0:T(8,128)(2,1)S(1)}, u32[]{:S(2)}, u32[]{:S(2)}) collective-permute-start(bf16[80,3200]{1,0:T(8,128)(2,1)S(1)} %collective-permute-done.5), channel_id=1, source_target_pairs={{0,28},{1,5},{4,0},{5,9},{8,4},{9,13},{12,8},{13,17},{16,12},{17,2... | collective-permute-start | bytes 1536008 | tf_op jit(solution)/shard_map/ppermute | solution.py:24
  31.3 9.9 %collective-permute-start.8 = (bf16[80,3200]{1,0:T(8,128)(2,1)S(1)}, bf16[80,3200]{1,0:T(8,128)(2,1)S(1)}, u32[]{:S(2)}, u32[]{:S(2)}) collective-permute-start(bf16[80,3200]{1,0:T(8,128)(2,1)S(1)} %collective-permute-done.5), channel_id=1, source_target_pairs={{0,32},{1,97},{32,0},{33,65},{64,96},{65,33},{96,64},{97,1},{2,34}... | collective-permute-start | bytes 1536008 | tf_op jit(solution)/shard_map/ppermute | solution.py:29
  40.4 9.2 %collective-permute-start.9 = (bf16[80,3200]{1,0:T(8,128)(2,1)S(1)}, bf16[80,3200]{1,0:T(8,128)(2,1)S(1)}, u32[]{:S(2)}, u32[]{:S(2)}) collective-permute-start(bf16[80,3200]{1,0:T(8,128)(2,1)S(1)} %collective-permute-done.6), channel_id=1, source_target_pairs={{0,28},{1,5},{4,0},{5,9},{8,4},{9,13},{12,8},{13,17},{16,12},{17,2... | collective-permute-start | bytes 1536008 | tf_op jit(solution)/shard_map/ppermute | solution.py:24
  40.4 11.7 %collective-permute-start.12 = (bf16[80,3200]{1,0:T(8,128)(2,1)S(1)}, bf16[80,3200]{1,0:T(8,128)(2,1)S(1)}, u32[]{:S(2)}, u32[]{:S(2)}) collective-permute-start(bf16[80,3200]{1,0:T(8,128)(2,1)S(1)} %collective-permute-done.6), channel_id=1, source_target_pairs={{0,32},{1,97},{32,0},{33,65},{64,96},{65,33},{96,64},{97,1},{2,34}... | collective-permute-start | bytes 1536008 | tf_op jit(solution)/shard_map/ppermute | solution.py:29
  42.5 7.1 %collective-permute-start.10 = (f32[80,1024]{1,0:T(8,128)S(1)}, f32[80,1024]{1,0:T(8,128)S(1)}, u32[]{:S(2)}, u32[]{:S(2)}) collective-permute-start(f32[80,1024]{1,0:T(8,128)S(1)} %shard_map.57), channel_id=1, source_target_pairs={{0,1},{1,0},{2,3},{3,2},{4,5},{5,4},{6,7},{7,6},{8,9},{9,8},{10,11... | collective-permute-start | bytes 983048 | tf_op jit(solution)/shard_map/ppermute | solution.py:38
  49.7 12.7 %collective-permute-start.13 = (bf16[80,3200]{1,0:T(8,128)(2,1)S(1)}, bf16[80,3200]{1,0:T(8,128)(2,1)S(1)}, u32[]{:S(2)}, u32[]{:S(2)}) collective-permute-start(bf16[80,3200]{1,0:T(8,128)(2,1)S(1)} %collective-permute-done.9), channel_id=1, source_target_pairs={{0,32},{1,97},{32,0},{33,65},{64,96},{65,33},{96,64},{97,1},{2,34}... | collective-permute-start | bytes 1536008 | tf_op jit(solution)/shard_map/ppermute | solution.py:29
  51.6 6.4 %collective-permute-start.11 = (bf16[40,3200]{1,0:T(8,128)(2,1)S(1)}, bf16[40,3200]{1,0:T(8,128)(2,1)S(1)}, u32[]{:S(2)}, u32[]{:S(2)}) collective-permute-start(bf16[40,3200]{1,0:T(8,128)(2,1)S(1)} %slice.24), channel_id=1, source_target_pairs={{0,28},{1,5},{4,0},{5,9},{8,4},{9,13},{12,8},{13,17},{16,12},{17,2... | collective-permute-start | bytes 768008 | tf_op jit(solution)/shard_map/ppermute | solution.py:24
  51.7 20.0 %collective-permute-start.17 = (f16[120,1024]{1,0:T(8,128)(2,1)S(1)}, f16[120,1024]{1,0:T(8,128)(2,1)S(1)}, u32[]{:S(2)}, u32[]{:S(2)}) collective-permute-start(f16[120,1024]{1,0:T(8,128)(2,1)S(1)} %convert_element_type.25), channel_id=1, source_target_pairs={{0,2},{2,0},{1,3},{3,1},{4,6},{6,4},{5,7},{7,5},{8,10},{10,8},{9,1... | collective-permute-start | bytes 737288 | tf_op jit(solution)/shard_map/ppermute | solution.py:42
  58.1 8.4 %collective-permute-start.15 = (f32[80,1024]{1,0:T(8,128)S(1)}, f32[80,1024]{1,0:T(8,128)S(1)}, u32[]{:S(2)}, u32[]{:S(2)}) collective-permute-start(f32[80,1024]{1,0:T(8,128)S(1)} %shard_map.59), channel_id=1, source_target_pairs={{0,1},{1,0},{2,3},{3,2},{4,5},{5,4},{6,7},{7,6},{8,9},{9,8},{10,11... | collective-permute-start | bytes 983048 | tf_op jit(solution)/shard_map/ppermute | solution.py:38
  62.3 6.4 %collective-permute-start.14 = (bf16[40,3200]{1,0:T(8,128)(2,1)S(1)}, bf16[40,3200]{1,0:T(8,128)(2,1)S(1)}, u32[]{:S(2)}, u32[]{:S(2)}) collective-permute-start(bf16[40,3200]{1,0:T(8,128)(2,1)S(1)} %collective-permute-done.11), channel_id=1, source_target_pairs={{0,32},{1,97},{32,0},{33,65},{64,96},{65,33},{96,64},{97,1},{2,34}... | collective-permute-start | bytes 768008 | tf_op jit(solution)/shard_map/ppermute | solution.py:29
  63.7 4.9 %collective-permute-start.16 = (f32[80,1024]{1,0:T(8,128)S(1)}, f32[80,1024]{1,0:T(8,128)S(1)}, u32[]{:S(2)}, u32[]{:S(2)}) collective-permute-start(f32[80,1024]{1,0:T(8,128)S(1)} %shard_map.60), channel_id=1, source_target_pairs={{0,1},{1,0},{2,3},{3,2},{4,5},{5,4},{6,7},{7,6},{8,9},{9,8},{10,11... | collective-permute-start | bytes 983048 | tf_op jit(solution)/shard_map/ppermute | solution.py:38
  66.4 5.3 %copy-start.1 = (s32[1024,2]{0,1:T(2,128)S(1)}, s32[1024,2]{0,1:T(2,128)}, u32[]{:S(2)}) copy-start(s32[1024,2]{0,1:T(2,128)} %param.9) | copy-start | bytes 24580
  66.5 11.3 %copy-start = (f32[320,1024]{1,0:T(8,128)S(1)}, f32[320,1024]{1,0:T(8,128)}, u32[]{:S(2)}) copy-start(f32[320,1024]{1,0:T(8,128)} %in_ref.1) | copy-start | bytes 3932164
  66.5 5.9 %collective-permute-start.18 = (f16[80,1024]{1,0:T(8,128)(2,1)S(1)}, f16[80,1024]{1,0:T(8,128)(2,1)S(1)}, u32[]{:S(2)}, u32[]{:S(2)}) collective-permute-start(f16[80,1024]{1,0:T(8,128)(2,1)S(1)} %convert_element_type.27), channel_id=1, source_target_pairs={{0,2},{2,0},{1,3},{3,1},{4,6},{6,4},{5,7},{7,5},{8,10},{10,8},{9,1... | collective-permute-start | bytes 491528 | tf_op jit(solution)/shard_map/ppermute | solution.py:42
  70.0 4.2 %collective-permute-start.20 = (f16[40,1024]{1,0:T(8,128)(2,1)S(1)}, f16[40,1024]{1,0:T(8,128)(2,1)S(1)}, u32[]{:S(2)}, u32[]{:S(2)}) collective-permute-start(f16[40,1024]{1,0:T(8,128)(2,1)S(1)} %convert_element_type.31), channel_id=1, source_target_pairs={{0,2},{2,0},{1,3},{3,1},{4,6},{6,4},{5,7},{7,5},{8,10},{10,8},{9,1... | collective-permute-start | bytes 245768 | tf_op jit(solution)/shard_map/ppermute | solution.py:42
  70.4 7.3 %collective-permute-start.19 = (f16[80,1024]{1,0:T(8,128)(2,1)S(1)}, f16[80,1024]{1,0:T(8,128)(2,1)S(1)}, u32[]{:S(2)}, u32[]{:S(2)}) collective-permute-start(f16[80,1024]{1,0:T(8,128)(2,1)S(1)} %convert_element_type.29), channel_id=1, source_target_pairs={{0,2},{2,0},{1,3},{3,1},{4,6},{6,4},{5,7},{7,5},{8,10},{10,8},{9,1... | collective-permute-start | bytes 491528 | tf_op jit(solution)/shard_map/ppermute | solution.py:42

commit v3 on v0

v3 whole, which is shorter than its diff:
```python
import jax
import jax.numpy as jnp
from jax import lax
from jax.experimental import pallas as pl
from jax.experimental.pallas import tpu as pltpu
from jax.sharding import Mesh
from jax.sharding import PartitionSpec as P

XH, Y, Z, XL = 2, 4, 8, 2
BLK = ("xh", "y", "z")
DS = ("xl", "core")
VMEM = pl.BlockSpec(memory_space=pltpu.VMEM)
F32, BF16, F16 = jnp.float32, jnp.bfloat16, jnp.float16
MIB = 1024 * 1024


def limit(size):
    return pltpu.CompilerParams(vmem_limit_bytes=size * MIB)


def turn(n, step):
    return [(i, (i + step) % n) for i in range(n)]


def up(x):
    return lax.ppermute(x, "z", turn(Z, -1))


def down(x):
    return lax.ppermute(x, "z", turn(Z, 1))


def either(x):
    route = [(2 * z + c, 2 * ((z + 2 * c - 1) % Z) + c) for z in range(Z) for c in range(2)]
    return lax.ppermute(x, ("z", "core"), route)


def swap(x):
    route = [(2 * y + c, 2 * (3 - y if c else y ^ 1) + c) for y in range(Y) for c in range(2)]
    return lax.ppermute(x, ("y", "core"), route)


def spread(x, flip):
    def at(x, y, c):
        return (x * Y + y) * 2 + c

    route = [(at(x, y, k), at(x ^ flip, y % 2 + 2 * k, y // 2)) for x in range(XH) for y in range(Y) for k in range(2)]
    return lax.ppermute(x, ("xh", "y", "core"), route)


def mate(x):
    return lax.ppermute(x, "core", turn(2, 1))


def trade(x):
    return lax.ppermute(x, "xl", turn(XL, 1))


def choose(first, pairs, axis, out_ref):
    for order, pair in enumerate((pairs, pairs[::-1])):

        @pl.when(first == order)
        def _(pair=pair):
            out_ref[...] = jnp.concatenate([r[...] for r in pair], axis=axis)


def local_call(kernel, shapes, *operands):
    return pl.pallas_call(
        kernel,
        out_shape=[jax.ShapeDtypeStruct(s, BF16) for s in shapes],
        in_specs=[VMEM] * len(operands),
        out_specs=[VMEM] * len(shapes),
        compiler_params=limit(8),
    )(*operands)


def join_kernel(mine_ref, mate_ref, out_ref):
    away = lax.axis_index("y") // 2 != lax.axis_index("core")
    choose(away.astype(jnp.int32), (mine_ref, mate_ref), 1, out_ref)


def pack_kernel(far_ref, near_ref, out_ref):
    away = lax.axis_index("xh") != lax.axis_index("xl")
    choose(away.astype(jnp.int32), (near_ref, far_ref), 0, out_ref)


def pair_kernel(up_ref, down_ref, out_ref, pick_ref):
    out_ref[...] = jnp.concatenate([up_ref[...], down_ref[...]], axis=0)
    for order, ref in enumerate((up_ref, down_ref)):

        @pl.when(lax.axis_index("core") == order)
        def _(ref=ref):
            pick_ref[...] = ref[...]


def stack(*parts):
    def kernel(*refs):
        refs[-1][...] = jnp.concatenate([r[...] for r in refs[:-1]], axis=0)

    return pl.pallas_call(
        kernel,
        out_shape=jax.ShapeDtypeStruct((sum(p.shape[0] for p in parts), parts[0].shape[1]), BF16),
        in_specs=[VMEM] * len(parts),
        out_specs=VMEM,
        compiler_params=limit(8),
    )(*parts)


def halves(*parts):
    depth = parts[0].shape[1] // 2

    def kernel(*refs):
        whole = jnp.concatenate([r[...] for r in refs[:-2]], axis=0)
        refs[-2][...] = whole[:, :depth]
        refs[-1][...] = whole[:, depth:]

    return local_call(kernel, [(sum(p.shape[0] for p in parts), depth)] * 2, *parts)


def low(*parts):
    def kernel(*refs):
        refs[-1][...] = jnp.concatenate([r[at:at + 20, :] for r, (_, at) in zip(refs, parts)], axis=0)

    rows = pl.pallas_call(
        kernel,
        out_shape=jax.ShapeDtypeStruct((20 * len(parts), parts[0][0].shape[1]), F32),
        in_specs=[VMEM] * len(parts),
        out_specs=VMEM,
        compiler_params=limit(8),
    )(*[p for p, _ in parts])
    return rows.astype(F16)


def last_kernel(in_ref, row_ref, col_ref, *refs):
    m0, m1, m2, m3, m4, b0, b2, b3, b4, out_ref, total, done, sems = refs
    here, z = lax.axis_index("y") % 2, lax.axis_index("z")
    there = 1 - here

    def put(half, shift, kept, at, back, start):
        value = kept[at:at + 20, :] + back[start:start + 20, :]
        total[half, lax.rem(z + shift + Z, Z)] = value

    put(here, 0, m0, 0, b0, 0)
    put(there, 0, m0, 40, b0, 20)
    for step, h, at, b, start, s, back in ((1, m0, 80, b0, 40, m1, (b0, 80)), (2, m1, 80, b2, 0, m2, (b2, 40)), (3, m2, 80, b2, 80, m3, (b3, 0))):
        put(here, step, h, at, b, start)
        put(here, -step, h, at + 40, b, start + 20)
        put(there, step, s, 0, back[0], back[1])
        put(there, -step, s, 40, back[0], back[1] + 20)
    put(here, 4, m3, 80, b3, 40)
    put(there, 4, m4, 0, b4, 0)
    copies = []
    for n in range(4):
        a, first = n // 2, 4 * (n % 2)
        rows = pl.ds(n * 80, 80)
        ladder = jnp.concatenate([total[a, i] for i in range(first, first + 4)], axis=0)
        done[rows, :] = in_ref[rows, :] + (row_ref[rows, :1] * scale(col_ref[...])) * ladder
        copies.append(pltpu.make_async_copy(done.at[rows], out_ref.at[rows], sems.at[n]))
        copies[-1].start()
    for copy in copies:
        copy.wait()


def finish(residual, row, col, parts):
    return pl.pallas_call(
        last_kernel,
        out_shape=jax.ShapeDtypeStruct(residual.shape, F32),
        in_specs=[VMEM] * (3 + len(parts)),
        out_specs=pl.BlockSpec(memory_space=pl.ANY),
        scratch_shapes=[
            pltpu.VMEM((2, Z, 20, residual.shape[1]), F32),
            pltpu.VMEM(residual.shape, F32),
            pltpu.SemaphoreType.DMA((4,)),
        ],
        compiler_params=limit(12),
    )(residual, row, col, *parts)


def fetch(x):
    def kernel(x_ref, out_ref, sem):
        copy = pltpu.make_async_copy(x_ref, out_ref, sem)
        copy.start()
        copy.wait()

    return pl.pallas_call(
        kernel,
        out_shape=jax.ShapeDtypeStruct(x.shape, x.dtype),
        in_specs=[pl.BlockSpec(memory_space=pl.ANY)],
        out_specs=VMEM,
        scratch_shapes=[pltpu.SemaphoreType.DMA],
        compiler_params=limit(1),
    )(x)


def scale(pairs):
    return jnp.where(pairs[0:1, :] == pairs[1:2, :], F32(0.5), F32(1.0))


def row_scale(pairs):
    count = pairs.shape[1]

    def kernel(pairs_ref, out_ref):
        out_ref[...] = jnp.broadcast_to(scale(pairs_ref[...]), (128, count)).T

    return pl.pallas_call(
        kernel,
        out_shape=jax.ShapeDtypeStruct((count, 128), F32),
        in_specs=[VMEM],
        out_specs=VMEM,
        compiler_params=limit(4),
    )(pairs)


def per_device(amplitudes, integrals, residual_in, pair_list, ab_list):
    tie = lax.optimization_barrier

    mine = amplitudes.reshape(amplitudes.shape[0], -1)
    own = integrals.reshape(-1, integrals.shape[2])
    pairs, depth = mine.shape
    block, double = (2 * pairs, 2 * depth), (4 * pairs, 2 * depth)

    mates, own = tie((mate(mine), own))
    (both,) = local_call(join_kernel, [(pairs, 2 * depth)], mine, mates)
    slots = spread(both, 1), spread(both, 0)
    other = mate(own)
    (held,) = local_call(pack_kernel, [block], *slots)

    def dot(*parts):
        left, right = halves(*parts)
        total = jnp.dot(left, own, preferred_element_type=F32)
        return total + jnp.dot(right, second, preferred_element_type=F32)

    above, below = up(held), down(held)
    swap0 = swap(held)
    above, below, second = tie((above, below, fetch(other)))
    old = above, below
    above, below = up(above), down(below)
    beside = stack(*old)
    swap1 = swap(beside)
    m0 = dot(held, swap0, beside)
    above, below, m0 = tie((above, below, m0))
    old = above, below
    above, below = up(above), down(below)
    beside = stack(*old)
    swap2 = swap(beside)
    m1 = dot(swap1, beside)
    goes0 = low((m0, 20), (m0, 60), (m0, 100), (m0, 140), (m1, 20), (m1, 60))
    above, below, m1, goes0 = tie((above, below, m1, goes0))
    beside, pick = local_call(pair_kernel, [double, block], above, below)
    opposite = either(pick)
    swap3 = swap(beside)
    b0 = trade(goes0)
    m2 = dot(swap2, beside)
    goes2 = low((m1, 100), (m1, 140), (m2, 20), (m2, 60), (m2, 100), (m2, 140))
    opposite, m2, goes2 = tie((opposite, m2, goes2))
    swap4 = swap(opposite)
    b2 = trade(goes2)
    m3 = dot(swap3, opposite)
    goes3 = low((m3, 20), (m3, 60), (m3, 100))
    swap4, m3, goes3 = tie((swap4, m3, goes3))
    b3 = trade(goes3)
    m4 = dot(swap4)
    goes4, pair_list, ab_list = tie((low((m4, 20)), pair_list.T, ab_list.T))
    b4 = trade(goes4)
    row = row_scale(pair_list)
    back = [b.astype(F32) for b in (b0, b2, b3, b4)]
    return finish(residual_in, row, ab_list, (m0, m1, m2, m3, m4, *back))


def solution(mesh):
    fine = Mesh(mesh.devices.reshape(XH, Y, Z, XL, 2), BLK + DS)
    placed = (P(BLK, None, DS), P(None, DS, BLK), P(DS, BLK), P(DS, None), P(BLK, None))
    return jax.shard_map(per_device, mesh=fine, in_specs=placed, out_specs=P(DS, BLK), check_vma=False)
```

time: 389 us -> 66.6 us (0.17)
  waiting for transfers between devices: 341 us -> 30.8 us
  starting transfers between devices: 0.04 us -> 23.2 us
  blocking collectives: 14.6 us -> 0 us
  between operations: 13.4 us -> 0.51 us
  local copies, waits for them, and re-layouts: 8.58 us -> 1.08 us
  matrix products: 11.7 us -> 7.36 us
    all_gather x2 -> x0, waiting for transfers between devices: 340 us -> none  [the longest x1 222 us: per_device(): every_amp = lax.all_gather(full_amps, 'blk', axis=0, tiled=True)]
    ppermute x0 -> x20, waiting for transfers between devices: none -> 30.8 us  [the longest x5 7.49 us: swap(): return lax.ppermute(x, ('y', 'core'), route)]
    ppermute x0 -> x20, starting transfers between devices: none -> 23.2 us  [the longest x3 7.59 us: up(): return lax.ppermute(x, 'z', turn(Z, -1))]
    all_gather x1 -> x0, blocking collectives: 14.6 us -> none  [per_device(): full_amps = lax.all_gather(amplitudes, 'dsplit', axis=2, tiled=True)]
    dynamic_slice x1 -> x0, local copies, waits for them, and re-layouts: 4.71 us -> none  [per_device(): mine = lax.dynamic_slice_in_dim(every_amp, first, rows, 0)]
    dot_general x1 -> x10, matrix products: 11.7 us -> 7.36 us  [the longest x5 3.74 us: dot(): total = jnp.dot(left, own, preferred_element_type=F32)]
  transfers between devices with their start and end apart: 2 -> 20, of which waited for: 2 -> 15; matrix products, arithmetic and copies ran while one was open for 1% -> 11% of each run, Pallas kernels for 0% -> 3%
where the time goes in v3:
time: 66.6 us; the launch traced here: 66.4 us
  waiting for transfers between devices  30.8 us (46%)
  starting transfers between devices  23.2 us (35%)
  matrix products  7.36 us (11%)
  Pallas kernels  3.29 us (5%)
  local copies, waits for them, and re-layouts  1.08 us (2%)
    ppermute x3, starting transfers between devices, up(): return lax.ppermute(x, 'z', turn(Z, -1))  7.59 us
    ppermute x5, waiting for transfers between devices, swap(): return lax.ppermute(x, ('y', 'core'), route)  7.49 us
    ppermute x3, waiting for transfers between devices, up(): return lax.ppermute(x, 'z', turn(Z, -1))  6.95 us
    ppermute x3, waiting for transfers between devices, down(): return lax.ppermute(x, 'z', turn(Z, 1))  6.92 us
    ppermute x2, starting transfers between devices, spread(): return lax.ppermute(x, ('xh', 'y', 'core'), route)  5.96 us
    ppermute x2, waiting for transfers between devices, spread(): return lax.ppermute(x, ('xh', 'y', 'core'), route)  5.82 us
    dot_general x5, matrix products, dot(): total = jnp.dot(left, own, preferred_element_type=F32)  3.74 us
    ppermute x2, starting transfers between devices, mate(): return lax.ppermute(x, 'core', turn(2, 1))  3.68 us
  transfers between devices with their start and end apart: 20, of which 15 were waited for; matrix products, arithmetic and copies ran while one was open for 11% of the time, Pallas kernels for 3%

profile of v3, /device:TPU:1, one launch (start us, length us, event | category | flops | bytes accessed | tf_op | source)
XLA Modules:
  0.0 66.4 jit_solution(7880970307074648536)
XLA Ops:
  0.0 1.1 %reshape.6.mine_ref = bf16[20,1600]{1,0:T(8,128)(2,1)S(1)} reshape(bf16[20,8,200]{2,1,0:T(8,128)(2,1)} %param.5) | data formatting | bytes 128000 | tf_op jit(solution)/shard_map/reshape | solution.py:217
  1.1 3.3 %collective-permute-start = (bf16[20,1600]{1,0:T(8,128)(2,1)S(1)}, bf16[20,1600]{1,0:T(8,128)(2,1)S(1)}, u32[]{:S(2)}, u32[]{:S(2)}) collective-permute-start(bf16[20,1600]{1,0:T(8,128)(2,1)S(1)} %reshape.6.mine_ref), channel_id=1, source_target_pairs={{0,1},{1,0},{2,3},{3,2},{4,5},{5,4},{6,7},{7,6},{8,9},{9,8},{10,11... | collective-permute-start | bytes 192008 | tf_op jit(solution)/shard_map/ppermute | solution.py:52
  4.4 0.9 %collective-permute-done.mate_ref = bf16[20,1600]{1,0:T(8,128)(2,1)S(1)} collective-permute-done((bf16[20,1600]{1,0:T(8,128)(2,1)S(1)}, bf16[20,1600]{1,0:T(8,128)(2,1)S(1)}, u32[]{:S(2)}, u32[]{:S(2)}) %collective-permute-start) | collective-permute-done | bytes 64032 | tf_op jit(solution)/shard_map/ppermute | solution.py:52
  5.3 0.4 collective-permute-start.5
  5.7 0.1 shard_map.55
  5.8 3.8 %collective-permute-start.1 = (bf16[20,3200]{1,0:T(8,128)(2,1)S(1)}, bf16[20,3200]{1,0:T(8,128)(2,1)S(1)}, u32[]{:S(2)}, u32[]{:S(2)}) collective-permute-start(bf16[20,3200]{1,0:T(8,128)(2,1)S(1)} %shard_map.55), channel_id=1, source_target_pairs={{0,128},{1,192},{32,160},{33,224},{64,129},{65,193},{96,161},{97,2... | collective-permute-start | bytes 384008 | tf_op jit(solution)/shard_map/ppermute | solution.py:48
  9.5 2.2 %collective-permute-start.2 = (bf16[20,3200]{1,0:T(8,128)(2,1)S(1)}, bf16[20,3200]{1,0:T(8,128)(2,1)S(1)}, u32[]{:S(2)}, u32[]{:S(2)}) collective-permute-start(bf16[20,3200]{1,0:T(8,128)(2,1)S(1)} %shard_map.55), channel_id=1, source_target_pairs={{0,0},{1,64},{32,32},{33,96},{64,1},{65,65},{96,33},{97,97},{128,1... | collective-permute-start | bytes 384008 | tf_op jit(solution)/shard_map/ppermute | solution.py:48
  11.7 2.7 %collective-permute-done.1.far_ref = bf16[20,3200]{1,0:T(8,128)(2,1)S(1)} collective-permute-done((bf16[20,3200]{1,0:T(8,128)(2,1)S(1)}, bf16[20,3200]{1,0:T(8,128)(2,1)S(1)}, u32[]{:S(2)}, u32[]{:S(2)}) %collective-permute-start.1) | collective-permute-done | bytes 128032 | tf_op jit(solution)/shard_map/ppermute | solution.py:48
  14.4 3.2 %collective-permute-done.2.near_ref = bf16[20,3200]{1,0:T(8,128)(2,1)S(1)} collective-permute-done((bf16[20,3200]{1,0:T(8,128)(2,1)S(1)}, bf16[20,3200]{1,0:T(8,128)(2,1)S(1)}, u32[]{:S(2)}, u32[]{:S(2)}) %collective-permute-start.2) | collective-permute-done | bytes 128032 | tf_op jit(solution)/shard_map/ppermute | solution.py:48
  17.6 5.7 %collective-permute-start.3 = (bf16[40,3200]{1,0:T(8,128)(2,1)S(1)}, bf16[40,3200]{1,0:T(8,128)(2,1)S(1)}, u32[]{:S(2)}, u32[]{:S(2)}) collective-permute-start(bf16[40,3200]{1,0:T(8,128)(2,1)S(1)} %shard_map.56.refs_0_), channel_id=1, source_target_pairs={{0,28},{4,0},{8,4},{12,8},{16,12},{20,16},{24,20},{28,24},{1,29},{... | collective-permute-start | bytes 768008 | tf_op jit(solution)/shard_map/ppermute | solution.py:26
  23.3 0.4 shard_map.57
  23.7 4.1 %collective-permute-done.3.refs_0_ = bf16[40,3200]{1,0:T(8,128)(2,1)S(1)} collective-permute-done((bf16[40,3200]{1,0:T(8,128)(2,1)S(1)}, bf16[40,3200]{1,0:T(8,128)(2,1)S(1)}, u32[]{:S(2)}, u32[]{:S(2)}) %collective-permute-start.3) | collective-permute-done | bytes 256032 | tf_op jit(solution)/shard_map/ppermute | solution.py:26
  27.8 3.0 %collective-permute-done.4.refs_1_ = bf16[40,3200]{1,0:T(8,128)(2,1)S(1)} collective-permute-done((bf16[40,3200]{1,0:T(8,128)(2,1)S(1)}, bf16[40,3200]{1,0:T(8,128)(2,1)S(1)}, u32[]{:S(2)}, u32[]{:S(2)}) %collective-permute-start.4) | collective-permute-done | bytes 256032 | tf_op jit(solution)/shard_map/ppermute | solution.py:30
  30.8 0.4 collective-permute-start.6
  31.2 1.1 %collective-permute-start.7 = (bf16[40,3200]{1,0:T(8,128)(2,1)S(1)}, bf16[40,3200]{1,0:T(8,128)(2,1)S(1)}, u32[]{:S(2)}, u32[]{:S(2)}) collective-permute-start(bf16[40,3200]{1,0:T(8,128)(2,1)S(1)} %collective-permute-done.4.refs_1_), channel_id=1, source_target_pairs={{0,4},{4,8},{8,12},{12,16},{16,20},{20,24},{24,28},{28,0},{1,5},{5... | collective-permute-start | bytes 768008 | tf_op jit(solution)/shard_map/ppermute | solution.py:30
  32.4 0.2 shard_map.59
  32.6 0.8 %fusion = f32[160,1024]{1,0:T(8,128)S(1)} fusion(bf16[160,1600]{1,0:T(8,128)(2,1)S(1)} %get-tuple-element.43, bf16[1600,1024]{1,0:T(8,128)(2,1)S(1)} %shard_map.57), kind=kOutput, calls=%fused_computation.5 | convolution fusion | flops 524288000 | bytes 4444160 | tf_op jit(solution)/shard_map/dot_general | solution.py:231
  33.4 0.8 %convolution_add_fusion.2.refs_0_.refs_1_.refs_2_.refs_3_ = f32[160,1024]{1,0:T(8,128)S(1)} fusion(f32[160,1024]{1,0:T(8,128)S(1)} %fusion, bf16[160,1600]{1,0:T(8,128)(2,1)S(1)} %get-tuple-element.42, bf16[1600,1024]{1,0:T(8,128)(2,1)S(1)} %bitcast.26), kind=kOutput, calls=%fused_computation.2 | convolution fusion | flops 524451840 | bytes 5099520 | tf_op jit(solution)/shard_map/dot_general | solution.py:230
  34.3 1.7 %collective-permute-done.6.refs_0_ = bf16[40,3200]{1,0:T(8,128)(2,1)S(1)} collective-permute-done((bf16[40,3200]{1,0:T(8,128)(2,1)S(1)}, bf16[40,3200]{1,0:T(8,128)(2,1)S(1)}, u32[]{:S(2)}, u32[]{:S(2)}) %collective-permute-start.6) | collective-permute-done | bytes 256032 | tf_op jit(solution)/shard_map/ppermute | solution.py:26
  35.9 2.5 %collective-permute-done.7.refs_1_ = bf16[40,3200]{1,0:T(8,128)(2,1)S(1)} collective-permute-done((bf16[40,3200]{1,0:T(8,128)(2,1)S(1)}, bf16[40,3200]{1,0:T(8,128)(2,1)S(1)}, u32[]{:S(2)}, u32[]{:S(2)}) %collective-permute-start.7) | collective-permute-done | bytes 256032 | tf_op jit(solution)/shard_map/ppermute | solution.py:30
  38.4 1.2 %collective-permute-start.10 = (bf16[40,3200]{1,0:T(8,128)(2,1)S(1)}, bf16[40,3200]{1,0:T(8,128)(2,1)S(1)}, u32[]{:S(2)}, u32[]{:S(2)}) collective-permute-start(bf16[40,3200]{1,0:T(8,128)(2,1)S(1)} %collective-permute-done.7.refs_1_), channel_id=1, source_target_pairs={{0,4},{4,8},{8,12},{12,16},{16,20},{20,24},{24,28},{28,0},{1,5},{5... | collective-permute-start | bytes 768008 | tf_op jit(solution)/shard_map/ppermute | solution.py:30
  39.7 1.5 %collective-permute-start.9 = (bf16[40,3200]{1,0:T(8,128)(2,1)S(1)}, bf16[40,3200]{1,0:T(8,128)(2,1)S(1)}, u32[]{:S(2)}, u32[]{:S(2)}) collective-permute-start(bf16[40,3200]{1,0:T(8,128)(2,1)S(1)} %collective-permute-done.6.refs_0_), channel_id=1, source_target_pairs={{0,28},{4,0},{8,4},{12,8},{16,12},{20,16},{24,20},{28,24},{1,29},{... | collective-permute-start | bytes 768008 | tf_op jit(solution)/shard_map/ppermute | solution.py:26
  41.2 0.2 collective-permute-done.11.refs_0_
  41.5 0.2 shard_map.61
  41.7 0.8 %fusion.1 = f32[160,1024]{1,0:T(8,128)S(1)} fusion(bf16[160,1600]{1,0:T(8,128)(2,1)S(1)} %get-tuple-element.48, bf16[1600,1024]{1,0:T(8,128)(2,1)S(1)} %shard_map.57), kind=kOutput, calls=%fused_computation.6 | convolution fusion | flops 524288000 | bytes 4444160 | tf_op jit(solution)/shard_map/dot_general | solution.py:231
  42.5 0.8 %convolution_add_fusion.1.refs_4_.refs_5_.refs_0_.refs_1_ = f32[160,1024]{1,0:T(8,128)S(1)} fusion(f32[160,1024]{1,0:T(8,128)S(1)} %fusion.1, bf16[160,1600]{1,0:T(8,128)(2,1)S(1)} %get-tuple-element.47, bf16[1600,1024]{1,0:T(8,128)(2,1)S(1)} %bitcast.27), kind=kOutput, calls=%fused_computation.1 | convolution fusion | flops 524451840 | bytes 5099520 | tf_op jit(solution)/shard_map/dot_general | solution.py:230
  43.4 1.4 %collective-permute-done.10.down_ref = bf16[40,3200]{1,0:T(8,128)(2,1)S(1)} collective-permute-done((bf16[40,3200]{1,0:T(8,128)(2,1)S(1)}, bf16[40,3200]{1,0:T(8,128)(2,1)S(1)}, u32[]{:S(2)}, u32[]{:S(2)}) %collective-permute-start.10) | collective-permute-done | bytes 256032 | tf_op jit(solution)/shard_map/ppermute | solution.py:30
  44.8 1.2 %collective-permute-done.9.up_ref = bf16[40,3200]{1,0:T(8,128)(2,1)S(1)} collective-permute-done((bf16[40,3200]{1,0:T(8,128)(2,1)S(1)}, bf16[40,3200]{1,0:T(8,128)(2,1)S(1)}, u32[]{:S(2)}, u32[]{:S(2)}) %collective-permute-start.9) | collective-permute-done | bytes 256032 | tf_op jit(solution)/shard_map/ppermute | solution.py:26
  46.1 1.2 %collective-permute-start.12 = (bf16[40,3200]{1,0:T(8,128)(2,1)S(1)}, bf16[40,3200]{1,0:T(8,128)(2,1)S(1)}, u32[]{:S(2)}, u32[]{:S(2)}) collective-permute-start(bf16[40,3200]{1,0:T(8,128)(2,1)S(1)} %get-tuple-element.52), channel_id=1, source_target_pairs={{0,28},{1,5},{4,0},{5,9},{8,4},{9,13},{12,8},{13,17},{16,12},{17,2... | collective-permute-start | bytes 768008 | tf_op jit(solution)/shard_map/ppermute | solution.py:35
  47.2 3.1 %collective-permute-done.13.refs_0_ = bf16[80,3200]{1,0:T(8,128)(2,1)S(1)} collective-permute-done((bf16[80,3200]{1,0:T(8,128)(2,1)S(1)}, bf16[80,3200]{1,0:T(8,128)(2,1)S(1)}, u32[]{:S(2)}, u32[]{:S(2)}) %collective-permute-start.13) | collective-permute-done | bytes 512032 | tf_op jit(solution)/shard_map/ppermute | solution.py:40
  50.3 0.2 shard_map.64
  50.6 0.8 %fusion.2 = f32[160,1024]{1,0:T(8,128)S(1)} fusion(bf16[160,1600]{1,0:T(8,128)(2,1)S(1)} %get-tuple-element.55, bf16[1600,1024]{1,0:T(8,128)(2,1)S(1)} %shard_map.57), kind=kOutput, calls=%fused_computation.7 | convolution fusion | flops 524288000 | bytes 4444160 | tf_op jit(solution)/shard_map/dot_general | solution.py:231
  51.4 0.8 %convolution_add_fusion.refs_2_.refs_3_.refs_4_.refs_5_ = f32[160,1024]{1,0:T(8,128)S(1)} fusion(f32[160,1024]{1,0:T(8,128)S(1)} %fusion.2, bf16[160,1600]{1,0:T(8,128)(2,1)S(1)} %get-tuple-element.54, bf16[1600,1024]{1,0:T(8,128)(2,1)S(1)} %bitcast.28), kind=kOutput, calls=%fused_computation | convolution fusion | flops 524451840 | bytes 5099520 | tf_op jit(solution)/shard_map/dot_general | solution.py:230
  52.2 0.3 collective-permute-done.12.refs_1_
  52.5 0.8 %collective-permute-start.17 = (f16[120,1024]{1,0:T(8,128)(2,1)S(1)}, f16[120,1024]{1,0:T(8,128)(2,1)S(1)}, u32[]{:S(2)}, u32[]{:S(2)}) collective-permute-start(f16[120,1024]{1,0:T(8,128)(2,1)S(1)} %convert_element_type.25), channel_id=1, source_target_pairs={{0,2},{2,0},{1,3},{3,1},{4,6},{6,4},{5,7},{7,5},{8,10},{10,8},{9,1... | collective-permute-start | bytes 737288 | tf_op jit(solution)/shard_map/ppermute | solution.py:56
  53.4 3.0 %collective-permute-done.15.refs_0_ = bf16[80,3200]{1,0:T(8,128)(2,1)S(1)} collective-permute-done((bf16[80,3200]{1,0:T(8,128)(2,1)S(1)}, bf16[80,3200]{1,0:T(8,128)(2,1)S(1)}, u32[]{:S(2)}, u32[]{:S(2)}) %collective-permute-start.15) | collective-permute-done | bytes 512032 | tf_op jit(solution)/shard_map/ppermute | solution.py:40
  56.3 0.2 shard_map.66
  56.5 0.6 fusion.3
  57.2 0.7 convolution_add_fusion.3.refs_0_.refs_1_.refs_2_.refs_3_
  57.9 1.2 %collective-permute-done.14.refs_0_ = bf16[40,3200]{1,0:T(8,128)(2,1)S(1)} collective-permute-done((bf16[40,3200]{1,0:T(8,128)(2,1)S(1)}, bf16[40,3200]{1,0:T(8,128)(2,1)S(1)}, u32[]{:S(2)}, u32[]{:S(2)}) %collective-permute-start.14) | collective-permute-done | bytes 256032 | tf_op jit(solution)/shard_map/ppermute | solution.py:40
  59.1 0.1 shard_map.68
  59.2 0.7 %fusion.4 = f32[40,1024]{1,0:T(8,128)S(1)} fusion(bf16[40,1600]{1,0:T(8,128)(2,1)S(1)} %get-tuple-element.62, bf16[1600,1024]{1,0:T(8,128)(2,1)S(1)} %shard_map.57), kind=kOutput, calls=%fused_computation.9 | convolution fusion | flops 131072000 | bytes 3568640 | tf_op jit(solution)/shard_map/dot_general | solution.py:231
  59.9 0.1 collective-permute-start.18
  60.0 0.7 %convolution_add_fusion.4.refs_0_.refs_4_ = f32[40,1024]{1,0:T(8,128)S(1)} fusion(f32[40,1024]{1,0:T(8,128)S(1)} %fusion.4, bf16[40,1600]{1,0:T(8,128)(2,1)S(1)} %get-tuple-element.61, bf16[1600,1024]{1,0:T(8,128)(2,1)S(1)} %bitcast.30), kind=kOutput, calls=%fused_computation.4 | convolution fusion | flops 131112960 | bytes 3732480 | tf_op jit(solution)/shard_map/dot_general | solution.py:230
  60.7 1.5 %collective-permute-start.19 = (f16[20,1024]{1,0:T(8,128)(2,1)S(1)}, f16[20,1024]{1,0:T(8,128)(2,1)S(1)}, u32[]{:S(2)}, u32[]{:S(2)}) collective-permute-start(f16[20,1024]{1,0:T(8,128)(2,1)S(1)} %convert_element_type.27), channel_id=1, source_target_pairs={{0,2},{2,0},{1,3},{3,1},{4,6},{6,4},{5,7},{7,5},{8,10},{10,8},{9,1... | collective-permute-start | bytes 122888 | tf_op jit(solution)/shard_map/ppermute | solution.py:56
  62.4 0.1 shard_map.70.row_ref
  62.5 2.4 %collective-permute-done.19 = f16[20,1024]{1,0:T(8,128)(2,1)S(1)} collective-permute-done((f16[20,1024]{1,0:T(8,128)(2,1)S(1)}, f16[20,1024]{1,0:T(8,128)(2,1)S(1)}, u32[]{:S(2)}, u32[]{:S(2)}) %collective-permute-start.19) | collective-permute-done | bytes 40992 | tf_op jit(solution)/shard_map/ppermute | solution.py:56
  64.9 1.3 %shard_map.71 = f32[320,1024]{1,0:T(8,128)} custom-call(f32[320,1024]{1,0:T(8,128)S(1)} %copy-done, f32[320,128]{1,0:T(8,128)S(1)} %shard_map.70.row_ref, s32[2,1024]{1,0:T(2,128)S(1)} %bitcast.23, f32[160,1024]{1,0:T(8,128)S(1)} %convolution_add_fusion.2.refs_0_.refs_1_.refs_2_.refs_3_, ...), custom_call_target="tpu_custom_call" | custom-call | tf_op jit(solution)/shard_map/pallas_call | solution.py:165
  (36 shorter events, 0.6 us)
Async XLA Ops:
  1.1 4.2 %collective-permute-start = (bf16[20,1600]{1,0:T(8,128)(2,1)S(1)}, bf16[20,1600]{1,0:T(8,128)(2,1)S(1)}, u32[]{:S(2)}, u32[]{:S(2)}) collective-permute-start(bf16[20,1600]{1,0:T(8,128)(2,1)S(1)} %reshape.6.mine_ref), channel_id=1, source_target_pairs={{0,1},{1,0},{2,3},{3,2},{4,5},{5,4},{6,7},{7,6},{8,9},{9,8},{10,11... | collective-permute-start | bytes 192008 | tf_op jit(solution)/shard_map/ppermute | solution.py:52
  5.3 18.0 %collective-permute-start.5 = (bf16[1600,1024]{1,0:T(8,128)(2,1)}, bf16[1600,1024]{1,0:T(8,128)(2,1)S(1)}, u32[]{:S(2)}, u32[]{:S(2)}) collective-permute-start(bf16[1600,1024]{1,0:T(8,128)(2,1)} %bitcast.25), channel_id=1, source_target_pairs={{0,1},{1,0},{2,3},{3,2},{4,5},{5,4},{6,7},{7,6},{8,9},{9,8},{10,11... | collective-permute-start | bytes 9830408 | tf_op jit(solution)/shard_map/ppermute | solution.py:52
  5.8 8.6 %collective-permute-start.1 = (bf16[20,3200]{1,0:T(8,128)(2,1)S(1)}, bf16[20,3200]{1,0:T(8,128)(2,1)S(1)}, u32[]{:S(2)}, u32[]{:S(2)}) collective-permute-start(bf16[20,3200]{1,0:T(8,128)(2,1)S(1)} %shard_map.55), channel_id=1, source_target_pairs={{0,128},{1,192},{32,160},{33,224},{64,129},{65,193},{96,161},{97,2... | collective-permute-start | bytes 384008 | tf_op jit(solution)/shard_map/ppermute | solution.py:48
  9.5 8.0 %collective-permute-start.2 = (bf16[20,3200]{1,0:T(8,128)(2,1)S(1)}, bf16[20,3200]{1,0:T(8,128)(2,1)S(1)}, u32[]{:S(2)}, u32[]{:S(2)}) collective-permute-start(bf16[20,3200]{1,0:T(8,128)(2,1)S(1)} %shard_map.55), channel_id=1, source_target_pairs={{0,0},{1,64},{32,32},{33,96},{64,1},{65,65},{96,33},{97,97},{128,1... | collective-permute-start | bytes 384008 | tf_op jit(solution)/shard_map/ppermute | solution.py:48
  17.6 10.2 %collective-permute-start.3 = (bf16[40,3200]{1,0:T(8,128)(2,1)S(1)}, bf16[40,3200]{1,0:T(8,128)(2,1)S(1)}, u32[]{:S(2)}, u32[]{:S(2)}) collective-permute-start(bf16[40,3200]{1,0:T(8,128)(2,1)S(1)} %shard_map.56.refs_0_), channel_id=1, source_target_pairs={{0,28},{4,0},{8,4},{12,8},{16,12},{20,16},{24,20},{28,24},{1,29},{... | collective-permute-start | bytes 768008 | tf_op jit(solution)/shard_map/ppermute | solution.py:26
  23.2 7.5 %collective-permute-start.4 = (bf16[40,3200]{1,0:T(8,128)(2,1)S(1)}, bf16[40,3200]{1,0:T(8,128)(2,1)S(1)}, u32[]{:S(2)}, u32[]{:S(2)}) collective-permute-start(bf16[40,3200]{1,0:T(8,128)(2,1)S(1)} %shard_map.56.refs_0_), channel_id=1, source_target_pairs={{0,4},{4,8},{8,12},{12,16},{16,20},{20,24},{24,28},{28,0},{1,5},{5... | collective-permute-start | bytes 768008 | tf_op jit(solution)/shard_map/ppermute | solution.py:30
  23.3 9.1 %collective-permute-start.8 = (bf16[40,3200]{1,0:T(8,128)(2,1)S(1)}, bf16[40,3200]{1,0:T(8,128)(2,1)S(1)}, u32[]{:S(2)}, u32[]{:S(2)}) collective-permute-start(bf16[40,3200]{1,0:T(8,128)(2,1)S(1)} %shard_map.56.refs_0_), channel_id=1, source_target_pairs={{0,32},{1,97},{32,0},{33,65},{64,96},{65,33},{96,64},{97,1},{2,34}... | collective-permute-start | bytes 768008 | tf_op jit(solution)/shard_map/ppermute | solution.py:40
  23.7 9.8 %copy-start.3 = (bf16[8,200,1024]{2,1,0:T(8,128)(2,1)S(1)}, bf16[8,200,1024]{2,1,0:T(8,128)(2,1)}, u32[]{:S(2)}) copy-start(bf16[8,200,1024]{2,1,0:T(8,128)(2,1)} %param.6) | copy-start | bytes 9830404
  30.8 5.2 %collective-permute-start.6 = (bf16[40,3200]{1,0:T(8,128)(2,1)S(1)}, bf16[40,3200]{1,0:T(8,128)(2,1)S(1)}, u32[]{:S(2)}, u32[]{:S(2)}) collective-permute-start(bf16[40,3200]{1,0:T(8,128)(2,1)S(1)} %collective-permute-done.3.refs_0_), channel_id=1, source_target_pairs={{0,28},{4,0},{8,4},{12,8},{16,12},{20,16},{24,20},{28,24},{1,29},{... | collective-permute-start | bytes 768008 | tf_op jit(solution)/shard_map/ppermute | solution.py:26
  31.2 7.2 %collective-permute-start.7 = (bf16[40,3200]{1,0:T(8,128)(2,1)S(1)}, bf16[40,3200]{1,0:T(8,128)(2,1)S(1)}, u32[]{:S(2)}, u32[]{:S(2)}) collective-permute-start(bf16[40,3200]{1,0:T(8,128)(2,1)S(1)} %collective-permute-done.4.refs_1_), channel_id=1, source_target_pairs={{0,4},{4,8},{8,12},{12,16},{16,20},{20,24},{24,28},{28,0},{1,5},{5... | collective-permute-start | bytes 768008 | tf_op jit(solution)/shard_map/ppermute | solution.py:30
  32.3 9.1 %collective-permute-start.11 = (bf16[80,3200]{1,0:T(8,128)(2,1)S(1)}, bf16[80,3200]{1,0:T(8,128)(2,1)S(1)}, u32[]{:S(2)}, u32[]{:S(2)}) collective-permute-start(bf16[80,3200]{1,0:T(8,128)(2,1)S(1)} %shard_map.58.refs_2_), channel_id=1, source_target_pairs={{0,32},{1,97},{32,0},{33,65},{64,96},{65,33},{96,64},{97,1},{2,34}... | collective-permute-start | bytes 1536008 | tf_op jit(solution)/shard_map/ppermute | solution.py:40
  38.4 6.4 %collective-permute-start.10 = (bf16[40,3200]{1,0:T(8,128)(2,1)S(1)}, bf16[40,3200]{1,0:T(8,128)(2,1)S(1)}, u32[]{:S(2)}, u32[]{:S(2)}) collective-permute-start(bf16[40,3200]{1,0:T(8,128)(2,1)S(1)} %collective-permute-done.7.refs_1_), channel_id=1, source_target_pairs={{0,4},{4,8},{8,12},{12,16},{16,20},{20,24},{24,28},{28,0},{1,5},{5... | collective-permute-start | bytes 768008 | tf_op jit(solution)/shard_map/ppermute | solution.py:30
  39.7 6.3 %collective-permute-start.9 = (bf16[40,3200]{1,0:T(8,128)(2,1)S(1)}, bf16[40,3200]{1,0:T(8,128)(2,1)S(1)}, u32[]{:S(2)}, u32[]{:S(2)}) collective-permute-start(bf16[40,3200]{1,0:T(8,128)(2,1)S(1)} %collective-permute-done.6.refs_0_), channel_id=1, source_target_pairs={{0,28},{4,0},{8,4},{12,8},{16,12},{20,16},{24,20},{28,24},{1,29},{... | collective-permute-start | bytes 768008 | tf_op jit(solution)/shard_map/ppermute | solution.py:26
  41.2 9.1 %collective-permute-start.13 = (bf16[80,3200]{1,0:T(8,128)(2,1)S(1)}, bf16[80,3200]{1,0:T(8,128)(2,1)S(1)}, u32[]{:S(2)}, u32[]{:S(2)}) collective-permute-start(bf16[80,3200]{1,0:T(8,128)(2,1)S(1)} %shard_map.60.refs_1_), channel_id=1, source_target_pairs={{0,32},{1,97},{32,0},{33,65},{64,96},{65,33},{96,64},{97,1},{2,34}... | collective-permute-start | bytes 1536008 | tf_op jit(solution)/shard_map/ppermute | solution.py:40
  46.1 6.4 %collective-permute-start.12 = (bf16[40,3200]{1,0:T(8,128)(2,1)S(1)}, bf16[40,3200]{1,0:T(8,128)(2,1)S(1)}, u32[]{:S(2)}, u32[]{:S(2)}) collective-permute-start(bf16[40,3200]{1,0:T(8,128)(2,1)S(1)} %get-tuple-element.52), channel_id=1, source_target_pairs={{0,28},{1,5},{4,0},{5,9},{8,4},{9,13},{12,8},{13,17},{16,12},{17,2... | collective-permute-start | bytes 768008 | tf_op jit(solution)/shard_map/ppermute | solution.py:35
  47.2 9.1 %collective-permute-start.15 = (bf16[80,3200]{1,0:T(8,128)(2,1)S(1)}, bf16[80,3200]{1,0:T(8,128)(2,1)S(1)}, u32[]{:S(2)}, u32[]{:S(2)}) collective-permute-start(bf16[80,3200]{1,0:T(8,128)(2,1)S(1)} %get-tuple-element.53.refs_1_), channel_id=1, source_target_pairs={{0,32},{1,97},{32,0},{33,65},{64,96},{65,33},{96,64},{97,1},{2,34}... | collective-permute-start | bytes 1536008 | tf_op jit(solution)/shard_map/ppermute | solution.py:40
  47.2 15.0 %collective-permute-start.16 = (f16[120,1024]{1,0:T(8,128)(2,1)S(1)}, f16[120,1024]{1,0:T(8,128)(2,1)S(1)}, u32[]{:S(2)}, u32[]{:S(2)}) collective-permute-start(f16[120,1024]{1,0:T(8,128)(2,1)S(1)} %convert_element_type.24), channel_id=1, source_target_pairs={{0,2},{2,0},{1,3},{3,1},{4,6},{6,4},{5,7},{7,5},{8,10},{10,8},{9,1... | collective-permute-start | bytes 737288 | tf_op jit(solution)/shard_map/ppermute | solution.py:56
  52.5 6.6 %collective-permute-start.14 = (bf16[40,3200]{1,0:T(8,128)(2,1)S(1)}, bf16[40,3200]{1,0:T(8,128)(2,1)S(1)}, u32[]{:S(2)}, u32[]{:S(2)}) collective-permute-start(bf16[40,3200]{1,0:T(8,128)(2,1)S(1)} %collective-permute-done.12.refs_1_), channel_id=1, source_target_pairs={{0,32},{1,97},{32,0},{33,65},{64,96},{65,33},{96,64},{97,1},{2,34}... | collective-permute-start | bytes 768008 | tf_op jit(solution)/shard_map/ppermute | solution.py:40
  52.5 9.8 %collective-permute-start.17 = (f16[120,1024]{1,0:T(8,128)(2,1)S(1)}, f16[120,1024]{1,0:T(8,128)(2,1)S(1)}, u32[]{:S(2)}, u32[]{:S(2)}) collective-permute-start(f16[120,1024]{1,0:T(8,128)(2,1)S(1)} %convert_element_type.25), channel_id=1, source_target_pairs={{0,2},{2,0},{1,3},{3,1},{4,6},{6,4},{5,7},{7,5},{8,10},{10,8},{9,1... | collective-permute-start | bytes 737288 | tf_op jit(solution)/shard_map/ppermute | solution.py:56
  59.9 2.5 %copy-start.2 = (s32[320,2]{0,1:T(2,128)S(1)}, s32[320,2]{0,1:T(2,128)}, u32[]{:S(2)}) copy-start(s32[320,2]{0,1:T(2,128)} %param.8) | copy-start | bytes 7684
  59.9 5.0 %copy-start = (f32[320,1024]{1,0:T(8,128)S(1)}, f32[320,1024]{1,0:T(8,128)}, u32[]{:S(2)}) copy-start(f32[320,1024]{1,0:T(8,128)} %in_ref.1) | copy-start | bytes 3932164
  59.9 5.0 %copy-start.1 = (s32[1024,2]{0,1:T(2,128)S(1)}, s32[1024,2]{0,1:T(2,128)}, u32[]{:S(2)}) copy-start(s32[1024,2]{0,1:T(2,128)} %param.9) | copy-start | bytes 24580
  59.9 5.0 %collective-permute-start.18 = (f16[60,1024]{1,0:T(8,128)(2,1)S(1)}, f16[60,1024]{1,0:T(8,128)(2,1)S(1)}, u32[]{:S(2)}, u32[]{:S(2)}) collective-permute-start(f16[60,1024]{1,0:T(8,128)(2,1)S(1)} %convert_element_type.26), channel_id=1, source_target_pairs={{0,2},{2,0},{1,3},{3,1},{4,6},{6,4},{5,7},{7,5},{8,10},{10,8},{9,1... | collective-permute-start | bytes 368648 | tf_op jit(solution)/shard_map/ppermute | solution.py:56
  60.7 4.1 %collective-permute-start.19 = (f16[20,1024]{1,0:T(8,128)(2,1)S(1)}, f16[20,1024]{1,0:T(8,128)(2,1)S(1)}, u32[]{:S(2)}, u32[]{:S(2)}) collective-permute-start(f16[20,1024]{1,0:T(8,128)(2,1)S(1)} %convert_element_type.27), channel_id=1, source_target_pairs={{0,2},{2,0},{1,3},{3,1},{4,6},{6,4},{5,7},{7,5},{8,10},{10,8},{9,1... | collective-permute-start | bytes 122888 | tf_op jit(solution)/shard_map/ppermute | solution.py:56

commit v4 on v3

--- a/solution.py
+++ b/solution.py
@@ -61,7 +61,7 @@
 
         @pl.when(first == order)
         def _(pair=pair):
-            out_ref[...] = jnp.concatenate([r[...] for r in pair], axis=axis)
+            out_ref[...] = jnp.concatenate(pair, axis=axis)
 
 
 def local_call(kernel, shapes, *operands):
@@ -76,12 +76,15 @@
 
 def join_kernel(mine_ref, mate_ref, out_ref):
     away = lax.axis_index("y") // 2 != lax.axis_index("core")
-    choose(away.astype(jnp.int32), (mine_ref, mate_ref), 1, out_ref)
+    other = mate_ref[...].reshape(mine_ref.shape)
+    choose(away.astype(jnp.int32), (mine_ref[...], other), 0, out_ref)
 
 
 def pack_kernel(far_ref, near_ref, out_ref):
     away = lax.axis_index("xh") != lax.axis_index("xl")
-    choose(away.astype(jnp.int32), (near_ref, far_ref), 0, out_ref)
+    half = near_ref.shape[0] // 2
+    wide = [jnp.concatenate([r[...][:half], r[...][half:]], axis=1) for r in (near_ref, far_ref)]
+    choose(away.astype(jnp.int32), wide, 0, out_ref)
 
 
 def pair_kernel(up_ref, down_ref, out_ref, pick_ref):
@@ -136,27 +139,32 @@
     here, z = lax.axis_index("y") % 2, lax.axis_index("z")
     there = 1 - here
 
-    def put(half, shift, kept, at, back, start):
-        value = kept[at:at + 20, :] + back[start:start + 20, :]
-        total[half, lax.rem(z + shift + Z, Z)] = value
-
-    put(here, 0, m0, 0, b0, 0)
-    put(there, 0, m0, 40, b0, 20)
-    for step, h, at, b, start, s, back in ((1, m0, 80, b0, 40, m1, (b0, 80)), (2, m1, 80, b2, 0, m2, (b2, 40)), (3, m2, 80, b2, 80, m3, (b3, 0))):
-        put(here, step, h, at, b, start)
-        put(here, -step, h, at + 40, b, start + 20)
-        put(there, step, s, 0, back[0], back[1])
-        put(there, -step, s, 40, back[0], back[1] + 20)
-    put(here, 4, m3, 80, b3, 40)
-    put(there, 4, m4, 0, b4, 0)
+    def put(shift, kept, at, back, start):
+        total[lax.rem(z + shift + Z, Z)] = kept[at:at + 20, :] + back[start:start + 20, :]
+
+    col = scale(col_ref[...])
     copies = []
-    for n in range(4):
-        a, first = n // 2, 4 * (n % 2)
-        rows = pl.ds(n * 80, 80)
-        ladder = jnp.concatenate([total[a, i] for i in range(first, first + 4)], axis=0)
-        done[rows, :] = in_ref[rows, :] + (row_ref[rows, :1] * scale(col_ref[...])) * ladder
-        copies.append(pltpu.make_async_copy(done.at[rows], out_ref.at[rows], sems.at[n]))
-        copies[-1].start()
+
+    def leave(a):
+        for n in range(2):
+            rows = pl.ds(pl.multiple_of(a * 160 + n * 80, 80), 80)
+            ladder = jnp.concatenate([total[i] for i in range(4 * n, 4 * n + 4)], axis=0)
+            done[rows, :] = in_ref[rows, :] + (row_ref[rows, :1] * col) * ladder
+            copies.append(pltpu.make_async_copy(done.at[rows], out_ref.at[rows], sems.at[len(copies)]))
+            copies[-1].start()
+
+    put(0, m0, 0, b0, 0)
+    for step, h, at, b, start in ((1, m0, 80, b0, 40), (2, m1, 80, b2, 0), (3, m2, 80, b2, 80)):
+        put(step, h, at, b, start)
+        put(-step, h, at + 40, b, start + 20)
+    put(4, m3, 80, b3, 40)
+    leave(here)
+    put(0, m0, 40, b0, 20)
+    for step, s, b, start in ((1, m1, b0, 80), (2, m2, b2, 40), (3, m3, b3, 0)):
+        put(step, s, 0, b, start)
+        put(-step, s, 40, b, start + 20)
+    put(4, m4, 0, b4, 0)
+    leave(there)
     for copy in copies:
         copy.wait()
 
@@ -168,7 +176,7 @@
         in_specs=[VMEM] * (3 + len(parts)),
         out_specs=pl.BlockSpec(memory_space=pl.ANY),
         scratch_shapes=[
-            pltpu.VMEM((2, Z, 20, residual.shape[1]), F32),
+            pltpu.VMEM((Z, 20, residual.shape[1]), F32),
             pltpu.VMEM(residual.shape, F32),
             pltpu.SemaphoreType.DMA((4,)),
         ],
@@ -214,13 +222,12 @@
 def per_device(amplitudes, integrals, residual_in, pair_list, ab_list):
     tie = lax.optimization_barrier
 
-    mine = amplitudes.reshape(amplitudes.shape[0], -1)
     own = integrals.reshape(-1, integrals.shape[2])
-    pairs, depth = mine.shape
+    pairs, depth = amplitudes.shape[0], own.shape[0]
     block, double = (2 * pairs, 2 * depth), (4 * pairs, 2 * depth)
 
-    mates, own = tie((mate(mine), own))
-    (both,) = local_call(join_kernel, [(pairs, 2 * depth)], mine, mates)
+    mates, mine, own = tie((mate(amplitudes), amplitudes.reshape(pairs, depth), own))
+    (both,) = local_call(join_kernel, [(2 * pairs, depth)], mine, mates)
     slots = spread(both, 1), spread(both, 0)
     other = mate(own)
     (held,) = local_call(pack_kernel, [block], *slots)

time: 66.6 us -> 65.6 us (0.985)
  waiting for transfers between devices: 30.8 us -> 29.3 us
    ppermute x2, waiting for transfers between devices: 0.92 us -> 0.08 us  [mate(): return lax.ppermute(x, 'core', turn(2, 1))]
  transfers between devices with their start and end apart: 20 -> 20, of which waited for: 15 -> 15; matrix products, arithmetic and copies ran while one was open for 11% -> 13% of each run, Pallas kernels for 3% -> 3%
where the time goes in v4:
time: 65.6 us; the launch traced here: 65.1 us
  waiting for transfers between devices  29.3 us (45%)
  starting transfers between devices  23.3 us (36%)
  matrix products  7.36 us (11%)
  Pallas kernels  3.35 us (5%)
  local copies, waits for them, and re-layouts  1.08 us (2%)
    ppermute x3, starting transfers between devices, up(): return lax.ppermute(x, 'z', turn(Z, -1))  7.59 us
    ppermute x5, waiting for transfers between devices, swap(): return lax.ppermute(x, ('y', 'core'), route)  7.47 us
    ppermute x3, waiting for transfers between devices, down(): return lax.ppermute(x, 'z', turn(Z, 1))  6.93 us
    ppermute x3, waiting for transfers between devices, up(): return lax.ppermute(x, 'z', turn(Z, -1))  6.78 us
    ppermute x2, starting transfers between devices, spread(): return lax.ppermute(x, ('xh', 'y', 'core'), route)  5.96 us
    ppermute x2, waiting for transfers between devices, spread(): return lax.ppermute(x, ('xh', 'y', 'core'), route)  5.62 us
    dot_general x5, matrix products, dot(): total = jnp.dot(left, own, preferred_element_type=F32)  3.74 us
    dot_general x5, matrix products, dot(): return total + jnp.dot(right, second, preferred_element_type=F32)  3.62 us
  transfers between devices with their start and end apart: 20, of which 15 were waited for; matrix products, arithmetic and copies ran while one was open for 13% of the time, Pallas kernels for 3%

profile of v4, /device:TPU:1, one launch (start us, length us, event | category | flops | bytes accessed | tf_op | source)
XLA Modules:
  0.0 65.1 jit_solution(17777407092009288245)
XLA Ops:
  0.0 3.2 %collective-permute-start = (bf16[20,8,200]{2,1,0:T(8,128)(2,1)}, bf16[20,8,200]{2,1,0:T(8,128)(2,1)S(1)}, u32[]{:S(2)}, u32[]{:S(2)}) collective-permute-start(bf16[20,8,200]{2,1,0:T(8,128)(2,1)} %param.5), channel_id=1, source_target_pairs={{0,1},{1,0},{2,3},{3,2},{4,5},{5,4},{6,7},{7,6},{8,9},{9,8},{10,11... | collective-permute-start | bytes 192008 | tf_op jit(solution)/shard_map/ppermute | solution.py:52
  3.2 1.1 %reshape.6.mine_ref = bf16[20,1600]{1,0:T(8,128)(2,1)S(1)} reshape(bf16[20,8,200]{2,1,0:T(8,128)(2,1)} %param.5) | data formatting | bytes 128000 | tf_op jit(solution)/shard_map/reshape | solution.py:229
  4.4 0.4 collective-permute-start.5
  4.7 0.1 shard_map.55
  4.9 3.8 %collective-permute-start.1 = (bf16[40,1600]{1,0:T(8,128)(2,1)S(1)}, bf16[40,1600]{1,0:T(8,128)(2,1)S(1)}, u32[]{:S(2)}, u32[]{:S(2)}) collective-permute-start(bf16[40,1600]{1,0:T(8,128)(2,1)S(1)} %shard_map.55), channel_id=1, source_target_pairs={{0,128},{1,192},{32,160},{33,224},{64,129},{65,193},{96,161},{97,2... | collective-permute-start | bytes 384008 | tf_op jit(solution)/shard_map/ppermute | solution.py:48
  8.6 2.2 %collective-permute-start.2 = (bf16[40,1600]{1,0:T(8,128)(2,1)S(1)}, bf16[40,1600]{1,0:T(8,128)(2,1)S(1)}, u32[]{:S(2)}, u32[]{:S(2)}) collective-permute-start(bf16[40,1600]{1,0:T(8,128)(2,1)S(1)} %shard_map.55), channel_id=1, source_target_pairs={{0,0},{1,64},{32,32},{33,96},{64,1},{65,65},{96,33},{97,97},{128,1... | collective-permute-start | bytes 384008 | tf_op jit(solution)/shard_map/ppermute | solution.py:48
  10.8 2.4 %collective-permute-done.1.far_ref = bf16[40,1600]{1,0:T(8,128)(2,1)S(1)} collective-permute-done((bf16[40,1600]{1,0:T(8,128)(2,1)S(1)}, bf16[40,1600]{1,0:T(8,128)(2,1)S(1)}, u32[]{:S(2)}, u32[]{:S(2)}) %collective-permute-start.1) | collective-permute-done | bytes 128032 | tf_op jit(solution)/shard_map/ppermute | solution.py:48
  13.3 3.2 %collective-permute-done.2.near_ref = bf16[40,1600]{1,0:T(8,128)(2,1)S(1)} collective-permute-done((bf16[40,1600]{1,0:T(8,128)(2,1)S(1)}, bf16[40,1600]{1,0:T(8,128)(2,1)S(1)}, u32[]{:S(2)}, u32[]{:S(2)}) %collective-permute-start.2) | collective-permute-done | bytes 128032 | tf_op jit(solution)/shard_map/ppermute | solution.py:48
  16.4 0.2 shard_map.56.refs_0_
  16.6 5.7 %collective-permute-start.3 = (bf16[40,3200]{1,0:T(8,128)(2,1)S(1)}, bf16[40,3200]{1,0:T(8,128)(2,1)S(1)}, u32[]{:S(2)}, u32[]{:S(2)}) collective-permute-start(bf16[40,3200]{1,0:T(8,128)(2,1)S(1)} %shard_map.56.refs_0_), channel_id=1, source_target_pairs={{0,28},{4,0},{8,4},{12,8},{16,12},{20,16},{24,20},{28,24},{1,29},{... | collective-permute-start | bytes 768008 | tf_op jit(solution)/shard_map/ppermute | solution.py:26
  22.3 0.4 shard_map.57
  22.7 4.1 %collective-permute-done.3.refs_0_ = bf16[40,3200]{1,0:T(8,128)(2,1)S(1)} collective-permute-done((bf16[40,3200]{1,0:T(8,128)(2,1)S(1)}, bf16[40,3200]{1,0:T(8,128)(2,1)S(1)}, u32[]{:S(2)}, u32[]{:S(2)}) %collective-permute-start.3) | collective-permute-done | bytes 256032 | tf_op jit(solution)/shard_map/ppermute | solution.py:26
  26.8 3.0 %collective-permute-done.4.refs_1_ = bf16[40,3200]{1,0:T(8,128)(2,1)S(1)} collective-permute-done((bf16[40,3200]{1,0:T(8,128)(2,1)S(1)}, bf16[40,3200]{1,0:T(8,128)(2,1)S(1)}, u32[]{:S(2)}, u32[]{:S(2)}) %collective-permute-start.4) | collective-permute-done | bytes 256032 | tf_op jit(solution)/shard_map/ppermute | solution.py:30
  29.8 0.4 collective-permute-start.6
  30.2 1.1 %collective-permute-start.7 = (bf16[40,3200]{1,0:T(8,128)(2,1)S(1)}, bf16[40,3200]{1,0:T(8,128)(2,1)S(1)}, u32[]{:S(2)}, u32[]{:S(2)}) collective-permute-start(bf16[40,3200]{1,0:T(8,128)(2,1)S(1)} %collective-permute-done.4.refs_1_), channel_id=1, source_target_pairs={{0,4},{4,8},{8,12},{12,16},{16,20},{20,24},{24,28},{28,0},{1,5},{5... | collective-permute-start | bytes 768008 | tf_op jit(solution)/shard_map/ppermute | solution.py:30
  31.4 0.2 shard_map.59
  31.6 0.8 %fusion = f32[160,1024]{1,0:T(8,128)S(1)} fusion(bf16[160,1600]{1,0:T(8,128)(2,1)S(1)} %get-tuple-element.45, bf16[1600,1024]{1,0:T(8,128)(2,1)S(1)} %shard_map.57), kind=kOutput, calls=%fused_computation.5 | convolution fusion | flops 524288000 | bytes 4444160 | tf_op jit(solution)/shard_map/dot_general | solution.py:238
  32.4 0.8 %convolution_add_fusion.2.refs_0_.refs_1_.refs_2_.refs_3_ = f32[160,1024]{1,0:T(8,128)S(1)} fusion(f32[160,1024]{1,0:T(8,128)S(1)} %fusion, bf16[160,1600]{1,0:T(8,128)(2,1)S(1)} %get-tuple-element.44, bf16[1600,1024]{1,0:T(8,128)(2,1)S(1)} %bitcast.26), kind=kOutput, calls=%fused_computation.2 | convolution fusion | flops 524451840 | bytes 5099520 | tf_op jit(solution)/shard_map/dot_general | solution.py:237
  33.3 1.7 %collective-permute-done.6.refs_0_ = bf16[40,3200]{1,0:T(8,128)(2,1)S(1)} collective-permute-done((bf16[40,3200]{1,0:T(8,128)(2,1)S(1)}, bf16[40,3200]{1,0:T(8,128)(2,1)S(1)}, u32[]{:S(2)}, u32[]{:S(2)}) %collective-permute-start.6) | collective-permute-done | bytes 256032 | tf_op jit(solution)/shard_map/ppermute | solution.py:26
  34.9 2.5 %collective-permute-done.7.refs_1_ = bf16[40,3200]{1,0:T(8,128)(2,1)S(1)} collective-permute-done((bf16[40,3200]{1,0:T(8,128)(2,1)S(1)}, bf16[40,3200]{1,0:T(8,128)(2,1)S(1)}, u32[]{:S(2)}, u32[]{:S(2)}) %collective-permute-start.7) | collective-permute-done | bytes 256032 | tf_op jit(solution)/shard_map/ppermute | solution.py:30
  37.5 1.2 %collective-permute-start.10 = (bf16[40,3200]{1,0:T(8,128)(2,1)S(1)}, bf16[40,3200]{1,0:T(8,128)(2,1)S(1)}, u32[]{:S(2)}, u32[]{:S(2)}) collective-permute-start(bf16[40,3200]{1,0:T(8,128)(2,1)S(1)} %collective-permute-done.7.refs_1_), channel_id=1, source_target_pairs={{0,4},{4,8},{8,12},{12,16},{16,20},{20,24},{24,28},{28,0},{1,5},{5... | collective-permute-start | bytes 768008 | tf_op jit(solution)/shard_map/ppermute | solution.py:30
  38.7 1.5 %collective-permute-start.9 = (bf16[40,3200]{1,0:T(8,128)(2,1)S(1)}, bf16[40,3200]{1,0:T(8,128)(2,1)S(1)}, u32[]{:S(2)}, u32[]{:S(2)}) collective-permute-start(bf16[40,3200]{1,0:T(8,128)(2,1)S(1)} %collective-permute-done.6.refs_0_), channel_id=1, source_target_pairs={{0,28},{4,0},{8,4},{12,8},{16,12},{20,16},{24,20},{28,24},{1,29},{... | collective-permute-start | bytes 768008 | tf_op jit(solution)/shard_map/ppermute | solution.py:26
  40.3 0.2 collective-permute-done.11.refs_0_
  40.5 0.2 shard_map.61
  40.7 0.8 %fusion.1 = f32[160,1024]{1,0:T(8,128)S(1)} fusion(bf16[160,1600]{1,0:T(8,128)(2,1)S(1)} %get-tuple-element.50, bf16[1600,1024]{1,0:T(8,128)(2,1)S(1)} %shard_map.57), kind=kOutput, calls=%fused_computation.6 | convolution fusion | flops 524288000 | bytes 4444160 | tf_op jit(solution)/shard_map/dot_general | solution.py:238
  41.5 0.8 %convolution_add_fusion.1.refs_4_.refs_5_.refs_0_.refs_1_ = f32[160,1024]{1,0:T(8,128)S(1)} fusion(f32[160,1024]{1,0:T(8,128)S(1)} %fusion.1, bf16[160,1600]{1,0:T(8,128)(2,1)S(1)} %get-tuple-element.49, bf16[1600,1024]{1,0:T(8,128)(2,1)S(1)} %bitcast.27), kind=kOutput, calls=%fused_computation.1 | convolution fusion | flops 524451840 | bytes 5099520 | tf_op jit(solution)/shard_map/dot_general | solution.py:237
  42.4 1.4 %collective-permute-done.10.down_ref = bf16[40,3200]{1,0:T(8,128)(2,1)S(1)} collective-permute-done((bf16[40,3200]{1,0:T(8,128)(2,1)S(1)}, bf16[40,3200]{1,0:T(8,128)(2,1)S(1)}, u32[]{:S(2)}, u32[]{:S(2)}) %collective-permute-start.10) | collective-permute-done | bytes 256032 | tf_op jit(solution)/shard_map/ppermute | solution.py:30
  43.8 1.0 %collective-permute-done.9.up_ref = bf16[40,3200]{1,0:T(8,128)(2,1)S(1)} collective-permute-done((bf16[40,3200]{1,0:T(8,128)(2,1)S(1)}, bf16[40,3200]{1,0:T(8,128)(2,1)S(1)}, u32[]{:S(2)}, u32[]{:S(2)}) %collective-permute-start.9) | collective-permute-done | bytes 256032 | tf_op jit(solution)/shard_map/ppermute | solution.py:26
  44.9 1.4 %collective-permute-start.12 = (bf16[40,3200]{1,0:T(8,128)(2,1)S(1)}, bf16[40,3200]{1,0:T(8,128)(2,1)S(1)}, u32[]{:S(2)}, u32[]{:S(2)}) collective-permute-start(bf16[40,3200]{1,0:T(8,128)(2,1)S(1)} %get-tuple-element.54), channel_id=1, source_target_pairs={{0,28},{1,5},{4,0},{5,9},{8,4},{9,13},{12,8},{13,17},{16,12},{17,2... | collective-permute-start | bytes 768008 | tf_op jit(solution)/shard_map/ppermute | solution.py:35
  46.3 3.1 %collective-permute-done.13.refs_0_ = bf16[80,3200]{1,0:T(8,128)(2,1)S(1)} collective-permute-done((bf16[80,3200]{1,0:T(8,128)(2,1)S(1)}, bf16[80,3200]{1,0:T(8,128)(2,1)S(1)}, u32[]{:S(2)}, u32[]{:S(2)}) %collective-permute-start.13) | collective-permute-done | bytes 512032 | tf_op jit(solution)/shard_map/ppermute | solution.py:40
  49.4 0.2 shard_map.64
  49.6 0.8 %fusion.2 = f32[160,1024]{1,0:T(8,128)S(1)} fusion(bf16[160,1600]{1,0:T(8,128)(2,1)S(1)} %get-tuple-element.57, bf16[1600,1024]{1,0:T(8,128)(2,1)S(1)} %shard_map.57), kind=kOutput, calls=%fused_computation.7 | convolution fusion | flops 524288000 | bytes 4444160 | tf_op jit(solution)/shard_map/dot_general | solution.py:238
  50.4 0.8 %convolution_add_fusion.refs_2_.refs_3_.refs_4_.refs_5_ = f32[160,1024]{1,0:T(8,128)S(1)} fusion(f32[160,1024]{1,0:T(8,128)S(1)} %fusion.2, bf16[160,1600]{1,0:T(8,128)(2,1)S(1)} %get-tuple-element.56, bf16[1600,1024]{1,0:T(8,128)(2,1)S(1)} %bitcast.28), kind=kOutput, calls=%fused_computation | convolution fusion | flops 524451840 | bytes 5099520 | tf_op jit(solution)/shard_map/dot_general | solution.py:237
  51.2 0.3 collective-permute-done.12.refs_1_
  51.6 0.8 %collective-permute-start.17 = (f16[120,1024]{1,0:T(8,128)(2,1)S(1)}, f16[120,1024]{1,0:T(8,128)(2,1)S(1)}, u32[]{:S(2)}, u32[]{:S(2)}) collective-permute-start(f16[120,1024]{1,0:T(8,128)(2,1)S(1)} %convert_element_type.25), channel_id=1, source_target_pairs={{0,2},{2,0},{1,3},{3,1},{4,6},{6,4},{5,7},{7,5},{8,10},{10,8},{9,1... | collective-permute-start | bytes 737288 | tf_op jit(solution)/shard_map/ppermute | solution.py:56
  52.4 3.0 %collective-permute-done.15.refs_0_ = bf16[80,3200]{1,0:T(8,128)(2,1)S(1)} collective-permute-done((bf16[80,3200]{1,0:T(8,128)(2,1)S(1)}, bf16[80,3200]{1,0:T(8,128)(2,1)S(1)}, u32[]{:S(2)}, u32[]{:S(2)}) %collective-permute-start.15) | collective-permute-done | bytes 512032 | tf_op jit(solution)/shard_map/ppermute | solution.py:40
  55.4 0.2 shard_map.66
  55.6 0.6 fusion.3
  56.2 0.7 %convolution_add_fusion.3.refs_0_.refs_1_.refs_2_.refs_3_ = f32[120,1024]{1,0:T(8,128)S(1)} fusion(f32[120,1024]{1,0:T(8,128)S(1)} %fusion.3, bf16[120,1600]{1,0:T(8,128)(2,1)S(1)} %get-tuple-element.60, bf16[1600,1024]{1,0:T(8,128)(2,1)S(1)} %bitcast.29), kind=kOutput, calls=%fused_computation.3 | convolution fusion | flops 393338880 | bytes 4643840 | tf_op jit(solution)/shard_map/dot_general | solution.py:237
  57.0 1.2 %collective-permute-done.14.refs_0_ = bf16[40,3200]{1,0:T(8,128)(2,1)S(1)} collective-permute-done((bf16[40,3200]{1,0:T(8,128)(2,1)S(1)}, bf16[40,3200]{1,0:T(8,128)(2,1)S(1)}, u32[]{:S(2)}, u32[]{:S(2)}) %collective-permute-start.14) | collective-permute-done | bytes 256032 | tf_op jit(solution)/shard_map/ppermute | solution.py:40
  58.1 0.1 shard_map.68
  58.2 0.7 %fusion.4 = f32[40,1024]{1,0:T(8,128)S(1)} fusion(bf16[40,1600]{1,0:T(8,128)(2,1)S(1)} %get-tuple-element.64, bf16[1600,1024]{1,0:T(8,128)(2,1)S(1)} %shard_map.57), kind=kOutput, calls=%fused_computation.9 | convolution fusion | flops 131072000 | bytes 3568640 | tf_op jit(solution)/shard_map/dot_general | solution.py:238
  58.9 0.1 collective-permute-start.18
  59.0 0.7 %convolution_add_fusion.4.refs_0_.refs_4_ = f32[40,1024]{1,0:T(8,128)S(1)} fusion(f32[40,1024]{1,0:T(8,128)S(1)} %fusion.4, bf16[40,1600]{1,0:T(8,128)(2,1)S(1)} %get-tuple-element.63, bf16[1600,1024]{1,0:T(8,128)(2,1)S(1)} %bitcast.30), kind=kOutput, calls=%fused_computation.4 | convolution fusion | flops 131112960 | bytes 3732480 | tf_op jit(solution)/shard_map/dot_general | solution.py:237
  59.8 1.5 %collective-permute-start.19 = (f16[20,1024]{1,0:T(8,128)(2,1)S(1)}, f16[20,1024]{1,0:T(8,128)(2,1)S(1)}, u32[]{:S(2)}, u32[]{:S(2)}) collective-permute-start(f16[20,1024]{1,0:T(8,128)(2,1)S(1)} %convert_element_type.27), channel_id=1, source_target_pairs={{0,2},{2,0},{1,3},{3,1},{4,6},{6,4},{5,7},{7,5},{8,10},{10,8},{9,1... | collective-permute-start | bytes 122888 | tf_op jit(solution)/shard_map/ppermute | solution.py:56
  61.4 0.1 shard_map.70.row_ref
  61.5 2.1 %collective-permute-done.19 = f16[20,1024]{1,0:T(8,128)(2,1)S(1)} collective-permute-done((f16[20,1024]{1,0:T(8,128)(2,1)S(1)}, f16[20,1024]{1,0:T(8,128)(2,1)S(1)}, u32[]{:S(2)}, u32[]{:S(2)}) %collective-permute-start.19) | collective-permute-done | bytes 40992 | tf_op jit(solution)/shard_map/ppermute | solution.py:56
  63.7 1.3 %shard_map.71 = f32[320,1024]{1,0:T(8,128)} custom-call(f32[320,1024]{1,0:T(8,128)S(1)} %copy-done, f32[320,128]{1,0:T(8,128)S(1)} %shard_map.70.row_ref, s32[2,1024]{1,0:T(2,128)S(1)} %bitcast.23, f32[160,1024]{1,0:T(8,128)S(1)} %convolution_add_fusion.2.refs_0_.refs_1_.refs_2_.refs_3_, ...), custom_call_target="tpu_custom_call" | custom-call | tf_op jit(solution)/shard_map/pallas_call | solution.py:173
  (36 shorter events, 0.6 us)
Async XLA Ops:
  0.0 4.4 %collective-permute-start = (bf16[20,8,200]{2,1,0:T(8,128)(2,1)}, bf16[20,8,200]{2,1,0:T(8,128)(2,1)S(1)}, u32[]{:S(2)}, u32[]{:S(2)}) collective-permute-start(bf16[20,8,200]{2,1,0:T(8,128)(2,1)} %param.5), channel_id=1, source_target_pairs={{0,1},{1,0},{2,3},{3,2},{4,5},{5,4},{6,7},{7,6},{8,9},{9,8},{10,11... | collective-permute-start | bytes 192008 | tf_op jit(solution)/shard_map/ppermute | solution.py:52
  4.4 17.9 %collective-permute-start.5 = (bf16[1600,1024]{1,0:T(8,128)(2,1)}, bf16[1600,1024]{1,0:T(8,128)(2,1)S(1)}, u32[]{:S(2)}, u32[]{:S(2)}) collective-permute-start(bf16[1600,1024]{1,0:T(8,128)(2,1)} %bitcast.25), channel_id=1, source_target_pairs={{0,1},{1,0},{2,3},{3,2},{4,5},{5,4},{6,7},{7,6},{8,9},{9,8},{10,11... | collective-permute-start | bytes 9830408 | tf_op jit(solution)/shard_map/ppermute | solution.py:52
  4.9 8.4 %collective-permute-start.1 = (bf16[40,1600]{1,0:T(8,128)(2,1)S(1)}, bf16[40,1600]{1,0:T(8,128)(2,1)S(1)}, u32[]{:S(2)}, u32[]{:S(2)}) collective-permute-start(bf16[40,1600]{1,0:T(8,128)(2,1)S(1)} %shard_map.55), channel_id=1, source_target_pairs={{0,128},{1,192},{32,160},{33,224},{64,129},{65,193},{96,161},{97,2... | collective-permute-start | bytes 384008 | tf_op jit(solution)/shard_map/ppermute | solution.py:48
  8.6 7.8 %collective-permute-start.2 = (bf16[40,1600]{1,0:T(8,128)(2,1)S(1)}, bf16[40,1600]{1,0:T(8,128)(2,1)S(1)}, u32[]{:S(2)}, u32[]{:S(2)}) collective-permute-start(bf16[40,1600]{1,0:T(8,128)(2,1)S(1)} %shard_map.55), channel_id=1, source_target_pairs={{0,0},{1,64},{32,32},{33,96},{64,1},{65,65},{96,33},{97,97},{128,1... | collective-permute-start | bytes 384008 | tf_op jit(solution)/shard_map/ppermute | solution.py:48
  16.6 10.2 %collective-permute-start.3 = (bf16[40,3200]{1,0:T(8,128)(2,1)S(1)}, bf16[40,3200]{1,0:T(8,128)(2,1)S(1)}, u32[]{:S(2)}, u32[]{:S(2)}) collective-permute-start(bf16[40,3200]{1,0:T(8,128)(2,1)S(1)} %shard_map.56.refs_0_), channel_id=1, source_target_pairs={{0,28},{4,0},{8,4},{12,8},{16,12},{20,16},{24,20},{28,24},{1,29},{... | collective-permute-start | bytes 768008 | tf_op jit(solution)/shard_map/ppermute | solution.py:26
  22.3 7.5 %collective-permute-start.4 = (bf16[40,3200]{1,0:T(8,128)(2,1)S(1)}, bf16[40,3200]{1,0:T(8,128)(2,1)S(1)}, u32[]{:S(2)}, u32[]{:S(2)}) collective-permute-start(bf16[40,3200]{1,0:T(8,128)(2,1)S(1)} %shard_map.56.refs_0_), channel_id=1, source_target_pairs={{0,4},{4,8},{8,12},{12,16},{16,20},{20,24},{24,28},{28,0},{1,5},{5... | collective-permute-start | bytes 768008 | tf_op jit(solution)/shard_map/ppermute | solution.py:30
  22.3 9.1 %collective-permute-start.8 = (bf16[40,3200]{1,0:T(8,128)(2,1)S(1)}, bf16[40,3200]{1,0:T(8,128)(2,1)S(1)}, u32[]{:S(2)}, u32[]{:S(2)}) collective-permute-start(bf16[40,3200]{1,0:T(8,128)(2,1)S(1)} %shard_map.56.refs_0_), channel_id=1, source_target_pairs={{0,32},{1,97},{32,0},{33,65},{64,96},{65,33},{96,64},{97,1},{2,34}... | collective-permute-start | bytes 768008 | tf_op jit(solution)/shard_map/ppermute | solution.py:40
  22.7 9.8 %copy-start.3 = (bf16[8,200,1024]{2,1,0:T(8,128)(2,1)S(1)}, bf16[8,200,1024]{2,1,0:T(8,128)(2,1)}, u32[]{:S(2)}) copy-start(bf16[8,200,1024]{2,1,0:T(8,128)(2,1)} %param.6) | copy-start | bytes 9830404
  29.8 5.2 %collective-permute-start.6 = (bf16[40,3200]{1,0:T(8,128)(2,1)S(1)}, bf16[40,3200]{1,0:T(8,128)(2,1)S(1)}, u32[]{:S(2)}, u32[]{:S(2)}) collective-permute-start(bf16[40,3200]{1,0:T(8,128)(2,1)S(1)} %collective-permute-done.3.refs_0_), channel_id=1, source_target_pairs={{0,28},{4,0},{8,4},{12,8},{16,12},{20,16},{24,20},{28,24},{1,29},{... | collective-permute-start | bytes 768008 | tf_op jit(solution)/shard_map/ppermute | solution.py:26
  30.2 7.2 %collective-permute-start.7 = (bf16[40,3200]{1,0:T(8,128)(2,1)S(1)}, bf16[40,3200]{1,0:T(8,128)(2,1)S(1)}, u32[]{:S(2)}, u32[]{:S(2)}) collective-permute-start(bf16[40,3200]{1,0:T(8,128)(2,1)S(1)} %collective-permute-done.4.refs_1_), channel_id=1, source_target_pairs={{0,4},{4,8},{8,12},{12,16},{16,20},{20,24},{24,28},{28,0},{1,5},{5... | collective-permute-start | bytes 768008 | tf_op jit(solution)/shard_map/ppermute | solution.py:30
  31.4 9.1 %collective-permute-start.11 = (bf16[80,3200]{1,0:T(8,128)(2,1)S(1)}, bf16[80,3200]{1,0:T(8,128)(2,1)S(1)}, u32[]{:S(2)}, u32[]{:S(2)}) collective-permute-start(bf16[80,3200]{1,0:T(8,128)(2,1)S(1)} %shard_map.58.refs_2_), channel_id=1, source_target_pairs={{0,32},{1,97},{32,0},{33,65},{64,96},{65,33},{96,64},{97,1},{2,34}... | collective-permute-start | bytes 1536008 | tf_op jit(solution)/shard_map/ppermute | solution.py:40
  37.5 6.4 %collective-permute-start.10 = (bf16[40,3200]{1,0:T(8,128)(2,1)S(1)}, bf16[40,3200]{1,0:T(8,128)(2,1)S(1)}, u32[]{:S(2)}, u32[]{:S(2)}) collective-permute-start(bf16[40,3200]{1,0:T(8,128)(2,1)S(1)} %collective-permute-done.7.refs_1_), channel_id=1, source_target_pairs={{0,4},{4,8},{8,12},{12,16},{16,20},{20,24},{24,28},{28,0},{1,5},{5... | collective-permute-start | bytes 768008 | tf_op jit(solution)/shard_map/ppermute | solution.py:30
  38.7 6.1 %collective-permute-start.9 = (bf16[40,3200]{1,0:T(8,128)(2,1)S(1)}, bf16[40,3200]{1,0:T(8,128)(2,1)S(1)}, u32[]{:S(2)}, u32[]{:S(2)}) collective-permute-start(bf16[40,3200]{1,0:T(8,128)(2,1)S(1)} %collective-permute-done.6.refs_0_), channel_id=1, source_target_pairs={{0,28},{4,0},{8,4},{12,8},{16,12},{20,16},{24,20},{28,24},{1,29},{... | collective-permute-start | bytes 768008 | tf_op jit(solution)/shard_map/ppermute | solution.py:26
  40.3 9.1 %collective-permute-start.13 = (bf16[80,3200]{1,0:T(8,128)(2,1)S(1)}, bf16[80,3200]{1,0:T(8,128)(2,1)S(1)}, u32[]{:S(2)}, u32[]{:S(2)}) collective-permute-start(bf16[80,3200]{1,0:T(8,128)(2,1)S(1)} %shard_map.60.refs_1_), channel_id=1, source_target_pairs={{0,32},{1,97},{32,0},{33,65},{64,96},{65,33},{96,64},{97,1},{2,34}... | collective-permute-start | bytes 1536008 | tf_op jit(solution)/shard_map/ppermute | solution.py:40
  44.9 6.6 %collective-permute-start.12 = (bf16[40,3200]{1,0:T(8,128)(2,1)S(1)}, bf16[40,3200]{1,0:T(8,128)(2,1)S(1)}, u32[]{:S(2)}, u32[]{:S(2)}) collective-permute-start(bf16[40,3200]{1,0:T(8,128)(2,1)S(1)} %get-tuple-element.54), channel_id=1, source_target_pairs={{0,28},{1,5},{4,0},{5,9},{8,4},{9,13},{12,8},{13,17},{16,12},{17,2... | collective-permute-start | bytes 768008 | tf_op jit(solution)/shard_map/ppermute | solution.py:35
  46.3 9.1 %collective-permute-start.15 = (bf16[80,3200]{1,0:T(8,128)(2,1)S(1)}, bf16[80,3200]{1,0:T(8,128)(2,1)S(1)}, u32[]{:S(2)}, u32[]{:S(2)}) collective-permute-start(bf16[80,3200]{1,0:T(8,128)(2,1)S(1)} %get-tuple-element.55.refs_1_), channel_id=1, source_target_pairs={{0,32},{1,97},{32,0},{33,65},{64,96},{65,33},{96,64},{97,1},{2,34}... | collective-permute-start | bytes 1536008 | tf_op jit(solution)/shard_map/ppermute | solution.py:40
  46.3 15.0 %collective-permute-start.16 = (f16[120,1024]{1,0:T(8,128)(2,1)S(1)}, f16[120,1024]{1,0:T(8,128)(2,1)S(1)}, u32[]{:S(2)}, u32[]{:S(2)}) collective-permute-start(f16[120,1024]{1,0:T(8,128)(2,1)S(1)} %convert_element_type.24), channel_id=1, source_target_pairs={{0,2},{2,0},{1,3},{3,1},{4,6},{6,4},{5,7},{7,5},{8,10},{10,8},{9,1... | collective-permute-start | bytes 737288 | tf_op jit(solution)/shard_map/ppermute | solution.py:56
  51.5 6.6 %collective-permute-start.14 = (bf16[40,3200]{1,0:T(8,128)(2,1)S(1)}, bf16[40,3200]{1,0:T(8,128)(2,1)S(1)}, u32[]{:S(2)}, u32[]{:S(2)}) collective-permute-start(bf16[40,3200]{1,0:T(8,128)(2,1)S(1)} %collective-permute-done.12.refs_1_), channel_id=1, source_target_pairs={{0,32},{1,97},{32,0},{33,65},{64,96},{65,33},{96,64},{97,1},{2,34}... | collective-permute-start | bytes 768008 | tf_op jit(solution)/shard_map/ppermute | solution.py:40
  51.6 9.8 %collective-permute-start.17 = (f16[120,1024]{1,0:T(8,128)(2,1)S(1)}, f16[120,1024]{1,0:T(8,128)(2,1)S(1)}, u32[]{:S(2)}, u32[]{:S(2)}) collective-permute-start(f16[120,1024]{1,0:T(8,128)(2,1)S(1)} %convert_element_type.25), channel_id=1, source_target_pairs={{0,2},{2,0},{1,3},{3,1},{4,6},{6,4},{5,7},{7,5},{8,10},{10,8},{9,1... | collective-permute-start | bytes 737288 | tf_op jit(solution)/shard_map/ppermute | solution.py:56
  58.9 2.5 %copy-start.2 = (s32[320,2]{0,1:T(2,128)S(1)}, s32[320,2]{0,1:T(2,128)}, u32[]{:S(2)}) copy-start(s32[320,2]{0,1:T(2,128)} %param.8) | copy-start | bytes 7684
  58.9 4.8 %copy-start = (f32[320,1024]{1,0:T(8,128)S(1)}, f32[320,1024]{1,0:T(8,128)}, u32[]{:S(2)}) copy-start(f32[320,1024]{1,0:T(8,128)} %in_ref.1) | copy-start | bytes 3932164
  58.9 4.8 %copy-start.1 = (s32[1024,2]{0,1:T(2,128)S(1)}, s32[1024,2]{0,1:T(2,128)}, u32[]{:S(2)}) copy-start(s32[1024,2]{0,1:T(2,128)} %param.9) | copy-start | bytes 24580
  58.9 4.7 %collective-permute-start.18 = (f16[60,1024]{1,0:T(8,128)(2,1)S(1)}, f16[60,1024]{1,0:T(8,128)(2,1)S(1)}, u32[]{:S(2)}, u32[]{:S(2)}) collective-permute-start(f16[60,1024]{1,0:T(8,128)(2,1)S(1)} %convert_element_type.26), channel_id=1, source_target_pairs={{0,2},{2,0},{1,3},{3,1},{4,6},{6,4},{5,7},{7,5},{8,10},{10,8},{9,1... | collective-permute-start | bytes 368648 | tf_op jit(solution)/shard_map/ppermute | solution.py:56
  59.8 3.9 %collective-permute-start.19 = (f16[20,1024]{1,0:T(8,128)(2,1)S(1)}, f16[20,1024]{1,0:T(8,128)(2,1)S(1)}, u32[]{:S(2)}, u32[]{:S(2)}) collective-permute-start(f16[20,1024]{1,0:T(8,128)(2,1)S(1)} %convert_element_type.27), channel_id=1, source_target_pairs={{0,2},{2,0},{1,3},{3,1},{4,6},{6,4},{5,7},{7,5},{8,10},{10,8},{9,1... | collective-permute-start | bytes 122888 | tf_op jit(solution)/shard_map/ppermute | solution.py:56

commit v5 on v4

--- a/solution.py
+++ b/solution.py
@@ -154,13 +154,13 @@
             copies[-1].start()
 
     put(0, m0, 0, b0, 0)
-    for step, h, at, b, start in ((1, m0, 80, b0, 40), (2, m1, 80, b2, 0), (3, m2, 80, b2, 80)):
+    for step, h, at, b, start in ((1, m0, 80, b0, 40), (2, m1, 80, b0, 120), (3, m2, 80, b2, 40)):
         put(step, h, at, b, start)
         put(-step, h, at + 40, b, start + 20)
     put(4, m3, 80, b3, 40)
     leave(here)
     put(0, m0, 40, b0, 20)
-    for step, s, b, start in ((1, m1, b0, 80), (2, m2, b2, 40), (3, m3, b3, 0)):
+    for step, s, b, start in ((1, m1, b0, 80), (2, m2, b2, 0), (3, m3, b3, 0)):
         put(step, s, 0, b, start)
         put(-step, s, 40, b, start + 20)
     put(4, m4, 0, b4, 0)
@@ -239,26 +239,26 @@
 
     above, below = up(held), down(held)
     swap0 = swap(held)
-    above, below, second = tie((above, below, fetch(other)))
+    above, second = tie((above, fetch(other)))
     old = above, below
     above, below = up(above), down(below)
     beside = stack(*old)
     swap1 = swap(beside)
     m0 = dot(held, swap0, beside)
-    above, below, m0 = tie((above, below, m0))
+    below, m0 = tie((below, m0))
     old = above, below
     above, below = up(above), down(below)
-    beside = stack(*old)
+    beside, swap1 = tie((stack(*old), swap1))
     swap2 = swap(beside)
     m1 = dot(swap1, beside)
-    goes0 = low((m0, 20), (m0, 60), (m0, 100), (m0, 140), (m1, 20), (m1, 60))
+    goes0 = low((m0, 20), (m0, 60), (m0, 100), (m0, 140), (m1, 20), (m1, 60), (m1, 100), (m1, 140))
     above, below, m1, goes0 = tie((above, below, m1, goes0))
     beside, pick = local_call(pair_kernel, [double, block], above, below)
     opposite = either(pick)
     swap3 = swap(beside)
     b0 = trade(goes0)
     m2 = dot(swap2, beside)
-    goes2 = low((m1, 100), (m1, 140), (m2, 20), (m2, 60), (m2, 100), (m2, 140))
+    goes2 = low((m2, 20), (m2, 60), (m2, 100), (m2, 140))
     opposite, m2, goes2 = tie((opposite, m2, goes2))
     swap4 = swap(opposite)
     b2 = trade(goes2)

time: 65.6 us -> 64.8 us (0.988)
  waiting for transfers between devices: 29.3 us -> 25.1 us
  starting transfers between devices: 23.3 us -> 26.7 us
    ppermute x3, waiting for transfers between devices: 6.78 us -> 0.01 us  [up(): return lax.ppermute(x, 'z', turn(Z, -1))]
    ppermute x5, starting transfers between devices: 0.05 us -> 3.3 us  [swap(): return lax.ppermute(x, ('y', 'core'), route)]
    ppermute x5, waiting for transfers between devices: 7.47 us -> 10.4 us  [swap(): return lax.ppermute(x, ('y', 'core'), route)]
    ppermute x3, starting transfers between devices: 7.59 us -> 10.1 us  [up(): return lax.ppermute(x, 'z', turn(Z, -1))]
    ppermute x1, starting transfers between devices: 1.35 us -> 0.26 us  [either(): return lax.ppermute(x, ('z', 'core'), route)]
    ppermute x4, starting transfers between devices: 2.44 us -> 1.73 us  [trade(): return lax.ppermute(x, 'xl', turn(XL, 1))]
  transfers between devices with their start and end apart: 20 -> 20, of which waited for: 15 -> 11; matrix products, arithmetic and copies ran while one was open for 13% -> 13% of each run, Pallas kernels for 3% -> 3%
where the time goes in v5:
time: 64.8 us; the launch traced here: 64.2 us
  starting transfers between devices  26.7 us (41%)
  waiting for transfers between devices  25.1 us (39%)
  matrix products  7.27 us (11%)
  Pallas kernels  3.34 us (5%)
  local copies, waits for them, and re-layouts  1.08 us (2%)
    ppermute x5, waiting for transfers between devices, swap(): return lax.ppermute(x, ('y', 'core'), route)  10.4 us
    ppermute x3, starting transfers between devices, up(): return lax.ppermute(x, 'z', turn(Z, -1))  10.1 us
    ppermute x3, waiting for transfers between devices, down(): return lax.ppermute(x, 'z', turn(Z, 1))  7.14 us
    ppermute x2, starting transfers between devices, spread(): return lax.ppermute(x, ('xh', 'y', 'core'), route)  5.96 us
    ppermute x2, waiting for transfers between devices, spread(): return lax.ppermute(x, ('xh', 'y', 'core'), route)  5.62 us
    dot_general x5, matrix products, dot(): total = jnp.dot(left, own, preferred_element_type=F32)  3.64 us
    dot_general x5, matrix products, dot(): return total + jnp.dot(right, second, preferred_element_type=F32)  3.63 us
    ppermute x2, starting transfers between devices, mate(): return lax.ppermute(x, 'core', turn(2, 1))  3.59 us
  transfers between devices with their start and end apart: 20, of which 11 were waited for; matrix products, arithmetic and copies ran while one was open for 13% of the time, Pallas kernels for 3%

profile of v5, /device:TPU:1, one launch (start us, length us, event | category | flops | bytes accessed | tf_op | source)
XLA Modules:
  0.0 64.2 jit_solution(2607831211707327854)
XLA Ops:
  0.0 3.2 %collective-permute-start = (bf16[20,8,200]{2,1,0:T(8,128)(2,1)}, bf16[20,8,200]{2,1,0:T(8,128)(2,1)S(1)}, u32[]{:S(2)}, u32[]{:S(2)}) collective-permute-start(bf16[20,8,200]{2,1,0:T(8,128)(2,1)} %param.5), channel_id=1, source_target_pairs={{0,1},{1,0},{2,3},{3,2},{4,5},{5,4},{6,7},{7,6},{8,9},{9,8},{10,11... | collective-permute-start | bytes 192008 | tf_op jit(solution)/shard_map/ppermute | solution.py:52
  3.2 1.1 %reshape.6.mine_ref = bf16[20,1600]{1,0:T(8,128)(2,1)S(1)} reshape(bf16[20,8,200]{2,1,0:T(8,128)(2,1)} %param.5) | data formatting | bytes 128000 | tf_op jit(solution)/shard_map/reshape | solution.py:229
  4.3 0.1 collective-permute-done.mate_ref
  4.4 0.4 collective-permute-start.4
  4.7 0.1 shard_map.55
  4.9 3.8 %collective-permute-start.1 = (bf16[40,1600]{1,0:T(8,128)(2,1)S(1)}, bf16[40,1600]{1,0:T(8,128)(2,1)S(1)}, u32[]{:S(2)}, u32[]{:S(2)}) collective-permute-start(bf16[40,1600]{1,0:T(8,128)(2,1)S(1)} %shard_map.55), channel_id=1, source_target_pairs={{0,128},{1,192},{32,160},{33,224},{64,129},{65,193},{96,161},{97,2... | collective-permute-start | bytes 384008 | tf_op jit(solution)/shard_map/ppermute | solution.py:48
  8.6 2.2 %collective-permute-start.2 = (bf16[40,1600]{1,0:T(8,128)(2,1)S(1)}, bf16[40,1600]{1,0:T(8,128)(2,1)S(1)}, u32[]{:S(2)}, u32[]{:S(2)}) collective-permute-start(bf16[40,1600]{1,0:T(8,128)(2,1)S(1)} %shard_map.55), channel_id=1, source_target_pairs={{0,0},{1,64},{32,32},{33,96},{64,1},{65,65},{96,33},{97,97},{128,1... | collective-permute-start | bytes 384008 | tf_op jit(solution)/shard_map/ppermute | solution.py:48
  10.8 2.4 %collective-permute-done.1.far_ref = bf16[40,1600]{1,0:T(8,128)(2,1)S(1)} collective-permute-done((bf16[40,1600]{1,0:T(8,128)(2,1)S(1)}, bf16[40,1600]{1,0:T(8,128)(2,1)S(1)}, u32[]{:S(2)}, u32[]{:S(2)}) %collective-permute-start.1) | collective-permute-done | bytes 128032 | tf_op jit(solution)/shard_map/ppermute | solution.py:48
  13.3 3.2 %collective-permute-done.2.near_ref = bf16[40,1600]{1,0:T(8,128)(2,1)S(1)} collective-permute-done((bf16[40,1600]{1,0:T(8,128)(2,1)S(1)}, bf16[40,1600]{1,0:T(8,128)(2,1)S(1)}, u32[]{:S(2)}, u32[]{:S(2)}) %collective-permute-start.2) | collective-permute-done | bytes 128032 | tf_op jit(solution)/shard_map/ppermute | solution.py:48
  16.4 0.2 shard_map.56.refs_0_
  16.6 1.7 %collective-permute-start.7 = (bf16[40,3200]{1,0:T(8,128)(2,1)S(1)}, bf16[40,3200]{1,0:T(8,128)(2,1)S(1)}, u32[]{:S(2)}, u32[]{:S(2)}) collective-permute-start(bf16[40,3200]{1,0:T(8,128)(2,1)S(1)} %shard_map.56.refs_0_), channel_id=1, source_target_pairs={{0,4},{4,8},{8,12},{12,16},{16,20},{20,24},{24,28},{28,0},{1,5},{5... | collective-permute-start | bytes 768008 | tf_op jit(solution)/shard_map/ppermute | solution.py:30
  18.3 4.0 %collective-permute-start.3 = (bf16[40,3200]{1,0:T(8,128)(2,1)S(1)}, bf16[40,3200]{1,0:T(8,128)(2,1)S(1)}, u32[]{:S(2)}, u32[]{:S(2)}) collective-permute-start(bf16[40,3200]{1,0:T(8,128)(2,1)S(1)} %shard_map.56.refs_0_), channel_id=1, source_target_pairs={{0,28},{4,0},{8,4},{12,8},{16,12},{20,16},{24,20},{28,24},{1,29},{... | collective-permute-start | bytes 768008 | tf_op jit(solution)/shard_map/ppermute | solution.py:26
  22.4 5.2 %collective-permute-done.7.refs_1_ = bf16[40,3200]{1,0:T(8,128)(2,1)S(1)} collective-permute-done((bf16[40,3200]{1,0:T(8,128)(2,1)S(1)}, bf16[40,3200]{1,0:T(8,128)(2,1)S(1)}, u32[]{:S(2)}, u32[]{:S(2)}) %collective-permute-start.7) | collective-permute-done | bytes 256032 | tf_op jit(solution)/shard_map/ppermute | solution.py:30
  27.6 0.4 shard_map.57
  28.0 2.7 %collective-permute-start.5 = (bf16[40,3200]{1,0:T(8,128)(2,1)S(1)}, bf16[40,3200]{1,0:T(8,128)(2,1)S(1)}, u32[]{:S(2)}, u32[]{:S(2)}) collective-permute-start(bf16[40,3200]{1,0:T(8,128)(2,1)S(1)} %collective-permute-done.3.refs_0_), channel_id=1, source_target_pairs={{0,28},{4,0},{8,4},{12,8},{16,12},{20,16},{24,20},{28,24},{1,29},{... | collective-permute-start | bytes 768008 | tf_op jit(solution)/shard_map/ppermute | solution.py:26
  30.8 0.1 collective-permute-start.11
  30.9 0.2 shard_map.59
  31.2 0.8 %fusion = f32[160,1024]{1,0:T(8,128)S(1)} fusion(bf16[160,1600]{1,0:T(8,128)(2,1)S(1)} %get-tuple-element.44, bf16[1600,1024]{1,0:T(8,128)(2,1)S(1)} %shard_map.57), kind=kOutput, calls=%fused_computation.5 | convolution fusion | flops 524288000 | bytes 4444160 | tf_op jit(solution)/shard_map/dot_general | solution.py:238
  32.0 0.8 %convolution_add_fusion.2.refs_0_.refs_1_.refs_2_.refs_3_ = f32[160,1024]{1,0:T(8,128)S(1)} fusion(f32[160,1024]{1,0:T(8,128)S(1)} %fusion, bf16[160,1600]{1,0:T(8,128)(2,1)S(1)} %get-tuple-element.43, bf16[1600,1024]{1,0:T(8,128)(2,1)S(1)} %bitcast.26), kind=kOutput, calls=%fused_computation.2 | convolution fusion | flops 524451840 | bytes 5099520 | tf_op jit(solution)/shard_map/dot_general | solution.py:237
  32.8 1.9 %collective-permute-done.8.refs_1_ = bf16[40,3200]{1,0:T(8,128)(2,1)S(1)} collective-permute-done((bf16[40,3200]{1,0:T(8,128)(2,1)S(1)}, bf16[40,3200]{1,0:T(8,128)(2,1)S(1)}, u32[]{:S(2)}, u32[]{:S(2)}) %collective-permute-start.8) | collective-permute-done | bytes 256032 | tf_op jit(solution)/shard_map/ppermute | solution.py:30
  34.7 3.3 %collective-permute-start.6 = (bf16[40,3200]{1,0:T(8,128)(2,1)S(1)}, bf16[40,3200]{1,0:T(8,128)(2,1)S(1)}, u32[]{:S(2)}, u32[]{:S(2)}) collective-permute-start(bf16[40,3200]{1,0:T(8,128)(2,1)S(1)} %collective-permute-done.5.refs_0_), channel_id=1, source_target_pairs={{0,28},{4,0},{8,4},{12,8},{16,12},{20,16},{24,20},{28,24},{1,29},{... | collective-permute-start | bytes 768008 | tf_op jit(solution)/shard_map/ppermute | solution.py:26
  38.1 1.9 %collective-permute-done.11.refs_0_ = bf16[80,3200]{1,0:T(8,128)(2,1)S(1)} collective-permute-done((bf16[80,3200]{1,0:T(8,128)(2,1)S(1)}, bf16[80,3200]{1,0:T(8,128)(2,1)S(1)}, u32[]{:S(2)}, u32[]{:S(2)}) %collective-permute-start.11) | collective-permute-done | bytes 512032 | tf_op jit(solution)/shard_map/ppermute | solution.py:40
  40.0 0.3 collective-permute-start.13
  40.3 0.2 shard_map.61
  40.6 0.8 %fusion.1 = f32[160,1024]{1,0:T(8,128)S(1)} fusion(bf16[160,1600]{1,0:T(8,128)(2,1)S(1)} %get-tuple-element.50, bf16[1600,1024]{1,0:T(8,128)(2,1)S(1)} %shard_map.57), kind=kOutput, calls=%fused_computation.6 | convolution fusion | flops 524288000 | bytes 4444160 | tf_op jit(solution)/shard_map/dot_general | solution.py:238
  41.3 0.8 %convolution_add_fusion.1.refs_4_.refs_5_.refs_6_.refs_7_.refs_1_ = f32[160,1024]{1,0:T(8,128)S(1)} fusion(f32[160,1024]{1,0:T(8,128)S(1)} %fusion.1, bf16[160,1600]{1,0:T(8,128)(2,1)S(1)} %get-tuple-element.49, bf16[1600,1024]{1,0:T(8,128)(2,1)S(1)} %bitcast.27), kind=kOutput, calls=%fused_computation.1 | convolution fusion | flops 524451840 | bytes 5099520 | tf_op jit(solution)/shard_map/dot_general | solution.py:237
  42.3 0.3 collective-permute-start.12
  42.6 2.5 %collective-permute-start.15 = (bf16[80,3200]{1,0:T(8,128)(2,1)S(1)}, bf16[80,3200]{1,0:T(8,128)(2,1)S(1)}, u32[]{:S(2)}, u32[]{:S(2)}) collective-permute-start(bf16[80,3200]{1,0:T(8,128)(2,1)S(1)} %get-tuple-element.55.refs_1_), channel_id=1, source_target_pairs={{0,32},{1,97},{32,0},{33,65},{64,96},{65,33},{96,64},{97,1},{2,34}... | collective-permute-start | bytes 1536008 | tf_op jit(solution)/shard_map/ppermute | solution.py:40
  45.1 4.0 %collective-permute-done.13.refs_0_ = bf16[80,3200]{1,0:T(8,128)(2,1)S(1)} collective-permute-done((bf16[80,3200]{1,0:T(8,128)(2,1)S(1)}, bf16[80,3200]{1,0:T(8,128)(2,1)S(1)}, u32[]{:S(2)}, u32[]{:S(2)}) %collective-permute-start.13) | collective-permute-done | bytes 512032 | tf_op jit(solution)/shard_map/ppermute | solution.py:40
  49.1 0.2 shard_map.64
  49.4 0.8 %fusion.2 = f32[160,1024]{1,0:T(8,128)S(1)} fusion(bf16[160,1600]{1,0:T(8,128)(2,1)S(1)} %get-tuple-element.57, bf16[1600,1024]{1,0:T(8,128)(2,1)S(1)} %shard_map.57), kind=kOutput, calls=%fused_computation.7 | convolution fusion | flops 524288000 | bytes 4444160 | tf_op jit(solution)/shard_map/dot_general | solution.py:238
  50.2 0.8 %convolution_add_fusion.refs_0_.refs_1_.refs_2_.refs_3_ = f32[160,1024]{1,0:T(8,128)S(1)} fusion(f32[160,1024]{1,0:T(8,128)S(1)} %fusion.2, bf16[160,1600]{1,0:T(8,128)(2,1)S(1)} %get-tuple-element.56, bf16[1600,1024]{1,0:T(8,128)(2,1)S(1)} %bitcast.28), kind=kOutput, calls=%fused_computation | convolution fusion | flops 524451840 | bytes 5099520 | tf_op jit(solution)/shard_map/dot_general | solution.py:237
  51.0 0.4 collective-permute-start.14
  51.4 3.2 %collective-permute-done.15.refs_0_ = bf16[80,3200]{1,0:T(8,128)(2,1)S(1)} collective-permute-done((bf16[80,3200]{1,0:T(8,128)(2,1)S(1)}, bf16[80,3200]{1,0:T(8,128)(2,1)S(1)}, u32[]{:S(2)}, u32[]{:S(2)}) %collective-permute-start.15) | collective-permute-done | bytes 512032 | tf_op jit(solution)/shard_map/ppermute | solution.py:40
  54.6 0.2 shard_map.66
  54.8 0.6 fusion.3
  55.5 0.7 %convolution_add_fusion.3.refs_0_.refs_1_.refs_2_.refs_3_ = f32[120,1024]{1,0:T(8,128)S(1)} fusion(f32[120,1024]{1,0:T(8,128)S(1)} %fusion.3, bf16[120,1600]{1,0:T(8,128)(2,1)S(1)} %get-tuple-element.59, bf16[1600,1024]{1,0:T(8,128)(2,1)S(1)} %bitcast.29), kind=kOutput, calls=%fused_computation.3 | convolution fusion | flops 393338880 | bytes 4643840 | tf_op jit(solution)/shard_map/dot_general | solution.py:237
  56.2 0.1 collective-permute-start.17
  56.3 1.2 %collective-permute-done.14.refs_0_ = bf16[40,3200]{1,0:T(8,128)(2,1)S(1)} collective-permute-done((bf16[40,3200]{1,0:T(8,128)(2,1)S(1)}, bf16[40,3200]{1,0:T(8,128)(2,1)S(1)}, u32[]{:S(2)}, u32[]{:S(2)}) %collective-permute-start.14) | collective-permute-done | bytes 256032 | tf_op jit(solution)/shard_map/ppermute | solution.py:40
  57.5 0.1 shard_map.68
  57.6 0.7 %fusion.4 = f32[40,1024]{1,0:T(8,128)S(1)} fusion(bf16[40,1600]{1,0:T(8,128)(2,1)S(1)} %get-tuple-element.63, bf16[1600,1024]{1,0:T(8,128)(2,1)S(1)} %shard_map.57), kind=kOutput, calls=%fused_computation.9 | convolution fusion | flops 131072000 | bytes 3568640 | tf_op jit(solution)/shard_map/dot_general | solution.py:238
  58.3 0.4 collective-permute-start.18
  58.6 0.7 %convolution_add_fusion.4.refs_0_.refs_4_ = f32[40,1024]{1,0:T(8,128)S(1)} fusion(f32[40,1024]{1,0:T(8,128)S(1)} %fusion.4, bf16[40,1600]{1,0:T(8,128)(2,1)S(1)} %get-tuple-element.62, bf16[1600,1024]{1,0:T(8,128)(2,1)S(1)} %bitcast.30), kind=kOutput, calls=%fused_computation.4 | convolution fusion | flops 131112960 | bytes 3732480 | tf_op jit(solution)/shard_map/dot_general | solution.py:237
  59.4 1.3 %collective-permute-start.19 = (f16[20,1024]{1,0:T(8,128)(2,1)S(1)}, f16[20,1024]{1,0:T(8,128)(2,1)S(1)}, u32[]{:S(2)}, u32[]{:S(2)}) collective-permute-start(f16[20,1024]{1,0:T(8,128)(2,1)S(1)} %convert_element_type.27), channel_id=1, source_target_pairs={{0,2},{2,0},{1,3},{3,1},{4,6},{6,4},{5,7},{7,5},{8,10},{10,8},{9,1... | collective-permute-start | bytes 122888 | tf_op jit(solution)/shard_map/ppermute | solution.py:56
  60.7 0.1 collective-permute-done.17
  60.8 0.1 shard_map.70.row_ref
  60.9 1.8 %collective-permute-done.19 = f16[20,1024]{1,0:T(8,128)(2,1)S(1)} collective-permute-done((f16[20,1024]{1,0:T(8,128)(2,1)S(1)}, f16[20,1024]{1,0:T(8,128)(2,1)S(1)}, u32[]{:S(2)}, u32[]{:S(2)}) %collective-permute-start.19) | collective-permute-done | bytes 40992 | tf_op jit(solution)/shard_map/ppermute | solution.py:56
  62.8 1.3 %shard_map.71 = f32[320,1024]{1,0:T(8,128)} custom-call(f32[320,1024]{1,0:T(8,128)S(1)} %copy-done, f32[320,128]{1,0:T(8,128)S(1)} %shard_map.70.row_ref, s32[2,1024]{1,0:T(2,128)S(1)} %bitcast.23, f32[160,1024]{1,0:T(8,128)S(1)} %convolution_add_fusion.2.refs_0_.refs_1_.refs_2_.refs_3_, ...), custom_call_target="tpu_custom_call" | custom-call | tf_op jit(solution)/shard_map/pallas_call | solution.py:173
  (36 shorter events, 0.5 us)
Async XLA Ops:
  0.0 4.4 %collective-permute-start = (bf16[20,8,200]{2,1,0:T(8,128)(2,1)}, bf16[20,8,200]{2,1,0:T(8,128)(2,1)S(1)}, u32[]{:S(2)}, u32[]{:S(2)}) collective-permute-start(bf16[20,8,200]{2,1,0:T(8,128)(2,1)} %param.5), channel_id=1, source_target_pairs={{0,1},{1,0},{2,3},{3,2},{4,5},{5,4},{6,7},{7,6},{8,9},{9,8},{10,11... | collective-permute-start | bytes 192008 | tf_op jit(solution)/shard_map/ppermute | solution.py:52
  4.4 23.2 %collective-permute-start.4 = (bf16[1600,1024]{1,0:T(8,128)(2,1)}, bf16[1600,1024]{1,0:T(8,128)(2,1)S(1)}, u32[]{:S(2)}, u32[]{:S(2)}) collective-permute-start(bf16[1600,1024]{1,0:T(8,128)(2,1)} %bitcast.25), channel_id=1, source_target_pairs={{0,1},{1,0},{2,3},{3,2},{4,5},{5,4},{6,7},{7,6},{8,9},{9,8},{10,11... | collective-permute-start | bytes 9830408 | tf_op jit(solution)/shard_map/ppermute | solution.py:52
  4.9 8.4 %collective-permute-start.1 = (bf16[40,1600]{1,0:T(8,128)(2,1)S(1)}, bf16[40,1600]{1,0:T(8,128)(2,1)S(1)}, u32[]{:S(2)}, u32[]{:S(2)}) collective-permute-start(bf16[40,1600]{1,0:T(8,128)(2,1)S(1)} %shard_map.55), channel_id=1, source_target_pairs={{0,128},{1,192},{32,160},{33,224},{64,129},{65,193},{96,161},{97,2... | collective-permute-start | bytes 384008 | tf_op jit(solution)/shard_map/ppermute | solution.py:48
  8.6 7.8 %collective-permute-start.2 = (bf16[40,1600]{1,0:T(8,128)(2,1)S(1)}, bf16[40,1600]{1,0:T(8,128)(2,1)S(1)}, u32[]{:S(2)}, u32[]{:S(2)}) collective-permute-start(bf16[40,1600]{1,0:T(8,128)(2,1)S(1)} %shard_map.55), channel_id=1, source_target_pairs={{0,0},{1,64},{32,32},{33,96},{64,1},{65,65},{96,33},{97,97},{128,1... | collective-permute-start | bytes 384008 | tf_op jit(solution)/shard_map/ppermute | solution.py:48
  16.6 11.0 %collective-permute-start.7 = (bf16[40,3200]{1,0:T(8,128)(2,1)S(1)}, bf16[40,3200]{1,0:T(8,128)(2,1)S(1)}, u32[]{:S(2)}, u32[]{:S(2)}) collective-permute-start(bf16[40,3200]{1,0:T(8,128)(2,1)S(1)} %shard_map.56.refs_0_), channel_id=1, source_target_pairs={{0,4},{4,8},{8,12},{12,16},{16,20},{20,24},{24,28},{28,0},{1,5},{5... | collective-permute-start | bytes 768008 | tf_op jit(solution)/shard_map/ppermute | solution.py:30
  18.3 9.7 %collective-permute-start.3 = (bf16[40,3200]{1,0:T(8,128)(2,1)S(1)}, bf16[40,3200]{1,0:T(8,128)(2,1)S(1)}, u32[]{:S(2)}, u32[]{:S(2)}) collective-permute-start(bf16[40,3200]{1,0:T(8,128)(2,1)S(1)} %shard_map.56.refs_0_), channel_id=1, source_target_pairs={{0,28},{4,0},{8,4},{12,8},{16,12},{20,16},{24,20},{28,24},{1,29},{... | collective-permute-start | bytes 768008 | tf_op jit(solution)/shard_map/ppermute | solution.py:26
  22.4 8.6 %collective-permute-start.9 = (bf16[40,3200]{1,0:T(8,128)(2,1)S(1)}, bf16[40,3200]{1,0:T(8,128)(2,1)S(1)}, u32[]{:S(2)}, u32[]{:S(2)}) collective-permute-start(bf16[40,3200]{1,0:T(8,128)(2,1)S(1)} %shard_map.56.refs_0_), channel_id=1, source_target_pairs={{0,32},{1,97},{32,0},{33,65},{64,96},{65,33},{96,64},{97,1},{2,34}... | collective-permute-start | bytes 768008 | tf_op jit(solution)/shard_map/ppermute | solution.py:40
  27.6 7.1 %collective-permute-start.8 = (bf16[40,3200]{1,0:T(8,128)(2,1)S(1)}, bf16[40,3200]{1,0:T(8,128)(2,1)S(1)}, u32[]{:S(2)}, u32[]{:S(2)}) collective-permute-start(bf16[40,3200]{1,0:T(8,128)(2,1)S(1)} %collective-permute-done.7.refs_1_), channel_id=1, source_target_pairs={{0,4},{4,8},{8,12},{12,16},{16,20},{20,24},{24,28},{28,0},{1,5},{5... | collective-permute-start | bytes 768008 | tf_op jit(solution)/shard_map/ppermute | solution.py:30
  28.0 4.0 %copy-start.3 = (bf16[8,200,1024]{2,1,0:T(8,128)(2,1)S(1)}, bf16[8,200,1024]{2,1,0:T(8,128)(2,1)}, u32[]{:S(2)}) copy-start(bf16[8,200,1024]{2,1,0:T(8,128)(2,1)} %param.6) | copy-start | bytes 9830404
  28.0 6.7 %collective-permute-start.5 = (bf16[40,3200]{1,0:T(8,128)(2,1)S(1)}, bf16[40,3200]{1,0:T(8,128)(2,1)S(1)}, u32[]{:S(2)}, u32[]{:S(2)}) collective-permute-start(bf16[40,3200]{1,0:T(8,128)(2,1)S(1)} %collective-permute-done.3.refs_0_), channel_id=1, source_target_pairs={{0,28},{4,0},{8,4},{12,8},{16,12},{20,16},{24,20},{28,24},{1,29},{... | collective-permute-start | bytes 768008 | tf_op jit(solution)/shard_map/ppermute | solution.py:26
  30.8 9.2 %collective-permute-start.11 = (bf16[80,3200]{1,0:T(8,128)(2,1)S(1)}, bf16[80,3200]{1,0:T(8,128)(2,1)S(1)}, u32[]{:S(2)}, u32[]{:S(2)}) collective-permute-start(bf16[80,3200]{1,0:T(8,128)(2,1)S(1)} %shard_map.58.refs_2_), channel_id=1, source_target_pairs={{0,32},{1,97},{32,0},{33,65},{64,96},{65,33},{96,64},{97,1},{2,34}... | collective-permute-start | bytes 1536008 | tf_op jit(solution)/shard_map/ppermute | solution.py:40
  34.7 7.5 %collective-permute-start.10 = (bf16[40,3200]{1,0:T(8,128)(2,1)S(1)}, bf16[40,3200]{1,0:T(8,128)(2,1)S(1)}, u32[]{:S(2)}, u32[]{:S(2)}) collective-permute-start(bf16[40,3200]{1,0:T(8,128)(2,1)S(1)} %collective-permute-done.8.refs_1_), channel_id=1, source_target_pairs={{0,4},{4,8},{8,12},{12,16},{16,20},{20,24},{24,28},{28,0},{1,5},{5... | collective-permute-start | bytes 768008 | tf_op jit(solution)/shard_map/ppermute | solution.py:30
  34.7 7.5 %collective-permute-start.6 = (bf16[40,3200]{1,0:T(8,128)(2,1)S(1)}, bf16[40,3200]{1,0:T(8,128)(2,1)S(1)}, u32[]{:S(2)}, u32[]{:S(2)}) collective-permute-start(bf16[40,3200]{1,0:T(8,128)(2,1)S(1)} %collective-permute-done.5.refs_0_), channel_id=1, source_target_pairs={{0,28},{4,0},{8,4},{12,8},{16,12},{20,16},{24,20},{28,24},{1,29},{... | collective-permute-start | bytes 768008 | tf_op jit(solution)/shard_map/ppermute | solution.py:26
  40.0 9.1 %collective-permute-start.13 = (bf16[80,3200]{1,0:T(8,128)(2,1)S(1)}, bf16[80,3200]{1,0:T(8,128)(2,1)S(1)}, u32[]{:S(2)}, u32[]{:S(2)}) collective-permute-start(bf16[80,3200]{1,0:T(8,128)(2,1)S(1)} %shard_map.60.refs_1_), channel_id=1, source_target_pairs={{0,32},{1,97},{32,0},{33,65},{64,96},{65,33},{96,64},{97,1},{2,34}... | collective-permute-start | bytes 1536008 | tf_op jit(solution)/shard_map/ppermute | solution.py:40
  42.3 8.7 %collective-permute-start.12 = (bf16[40,3200]{1,0:T(8,128)(2,1)S(1)}, bf16[40,3200]{1,0:T(8,128)(2,1)S(1)}, u32[]{:S(2)}, u32[]{:S(2)}) collective-permute-start(bf16[40,3200]{1,0:T(8,128)(2,1)S(1)} %get-tuple-element.54), channel_id=1, source_target_pairs={{0,28},{1,5},{4,0},{5,9},{8,4},{9,13},{12,8},{13,17},{16,12},{17,2... | collective-permute-start | bytes 768008 | tf_op jit(solution)/shard_map/ppermute | solution.py:35
  42.6 12.0 %collective-permute-start.15 = (bf16[80,3200]{1,0:T(8,128)(2,1)S(1)}, bf16[80,3200]{1,0:T(8,128)(2,1)S(1)}, u32[]{:S(2)}, u32[]{:S(2)}) collective-permute-start(bf16[80,3200]{1,0:T(8,128)(2,1)S(1)} %get-tuple-element.55.refs_1_), channel_id=1, source_target_pairs={{0,32},{1,97},{32,0},{33,65},{64,96},{65,33},{96,64},{97,1},{2,34}... | collective-permute-start | bytes 1536008 | tf_op jit(solution)/shard_map/ppermute | solution.py:40
  45.1 15.5 %collective-permute-start.16 = (f16[160,1024]{1,0:T(8,128)(2,1)S(1)}, f16[160,1024]{1,0:T(8,128)(2,1)S(1)}, u32[]{:S(2)}, u32[]{:S(2)}) collective-permute-start(f16[160,1024]{1,0:T(8,128)(2,1)S(1)} %convert_element_type.24), channel_id=1, source_target_pairs={{0,2},{2,0},{1,3},{3,1},{4,6},{6,4},{5,7},{7,5},{8,10},{10,8},{9,1... | collective-permute-start | bytes 983048 | tf_op jit(solution)/shard_map/ppermute | solution.py:56
  51.0 6.5 %collective-permute-start.14 = (bf16[40,3200]{1,0:T(8,128)(2,1)S(1)}, bf16[40,3200]{1,0:T(8,128)(2,1)S(1)}, u32[]{:S(2)}, u32[]{:S(2)}) collective-permute-start(bf16[40,3200]{1,0:T(8,128)(2,1)S(1)} %collective-permute-done.12.refs_1_), channel_id=1, source_target_pairs={{0,32},{1,97},{32,0},{33,65},{64,96},{65,33},{96,64},{97,1},{2,34}... | collective-permute-start | bytes 768008 | tf_op jit(solution)/shard_map/ppermute | solution.py:40
  56.2 4.6 %collective-permute-start.17 = (f16[80,1024]{1,0:T(8,128)(2,1)S(1)}, f16[80,1024]{1,0:T(8,128)(2,1)S(1)}, u32[]{:S(2)}, u32[]{:S(2)}) collective-permute-start(f16[80,1024]{1,0:T(8,128)(2,1)S(1)} %convert_element_type.25), channel_id=1, source_target_pairs={{0,2},{2,0},{1,3},{3,1},{4,6},{6,4},{5,7},{7,5},{8,10},{10,8},{9,1... | collective-permute-start | bytes 491528 | tf_op jit(solution)/shard_map/ppermute | solution.py:56
  58.2 2.6 %copy-start.2 = (s32[320,2]{0,1:T(2,128)S(1)}, s32[320,2]{0,1:T(2,128)}, u32[]{:S(2)}) copy-start(s32[320,2]{0,1:T(2,128)} %param.8) | copy-start | bytes 7684
  58.3 4.5 %copy-start = (f32[320,1024]{1,0:T(8,128)S(1)}, f32[320,1024]{1,0:T(8,128)}, u32[]{:S(2)}) copy-start(f32[320,1024]{1,0:T(8,128)} %in_ref.1) | copy-start | bytes 3932164
  58.3 4.5 %copy-start.1 = (s32[1024,2]{0,1:T(2,128)S(1)}, s32[1024,2]{0,1:T(2,128)}, u32[]{:S(2)}) copy-start(s32[1024,2]{0,1:T(2,128)} %param.9) | copy-start | bytes 24580
  58.3 4.5 %collective-permute-start.18 = (f16[60,1024]{1,0:T(8,128)(2,1)S(1)}, f16[60,1024]{1,0:T(8,128)(2,1)S(1)}, u32[]{:S(2)}, u32[]{:S(2)}) collective-permute-start(f16[60,1024]{1,0:T(8,128)(2,1)S(1)} %convert_element_type.26), channel_id=1, source_target_pairs={{0,2},{2,0},{1,3},{3,1},{4,6},{6,4},{5,7},{7,5},{8,10},{10,8},{9,1... | collective-permute-start | bytes 368648 | tf_op jit(solution)/shard_map/ppermute | solution.py:56
  59.4 3.4 %collective-permute-start.19 = (f16[20,1024]{1,0:T(8,128)(2,1)S(1)}, f16[20,1024]{1,0:T(8,128)(2,1)S(1)}, u32[]{:S(2)}, u32[]{:S(2)}) collective-permute-start(f16[20,1024]{1,0:T(8,128)(2,1)S(1)} %convert_element_type.27), channel_id=1, source_target_pairs={{0,2},{2,0},{1,3},{3,1},{4,6},{6,4},{5,7},{7,5},{8,10},{10,8},{9,1... | collective-permute-start | bytes 122888 | tf_op jit(solution)/shard_map/ppermute | solution.py:56

commit v6 on v5

--- a/solution.py
+++ b/solution.py
@@ -135,7 +135,7 @@
 
 
 def last_kernel(in_ref, row_ref, col_ref, *refs):
-    m0, m1, m2, m3, m4, b0, b2, b3, b4, out_ref, total, done, sems = refs
+    m0, m1, m2, m3, m4, b0, b3, b4, out_ref, total, done, sems = refs
     here, z = lax.axis_index("y") % 2, lax.axis_index("z")
     there = 1 - here
 
@@ -154,13 +154,13 @@
             copies[-1].start()
 
     put(0, m0, 0, b0, 0)
-    for step, h, at, b, start in ((1, m0, 80, b0, 40), (2, m1, 80, b0, 120), (3, m2, 80, b2, 40)):
+    for step, h, at, b, start in ((1, m0, 80, b0, 40), (2, m1, 80, b0, 120), (3, m2, 80, b3, 40)):
         put(step, h, at, b, start)
         put(-step, h, at + 40, b, start + 20)
-    put(4, m3, 80, b3, 40)
+    put(4, m3, 80, b3, 120)
     leave(here)
     put(0, m0, 40, b0, 20)
-    for step, s, b, start in ((1, m1, b0, 80), (2, m2, b2, 0), (3, m3, b3, 0)):
+    for step, s, b, start in ((1, m1, b0, 80), (2, m2, b3, 0), (3, m3, b3, 80)):
         put(step, s, 0, b, start)
         put(-step, s, 40, b, start + 20)
     put(4, m4, 0, b4, 0)
@@ -258,19 +258,17 @@
     swap3 = swap(beside)
     b0 = trade(goes0)
     m2 = dot(swap2, beside)
-    goes2 = low((m2, 20), (m2, 60), (m2, 100), (m2, 140))
-    opposite, m2, goes2 = tie((opposite, m2, goes2))
+    opposite, m2 = tie((opposite, m2))
     swap4 = swap(opposite)
-    b2 = trade(goes2)
     m3 = dot(swap3, opposite)
-    goes3 = low((m3, 20), (m3, 60), (m3, 100))
+    goes3 = low((m2, 20), (m2, 60), (m2, 100), (m2, 140), (m3, 20), (m3, 60), (m3, 100))
     swap4, m3, goes3 = tie((swap4, m3, goes3))
     b3 = trade(goes3)
     m4 = dot(swap4)
     goes4, pair_list, ab_list = tie((low((m4, 20)), pair_list.T, ab_list.T))
     b4 = trade(goes4)
     row = row_scale(pair_list)
-    back = [b.astype(F32) for b in (b0, b2, b3, b4)]
+    back = [b.astype(F32) for b in (b0, b3, b4)]
     return finish(residual_in, row, ab_list, (m0, m1, m2, m3, m4, *back))
 
 

time: 64.8 us -> 66.6 us (1.028)
  waiting for transfers between devices: 25.1 us -> 26.8 us
    ppermute x4 -> x3, waiting for transfers between devices: 1.89 us -> 3.65 us  [trade(): return lax.ppermute(x, 'xl', turn(XL, 1))]
    ppermute x4 -> x3, starting transfers between devices: 1.73 us -> 1.63 us  [trade(): return lax.ppermute(x, 'xl', turn(XL, 1))]
  transfers between devices with their start and end apart: 20 -> 19, of which waited for: 11 -> 10; matrix products, arithmetic and copies ran while one was open for 13% -> 13% of each run, Pallas kernels for 3% -> 3%
where the time goes in v6:
time: 66.6 us; the launch traced here: 65.9 us
  waiting for transfers between devices  26.8 us (40%)
  starting transfers between devices  26.7 us (40%)
  matrix products  7.27 us (11%)
  Pallas kernels  3.33 us (5%)
  local copies, waits for them, and re-layouts  1.08 us (2%)
    ppermute x5, waiting for transfers between devices, swap(): return lax.ppermute(x, ('y', 'core'), route)  10.3 us
    ppermute x3, starting transfers between devices, up(): return lax.ppermute(x, 'z', turn(Z, -1))  10.2 us
    ppermute x3, waiting for transfers between devices, down(): return lax.ppermute(x, 'z', turn(Z, 1))  7.14 us
    ppermute x2, starting transfers between devices, spread(): return lax.ppermute(x, ('xh', 'y', 'core'), route)  5.96 us
    ppermute x2, waiting for transfers between devices, spread(): return lax.ppermute(x, ('xh', 'y', 'core'), route)  5.62 us
    ppermute x3, waiting for transfers between devices, trade(): return lax.ppermute(x, 'xl', turn(XL, 1))  3.65 us
    dot_general x5, matrix products, dot(): total = jnp.dot(left, own, preferred_element_type=F32)  3.64 us
    dot_general x5, matrix products, dot(): return total + jnp.dot(right, second, preferred_element_type=F32)  3.63 us
  transfers between devices with their start and end apart: 19, of which 10 were waited for; matrix products, arithmetic and copies ran while one was open for 13% of the time, Pallas kernels for 3%

profile of v6, /device:TPU:1, one launch (start us, length us, event | category | flops | bytes accessed | tf_op | source)
XLA Modules:
  0.0 65.9 jit_solution(11685001914717597651)
XLA Ops:
  0.0 3.2 %collective-permute-start = (bf16[20,8,200]{2,1,0:T(8,128)(2,1)}, bf16[20,8,200]{2,1,0:T(8,128)(2,1)S(1)}, u32[]{:S(2)}, u32[]{:S(2)}) collective-permute-start(bf16[20,8,200]{2,1,0:T(8,128)(2,1)} %param.5), channel_id=1, source_target_pairs={{0,1},{1,0},{2,3},{3,2},{4,5},{5,4},{6,7},{7,6},{8,9},{9,8},{10,11... | collective-permute-start | bytes 192008 | tf_op jit(solution)/shard_map/ppermute | solution.py:52
  3.2 1.1 %reshape.6.mine_ref = bf16[20,1600]{1,0:T(8,128)(2,1)S(1)} reshape(bf16[20,8,200]{2,1,0:T(8,128)(2,1)} %param.5) | data formatting | bytes 128000 | tf_op jit(solution)/shard_map/reshape | solution.py:229
  4.3 0.1 collective-permute-done.mate_ref
  4.4 0.4 collective-permute-start.4
  4.7 0.1 shard_map.55
  4.9 3.8 %collective-permute-start.1 = (bf16[40,1600]{1,0:T(8,128)(2,1)S(1)}, bf16[40,1600]{1,0:T(8,128)(2,1)S(1)}, u32[]{:S(2)}, u32[]{:S(2)}) collective-permute-start(bf16[40,1600]{1,0:T(8,128)(2,1)S(1)} %shard_map.55), channel_id=1, source_target_pairs={{0,128},{1,192},{32,160},{33,224},{64,129},{65,193},{96,161},{97,2... | collective-permute-start | bytes 384008 | tf_op jit(solution)/shard_map/ppermute | solution.py:48
  8.6 2.2 %collective-permute-start.2 = (bf16[40,1600]{1,0:T(8,128)(2,1)S(1)}, bf16[40,1600]{1,0:T(8,128)(2,1)S(1)}, u32[]{:S(2)}, u32[]{:S(2)}) collective-permute-start(bf16[40,1600]{1,0:T(8,128)(2,1)S(1)} %shard_map.55), channel_id=1, source_target_pairs={{0,0},{1,64},{32,32},{33,96},{64,1},{65,65},{96,33},{97,97},{128,1... | collective-permute-start | bytes 384008 | tf_op jit(solution)/shard_map/ppermute | solution.py:48
  10.8 2.4 %collective-permute-done.1.far_ref = bf16[40,1600]{1,0:T(8,128)(2,1)S(1)} collective-permute-done((bf16[40,1600]{1,0:T(8,128)(2,1)S(1)}, bf16[40,1600]{1,0:T(8,128)(2,1)S(1)}, u32[]{:S(2)}, u32[]{:S(2)}) %collective-permute-start.1) | collective-permute-done | bytes 128032 | tf_op jit(solution)/shard_map/ppermute | solution.py:48
  13.3 3.2 %collective-permute-done.2.near_ref = bf16[40,1600]{1,0:T(8,128)(2,1)S(1)} collective-permute-done((bf16[40,1600]{1,0:T(8,128)(2,1)S(1)}, bf16[40,1600]{1,0:T(8,128)(2,1)S(1)}, u32[]{:S(2)}, u32[]{:S(2)}) %collective-permute-start.2) | collective-permute-done | bytes 128032 | tf_op jit(solution)/shard_map/ppermute | solution.py:48
  16.4 0.2 shard_map.56.refs_0_
  16.6 1.7 %collective-permute-start.7 = (bf16[40,3200]{1,0:T(8,128)(2,1)S(1)}, bf16[40,3200]{1,0:T(8,128)(2,1)S(1)}, u32[]{:S(2)}, u32[]{:S(2)}) collective-permute-start(bf16[40,3200]{1,0:T(8,128)(2,1)S(1)} %shard_map.56.refs_0_), channel_id=1, source_target_pairs={{0,4},{4,8},{8,12},{12,16},{16,20},{20,24},{24,28},{28,0},{1,5},{5... | collective-permute-start | bytes 768008 | tf_op jit(solution)/shard_map/ppermute | solution.py:30
  18.3 4.0 %collective-permute-start.3 = (bf16[40,3200]{1,0:T(8,128)(2,1)S(1)}, bf16[40,3200]{1,0:T(8,128)(2,1)S(1)}, u32[]{:S(2)}, u32[]{:S(2)}) collective-permute-start(bf16[40,3200]{1,0:T(8,128)(2,1)S(1)} %shard_map.56.refs_0_), channel_id=1, source_target_pairs={{0,28},{4,0},{8,4},{12,8},{16,12},{20,16},{24,20},{28,24},{1,29},{... | collective-permute-start | bytes 768008 | tf_op jit(solution)/shard_map/ppermute | solution.py:26
  22.4 5.2 %collective-permute-done.7.refs_1_ = bf16[40,3200]{1,0:T(8,128)(2,1)S(1)} collective-permute-done((bf16[40,3200]{1,0:T(8,128)(2,1)S(1)}, bf16[40,3200]{1,0:T(8,128)(2,1)S(1)}, u32[]{:S(2)}, u32[]{:S(2)}) %collective-permute-start.7) | collective-permute-done | bytes 256032 | tf_op jit(solution)/shard_map/ppermute | solution.py:30
  27.6 0.4 shard_map.57
  28.0 2.7 %collective-permute-start.5 = (bf16[40,3200]{1,0:T(8,128)(2,1)S(1)}, bf16[40,3200]{1,0:T(8,128)(2,1)S(1)}, u32[]{:S(2)}, u32[]{:S(2)}) collective-permute-start(bf16[40,3200]{1,0:T(8,128)(2,1)S(1)} %collective-permute-done.3.refs_0_), channel_id=1, source_target_pairs={{0,28},{4,0},{8,4},{12,8},{16,12},{20,16},{24,20},{28,24},{1,29},{... | collective-permute-start | bytes 768008 | tf_op jit(solution)/shard_map/ppermute | solution.py:26
  30.8 0.1 collective-permute-start.11
  30.9 0.2 shard_map.59
  31.2 0.8 %fusion = f32[160,1024]{1,0:T(8,128)S(1)} fusion(bf16[160,1600]{1,0:T(8,128)(2,1)S(1)} %get-tuple-element.43, bf16[1600,1024]{1,0:T(8,128)(2,1)S(1)} %shard_map.57), kind=kOutput, calls=%fused_computation.5 | convolution fusion | flops 524288000 | bytes 4444160 | tf_op jit(solution)/shard_map/dot_general | solution.py:238
  32.0 0.8 %convolution_add_fusion.2.refs_0_.refs_1_.refs_2_.refs_3_ = f32[160,1024]{1,0:T(8,128)S(1)} fusion(f32[160,1024]{1,0:T(8,128)S(1)} %fusion, bf16[160,1600]{1,0:T(8,128)(2,1)S(1)} %get-tuple-element.42, bf16[1600,1024]{1,0:T(8,128)(2,1)S(1)} %bitcast.26), kind=kOutput, calls=%fused_computation.2 | convolution fusion | flops 524451840 | bytes 5099520 | tf_op jit(solution)/shard_map/dot_general | solution.py:237
  32.8 1.9 %collective-permute-done.8.refs_1_ = bf16[40,3200]{1,0:T(8,128)(2,1)S(1)} collective-permute-done((bf16[40,3200]{1,0:T(8,128)(2,1)S(1)}, bf16[40,3200]{1,0:T(8,128)(2,1)S(1)}, u32[]{:S(2)}, u32[]{:S(2)}) %collective-permute-start.8) | collective-permute-done | bytes 256032 | tf_op jit(solution)/shard_map/ppermute | solution.py:30
  34.7 3.4 %collective-permute-start.6 = (bf16[40,3200]{1,0:T(8,128)(2,1)S(1)}, bf16[40,3200]{1,0:T(8,128)(2,1)S(1)}, u32[]{:S(2)}, u32[]{:S(2)}) collective-permute-start(bf16[40,3200]{1,0:T(8,128)(2,1)S(1)} %collective-permute-done.5.refs_0_), channel_id=1, source_target_pairs={{0,28},{4,0},{8,4},{12,8},{16,12},{20,16},{24,20},{28,24},{1,29},{... | collective-permute-start | bytes 768008 | tf_op jit(solution)/shard_map/ppermute | solution.py:26
  38.1 1.9 %collective-permute-done.11.refs_0_ = bf16[80,3200]{1,0:T(8,128)(2,1)S(1)} collective-permute-done((bf16[80,3200]{1,0:T(8,128)(2,1)S(1)}, bf16[80,3200]{1,0:T(8,128)(2,1)S(1)}, u32[]{:S(2)}, u32[]{:S(2)}) %collective-permute-start.11) | collective-permute-done | bytes 512032 | tf_op jit(solution)/shard_map/ppermute | solution.py:40
  40.0 0.3 collective-permute-start.13
  40.3 0.2 shard_map.61
  40.6 0.8 %fusion.1 = f32[160,1024]{1,0:T(8,128)S(1)} fusion(bf16[160,1600]{1,0:T(8,128)(2,1)S(1)} %get-tuple-element.49, bf16[1600,1024]{1,0:T(8,128)(2,1)S(1)} %shard_map.57), kind=kOutput, calls=%fused_computation.6 | convolution fusion | flops 524288000 | bytes 4444160 | tf_op jit(solution)/shard_map/dot_general | solution.py:238
  41.3 0.8 %convolution_add_fusion.1.refs_4_.refs_5_.refs_6_.refs_7_.refs_1_ = f32[160,1024]{1,0:T(8,128)S(1)} fusion(f32[160,1024]{1,0:T(8,128)S(1)} %fusion.1, bf16[160,1600]{1,0:T(8,128)(2,1)S(1)} %get-tuple-element.48, bf16[1600,1024]{1,0:T(8,128)(2,1)S(1)} %bitcast.27), kind=kOutput, calls=%fused_computation.1 | convolution fusion | flops 524451840 | bytes 5099520 | tf_op jit(solution)/shard_map/dot_general | solution.py:237
  42.1 0.1 shard_map.62
  42.2 0.1 shard_map.63
  42.3 0.3 collective-permute-start.12
  42.6 2.5 %collective-permute-start.15 = (bf16[80,3200]{1,0:T(8,128)(2,1)S(1)}, bf16[80,3200]{1,0:T(8,128)(2,1)S(1)}, u32[]{:S(2)}, u32[]{:S(2)}) collective-permute-start(bf16[80,3200]{1,0:T(8,128)(2,1)S(1)} %get-tuple-element.54.refs_1_), channel_id=1, source_target_pairs={{0,32},{1,97},{32,0},{33,65},{64,96},{65,33},{96,64},{97,1},{2,34}... | collective-permute-start | bytes 1536008 | tf_op jit(solution)/shard_map/ppermute | solution.py:40
  45.1 4.0 %collective-permute-done.13.refs_0_ = bf16[80,3200]{1,0:T(8,128)(2,1)S(1)} collective-permute-done((bf16[80,3200]{1,0:T(8,128)(2,1)S(1)}, bf16[80,3200]{1,0:T(8,128)(2,1)S(1)}, u32[]{:S(2)}, u32[]{:S(2)}) %collective-permute-start.13) | collective-permute-done | bytes 512032 | tf_op jit(solution)/shard_map/ppermute | solution.py:40
  49.1 0.2 shard_map.64
  49.4 0.8 %fusion.2 = f32[160,1024]{1,0:T(8,128)S(1)} fusion(bf16[160,1600]{1,0:T(8,128)(2,1)S(1)} %get-tuple-element.56, bf16[1600,1024]{1,0:T(8,128)(2,1)S(1)} %shard_map.57), kind=kOutput, calls=%fused_computation.7 | convolution fusion | flops 524288000 | bytes 4444160 | tf_op jit(solution)/shard_map/dot_general | solution.py:238
  50.2 0.8 %convolution_add_fusion.refs_0_.refs_1_.refs_2_.refs_3_ = f32[160,1024]{1,0:T(8,128)S(1)} fusion(f32[160,1024]{1,0:T(8,128)S(1)} %fusion.2, bf16[160,1600]{1,0:T(8,128)(2,1)S(1)} %get-tuple-element.55, bf16[1600,1024]{1,0:T(8,128)(2,1)S(1)} %bitcast.28), kind=kOutput, calls=%fused_computation | convolution fusion | flops 524451840 | bytes 5099520 | tf_op jit(solution)/shard_map/dot_general | solution.py:237
  50.9 0.4 collective-permute-start.14
  51.4 3.2 %collective-permute-done.15.refs_0_ = bf16[80,3200]{1,0:T(8,128)(2,1)S(1)} collective-permute-done((bf16[80,3200]{1,0:T(8,128)(2,1)S(1)}, bf16[80,3200]{1,0:T(8,128)(2,1)S(1)}, u32[]{:S(2)}, u32[]{:S(2)}) %collective-permute-start.15) | collective-permute-done | bytes 512032 | tf_op jit(solution)/shard_map/ppermute | solution.py:40
  54.6 0.2 shard_map.65
  54.8 0.6 fusion.3
  55.5 0.7 convolution_add_fusion.3.refs_4_.refs_5_.refs_6_.refs_3_
  56.2 1.2 %collective-permute-done.14.refs_0_ = bf16[40,3200]{1,0:T(8,128)(2,1)S(1)} collective-permute-done((bf16[40,3200]{1,0:T(8,128)(2,1)S(1)}, bf16[40,3200]{1,0:T(8,128)(2,1)S(1)}, u32[]{:S(2)}, u32[]{:S(2)}) %collective-permute-start.14) | collective-permute-done | bytes 256032 | tf_op jit(solution)/shard_map/ppermute | solution.py:40
  57.4 0.1 shard_map.67
  57.5 0.7 %fusion.4 = f32[40,1024]{1,0:T(8,128)S(1)} fusion(bf16[40,1600]{1,0:T(8,128)(2,1)S(1)} %get-tuple-element.63, bf16[1600,1024]{1,0:T(8,128)(2,1)S(1)} %shard_map.57), kind=kOutput, calls=%fused_computation.9 | convolution fusion | flops 131072000 | bytes 3568640 | tf_op jit(solution)/shard_map/dot_general | solution.py:238
  58.2 0.1 collective-permute-start.17
  58.3 0.7 %convolution_add_fusion.4.refs_0_.refs_4_ = f32[40,1024]{1,0:T(8,128)S(1)} fusion(f32[40,1024]{1,0:T(8,128)S(1)} %fusion.4, bf16[40,1600]{1,0:T(8,128)(2,1)S(1)} %get-tuple-element.62, bf16[1600,1024]{1,0:T(8,128)(2,1)S(1)} %bitcast.30), kind=kOutput, calls=%fused_computation.4 | convolution fusion | flops 131112960 | bytes 3732480 | tf_op jit(solution)/shard_map/dot_general | solution.py:237
  59.0 1.5 %collective-permute-start.18 = (f16[20,1024]{1,0:T(8,128)(2,1)S(1)}, f16[20,1024]{1,0:T(8,128)(2,1)S(1)}, u32[]{:S(2)}, u32[]{:S(2)}) collective-permute-start(f16[20,1024]{1,0:T(8,128)(2,1)S(1)} %convert_element_type.20), channel_id=1, source_target_pairs={{0,2},{2,0},{1,3},{3,1},{4,6},{6,4},{5,7},{7,5},{8,10},{10,8},{9,1... | collective-permute-start | bytes 122888 | tf_op jit(solution)/shard_map/ppermute | solution.py:56
  60.6 0.1 shard_map.69.row_ref
  60.8 3.6 %collective-permute-done.18 = f16[20,1024]{1,0:T(8,128)(2,1)S(1)} collective-permute-done((f16[20,1024]{1,0:T(8,128)(2,1)S(1)}, f16[20,1024]{1,0:T(8,128)(2,1)S(1)}, u32[]{:S(2)}, u32[]{:S(2)}) %collective-permute-start.18) | collective-permute-done | bytes 40992 | tf_op jit(solution)/shard_map/ppermute | solution.py:56
  64.5 1.3 %shard_map.70 = f32[320,1024]{1,0:T(8,128)} custom-call(f32[320,1024]{1,0:T(8,128)S(1)} %copy-done, f32[320,128]{1,0:T(8,128)S(1)} %shard_map.69.row_ref, s32[2,1024]{1,0:T(2,128)S(1)} %bitcast.23, f32[160,1024]{1,0:T(8,128)S(1)} %convolution_add_fusion.2.refs_0_.refs_1_.refs_2_.refs_3_, ...), custom_call_target="tpu_custom_call" | custom-call | tf_op jit(solution)/shard_map/pallas_call | solution.py:173
  (31 shorter events, 0.4 us)
Async XLA Ops:
  0.0 4.4 %collective-permute-start = (bf16[20,8,200]{2,1,0:T(8,128)(2,1)}, bf16[20,8,200]{2,1,0:T(8,128)(2,1)S(1)}, u32[]{:S(2)}, u32[]{:S(2)}) collective-permute-start(bf16[20,8,200]{2,1,0:T(8,128)(2,1)} %param.5), channel_id=1, source_target_pairs={{0,1},{1,0},{2,3},{3,2},{4,5},{5,4},{6,7},{7,6},{8,9},{9,8},{10,11... | collective-permute-start | bytes 192008 | tf_op jit(solution)/shard_map/ppermute | solution.py:52
  4.4 23.2 %collective-permute-start.4 = (bf16[1600,1024]{1,0:T(8,128)(2,1)}, bf16[1600,1024]{1,0:T(8,128)(2,1)S(1)}, u32[]{:S(2)}, u32[]{:S(2)}) collective-permute-start(bf16[1600,1024]{1,0:T(8,128)(2,1)} %bitcast.25), channel_id=1, source_target_pairs={{0,1},{1,0},{2,3},{3,2},{4,5},{5,4},{6,7},{7,6},{8,9},{9,8},{10,11... | collective-permute-start | bytes 9830408 | tf_op jit(solution)/shard_map/ppermute | solution.py:52
  4.9 8.4 %collective-permute-start.1 = (bf16[40,1600]{1,0:T(8,128)(2,1)S(1)}, bf16[40,1600]{1,0:T(8,128)(2,1)S(1)}, u32[]{:S(2)}, u32[]{:S(2)}) collective-permute-start(bf16[40,1600]{1,0:T(8,128)(2,1)S(1)} %shard_map.55), channel_id=1, source_target_pairs={{0,128},{1,192},{32,160},{33,224},{64,129},{65,193},{96,161},{97,2... | collective-permute-start | bytes 384008 | tf_op jit(solution)/shard_map/ppermute | solution.py:48
  8.6 7.8 %collective-permute-start.2 = (bf16[40,1600]{1,0:T(8,128)(2,1)S(1)}, bf16[40,1600]{1,0:T(8,128)(2,1)S(1)}, u32[]{:S(2)}, u32[]{:S(2)}) collective-permute-start(bf16[40,1600]{1,0:T(8,128)(2,1)S(1)} %shard_map.55), channel_id=1, source_target_pairs={{0,0},{1,64},{32,32},{33,96},{64,1},{65,65},{96,33},{97,97},{128,1... | collective-permute-start | bytes 384008 | tf_op jit(solution)/shard_map/ppermute | solution.py:48
  16.6 11.0 %collective-permute-start.7 = (bf16[40,3200]{1,0:T(8,128)(2,1)S(1)}, bf16[40,3200]{1,0:T(8,128)(2,1)S(1)}, u32[]{:S(2)}, u32[]{:S(2)}) collective-permute-start(bf16[40,3200]{1,0:T(8,128)(2,1)S(1)} %shard_map.56.refs_0_), channel_id=1, source_target_pairs={{0,4},{4,8},{8,12},{12,16},{16,20},{20,24},{24,28},{28,0},{1,5},{5... | collective-permute-start | bytes 768008 | tf_op jit(solution)/shard_map/ppermute | solution.py:30
  18.3 9.7 %collective-permute-start.3 = (bf16[40,3200]{1,0:T(8,128)(2,1)S(1)}, bf16[40,3200]{1,0:T(8,128)(2,1)S(1)}, u32[]{:S(2)}, u32[]{:S(2)}) collective-permute-start(bf16[40,3200]{1,0:T(8,128)(2,1)S(1)} %shard_map.56.refs_0_), channel_id=1, source_target_pairs={{0,28},{4,0},{8,4},{12,8},{16,12},{20,16},{24,20},{28,24},{1,29},{... | collective-permute-start | bytes 768008 | tf_op jit(solution)/shard_map/ppermute | solution.py:26
  22.4 8.6 %collective-permute-start.9 = (bf16[40,3200]{1,0:T(8,128)(2,1)S(1)}, bf16[40,3200]{1,0:T(8,128)(2,1)S(1)}, u32[]{:S(2)}, u32[]{:S(2)}) collective-permute-start(bf16[40,3200]{1,0:T(8,128)(2,1)S(1)} %shard_map.56.refs_0_), channel_id=1, source_target_pairs={{0,32},{1,97},{32,0},{33,65},{64,96},{65,33},{96,64},{97,1},{2,34}... | collective-permute-start | bytes 768008 | tf_op jit(solution)/shard_map/ppermute | solution.py:40
  27.6 7.1 %collective-permute-start.8 = (bf16[40,3200]{1,0:T(8,128)(2,1)S(1)}, bf16[40,3200]{1,0:T(8,128)(2,1)S(1)}, u32[]{:S(2)}, u32[]{:S(2)}) collective-permute-start(bf16[40,3200]{1,0:T(8,128)(2,1)S(1)} %collective-permute-done.7.refs_1_), channel_id=1, source_target_pairs={{0,4},{4,8},{8,12},{12,16},{16,20},{20,24},{24,28},{28,0},{1,5},{5... | collective-permute-start | bytes 768008 | tf_op jit(solution)/shard_map/ppermute | solution.py:30
  28.0 4.0 %copy-start.3 = (bf16[8,200,1024]{2,1,0:T(8,128)(2,1)S(1)}, bf16[8,200,1024]{2,1,0:T(8,128)(2,1)}, u32[]{:S(2)}) copy-start(bf16[8,200,1024]{2,1,0:T(8,128)(2,1)} %param.6) | copy-start | bytes 9830404
  28.0 6.7 %collective-permute-start.5 = (bf16[40,3200]{1,0:T(8,128)(2,1)S(1)}, bf16[40,3200]{1,0:T(8,128)(2,1)S(1)}, u32[]{:S(2)}, u32[]{:S(2)}) collective-permute-start(bf16[40,3200]{1,0:T(8,128)(2,1)S(1)} %collective-permute-done.3.refs_0_), channel_id=1, source_target_pairs={{0,28},{4,0},{8,4},{12,8},{16,12},{20,16},{24,20},{28,24},{1,29},{... | collective-permute-start | bytes 768008 | tf_op jit(solution)/shard_map/ppermute | solution.py:26
  30.8 9.2 %collective-permute-start.11 = (bf16[80,3200]{1,0:T(8,128)(2,1)S(1)}, bf16[80,3200]{1,0:T(8,128)(2,1)S(1)}, u32[]{:S(2)}, u32[]{:S(2)}) collective-permute-start(bf16[80,3200]{1,0:T(8,128)(2,1)S(1)} %shard_map.58.refs_2_), channel_id=1, source_target_pairs={{0,32},{1,97},{32,0},{33,65},{64,96},{65,33},{96,64},{97,1},{2,34}... | collective-permute-start | bytes 1536008 | tf_op jit(solution)/shard_map/ppermute | solution.py:40
  34.7 7.5 %collective-permute-start.10 = (bf16[40,3200]{1,0:T(8,128)(2,1)S(1)}, bf16[40,3200]{1,0:T(8,128)(2,1)S(1)}, u32[]{:S(2)}, u32[]{:S(2)}) collective-permute-start(bf16[40,3200]{1,0:T(8,128)(2,1)S(1)} %collective-permute-done.8.refs_1_), channel_id=1, source_target_pairs={{0,4},{4,8},{8,12},{12,16},{16,20},{20,24},{24,28},{28,0},{1,5},{5... | collective-permute-start | bytes 768008 | tf_op jit(solution)/shard_map/ppermute | solution.py:30
  34.7 7.5 %collective-permute-start.6 = (bf16[40,3200]{1,0:T(8,128)(2,1)S(1)}, bf16[40,3200]{1,0:T(8,128)(2,1)S(1)}, u32[]{:S(2)}, u32[]{:S(2)}) collective-permute-start(bf16[40,3200]{1,0:T(8,128)(2,1)S(1)} %collective-permute-done.5.refs_0_), channel_id=1, source_target_pairs={{0,28},{4,0},{8,4},{12,8},{16,12},{20,16},{24,20},{28,24},{1,29},{... | collective-permute-start | bytes 768008 | tf_op jit(solution)/shard_map/ppermute | solution.py:26
  40.0 9.1 %collective-permute-start.13 = (bf16[80,3200]{1,0:T(8,128)(2,1)S(1)}, bf16[80,3200]{1,0:T(8,128)(2,1)S(1)}, u32[]{:S(2)}, u32[]{:S(2)}) collective-permute-start(bf16[80,3200]{1,0:T(8,128)(2,1)S(1)} %shard_map.60.refs_1_), channel_id=1, source_target_pairs={{0,32},{1,97},{32,0},{33,65},{64,96},{65,33},{96,64},{97,1},{2,34}... | collective-permute-start | bytes 1536008 | tf_op jit(solution)/shard_map/ppermute | solution.py:40
  42.3 8.6 %collective-permute-start.12 = (bf16[40,3200]{1,0:T(8,128)(2,1)S(1)}, bf16[40,3200]{1,0:T(8,128)(2,1)S(1)}, u32[]{:S(2)}, u32[]{:S(2)}) collective-permute-start(bf16[40,3200]{1,0:T(8,128)(2,1)S(1)} %get-tuple-element.53), channel_id=1, source_target_pairs={{0,28},{1,5},{4,0},{5,9},{8,4},{9,13},{12,8},{13,17},{16,12},{17,2... | collective-permute-start | bytes 768008 | tf_op jit(solution)/shard_map/ppermute | solution.py:35
  42.6 12.0 %collective-permute-start.15 = (bf16[80,3200]{1,0:T(8,128)(2,1)S(1)}, bf16[80,3200]{1,0:T(8,128)(2,1)S(1)}, u32[]{:S(2)}, u32[]{:S(2)}) collective-permute-start(bf16[80,3200]{1,0:T(8,128)(2,1)S(1)} %get-tuple-element.54.refs_1_), channel_id=1, source_target_pairs={{0,32},{1,97},{32,0},{33,65},{64,96},{65,33},{96,64},{97,1},{2,34}... | collective-permute-start | bytes 1536008 | tf_op jit(solution)/shard_map/ppermute | solution.py:40
  45.1 15.5 %collective-permute-start.16 = (f16[160,1024]{1,0:T(8,128)(2,1)S(1)}, f16[160,1024]{1,0:T(8,128)(2,1)S(1)}, u32[]{:S(2)}, u32[]{:S(2)}) collective-permute-start(f16[160,1024]{1,0:T(8,128)(2,1)S(1)} %convert_element_type.18), channel_id=1, source_target_pairs={{0,2},{2,0},{1,3},{3,1},{4,6},{6,4},{5,7},{7,5},{8,10},{10,8},{9,1... | collective-permute-start | bytes 983048 | tf_op jit(solution)/shard_map/ppermute | solution.py:56
  50.9 6.5 %collective-permute-start.14 = (bf16[40,3200]{1,0:T(8,128)(2,1)S(1)}, bf16[40,3200]{1,0:T(8,128)(2,1)S(1)}, u32[]{:S(2)}, u32[]{:S(2)}) collective-permute-start(bf16[40,3200]{1,0:T(8,128)(2,1)S(1)} %collective-permute-done.12.refs_1_), channel_id=1, source_target_pairs={{0,32},{1,97},{32,0},{33,65},{64,96},{65,33},{96,64},{97,1},{2,34}... | collective-permute-start | bytes 768008 | tf_op jit(solution)/shard_map/ppermute | solution.py:40
  58.2 2.5 %copy-start.2 = (s32[320,2]{0,1:T(2,128)S(1)}, s32[320,2]{0,1:T(2,128)}, u32[]{:S(2)}) copy-start(s32[320,2]{0,1:T(2,128)} %param.8) | copy-start | bytes 7684
  58.2 6.3 %copy-start = (f32[320,1024]{1,0:T(8,128)S(1)}, f32[320,1024]{1,0:T(8,128)}, u32[]{:S(2)}) copy-start(f32[320,1024]{1,0:T(8,128)} %in_ref.1) | copy-start | bytes 3932164
  58.2 6.3 %copy-start.1 = (s32[1024,2]{0,1:T(2,128)S(1)}, s32[1024,2]{0,1:T(2,128)}, u32[]{:S(2)}) copy-start(s32[1024,2]{0,1:T(2,128)} %param.9) | copy-start | bytes 24580
  58.2 6.2 %collective-permute-start.17 = (f16[140,1024]{1,0:T(8,128)(2,1)S(1)}, f16[140,1024]{1,0:T(8,128)(2,1)S(1)}, u32[]{:S(2)}, u32[]{:S(2)}) collective-permute-start(f16[140,1024]{1,0:T(8,128)(2,1)S(1)} %convert_element_type.19), channel_id=1, source_target_pairs={{0,2},{2,0},{1,3},{3,1},{4,6},{6,4},{5,7},{7,5},{8,10},{10,8},{9,1... | collective-permute-start | bytes 860168 | tf_op jit(solution)/shard_map/ppermute | solution.py:56
  59.0 5.4 %collective-permute-start.18 = (f16[20,1024]{1,0:T(8,128)(2,1)S(1)}, f16[20,1024]{1,0:T(8,128)(2,1)S(1)}, u32[]{:S(2)}, u32[]{:S(2)}) collective-permute-start(f16[20,1024]{1,0:T(8,128)(2,1)S(1)} %convert_element_type.20), channel_id=1, source_target_pairs={{0,2},{2,0},{1,3},{3,1},{4,6},{6,4},{5,7},{7,5},{8,10},{10,8},{9,1... | collective-permute-start | bytes 122888 | tf_op jit(solution)/shard_map/ppermute | solution.py:56
